TPU v7x, 32 devices: a whole 2x2x4 slice. The times are simulated.
32 devices in a mesh: dp: 4 (over z), head: 4 (over y, x), blk: 2 (over core).
Axes of the slice: x: 2, y: 2, z: 4, core: 2. Of those that a mesh axis runs over, the one named last changes fastest.
Arguments:
- block_in: bfloat16 [4, 2048, 2048], P('dp', ('head', 'blk')), may hold values from -6 to 6
- cotangent: bfloat16 [4, 2048, 2048], P('dp', ('head', 'blk')), may hold values from -6 to 6
- seg_lengths: int32 [4, 4], P('dp'), may hold values from 0 to 2048, as said below
- ln1_gain: bfloat16 [2048], replicated, may hold values from 0.5 to 1.5
- ln1_bias: bfloat16 [2048], replicated, may hold values from -1.5 to 1.5
- qkv_weight: bfloat16 [2048, 6144], P('dp'), may hold values from -0.125 to 0.125
- qkv_bias: bfloat16 [6144], replicated, may hold values from -1.5 to 1.5
- out_weight: bfloat16 [2048, 2048], P('dp'), may hold values from -1 to 1
- out_bias: bfloat16 [2048], replicated, may hold values from -1.5 to 1.5
- ln2_gain: bfloat16 [2048], replicated, may hold values from 0.5 to 1.5
- ln2_bias: bfloat16 [2048], replicated, may hold values from -1.5 to 1.5
- fc1_weight: bfloat16 [2048, 8192], P('dp'), may hold values from -0.125 to 0.125
- fc1_bias: bfloat16 [8192], replicated, may hold values from -1.5 to 1.5
- fc2_weight: bfloat16 [2048, 8192], P('dp'), may hold values from -0.0625 to 0.0625
- fc2_bias: bfloat16 [2048], replicated, may hold values from -1.5 to 1.5
Outputs:
- block_out: bfloat16 [4, 2048, 2048], P('dp', ('head', 'blk'))
- input_grad: bfloat16 [4, 2048, 2048], P('dp', ('head', 'blk'))
- ln1_gain_grad: float32 [2048], replicated
- ln1_bias_grad: float32 [2048], replicated
- qkv_weight_grad: float32 [2048, 6144], P('dp')
- qkv_bias_grad: float32 [6144], replicated
- out_weight_grad: float32 [2048, 2048], P('dp')
- out_bias_grad: float32 [2048], replicated
- ln2_gain_grad: float32 [2048], replicated
- ln2_bias_grad: float32 [2048], replicated
- fc1_weight_grad: float32 [2048, 8192], P('dp')
- fc1_bias_grad: float32 [8192], replicated
- fc2_weight_grad: float32 [2048, 8192], P('dp')
- fc2_bias_grad: float32 [2048], replicated
- attn_rms: float32 [], replicated
- mlp_rms: float32 [], replicated
Inputs may be any that keep to these rules, and one draw needn't show every extreme that they name: `seg_lengths`: each row lists one to four segment lengths, each 512, 1024 or 2048, that sum to 2048, followed by zeros; some row holds a single segment of 2048 tokens.
All inputs are finite; a program needn't handle non-finite values.
Results may differ from a plain program's by a relative error of at most 0.017.
Values may be sent and summed in bfloat16 or wider, within the bound.
No kernel may reach another device: no remote copies, remote signals or barrier semaphores. Data moves between devices by JAX's collectives and lax.ppermute only.
A program may use at most 768 MiB of HBM per device.

v0:
```python
import jax
import jax.numpy as jnp
from jax import lax
from jax.sharding import PartitionSpec as P

HEADS = 8
HEAD_SIZE = 256
ROT = 64


NORM_EPS = 1e-05
NEG_FILL = -1e30
ROT_BASE = 10000.0


def normalize(inputs):
    centred = inputs - jnp.mean(inputs, axis=-1, keepdims=True)
    spread = jnp.mean(centred * centred, axis=-1, keepdims=True)
    scaled = lax.rsqrt(spread + NORM_EPS)
    return (centred * scaled, scaled)


def norm_back(normed, scaled, gain_vec, upstream):
    inner_grad = upstream * gain_vec
    share_part = scaled * (
        inner_grad
        - jnp.mean(inner_grad, axis=-1, keepdims=True)
        - normed * jnp.mean(inner_grad * normed, axis=-1, keepdims=True)
    )
    return (share_part, jnp.sum(upstream * normed, axis=0), jnp.sum(upstream, axis=0))


def segment_info(lengths, places):
    seg_ends = jnp.cumsum(lengths, axis=-1)
    passed = (places[..., :, None] >= seg_ends[..., None, :]).astype(jnp.int32)
    segment = jnp.sum(passed, axis=-1)
    seg_start = jnp.sum(passed * lengths[..., None, :], axis=-1)
    return (segment, places - seg_start)


def rotate(values, places, direction):
    half_rot = ROT // 2
    frequency = ROT_BASE ** (-(2.0 * jnp.arange(half_rot, dtype=jnp.float32)) / ROT)
    angles = places.astype(jnp.float32)[..., None] * frequency
    cosine = jnp.cos(angles)[..., None, :]
    sine_part = direction * jnp.sin(angles)[..., None, :]
    lower_half = values[..., :half_rot]
    upper_half = values[..., half_rot:ROT]
    return jnp.concatenate(
        [
            lower_half * cosine - upper_half * sine_part,
            upper_half * cosine + lower_half * sine_part,
            values[..., ROT:],
        ],
        axis=-1,
    )


def exact_gelu(values):
    return jax.nn.gelu(values, approximate=False)


def body(
    block_in,
    cotangent,
    seg_lengths,
    ln1_gain,
    ln1_bias,
    qkv_weight,
    qkv_bias,
    out_weight,
    out_bias,
    ln2_gain,
    ln2_bias,
    fc1_weight,
    fc1_bias,
    fc2_weight,
    fc2_bias,
):
    rows_here, span_len, model_width = block_in.shape
    hidden_units = fc1_weight.shape[1]
    tokens_here = rows_here * span_len
    data_count = lax.axis_size("dp")
    head_count = lax.axis_size("head")
    blk_count = lax.axis_size("blk")
    head_place = lax.axis_index("head")
    blk_place = lax.axis_index("blk")
    local_heads = HEADS // head_count
    gathered_len = head_count * span_len
    score_scale = HEAD_SIZE ** (-0.5)
    contract_last = (((1,), (1,)), ((), ()))
    own_places = (head_place * blk_count + blk_place) * span_len + jnp.arange(
        span_len, dtype=jnp.int32
    )
    own_offset = segment_info(seg_lengths, own_places)[1]

    def head_places(token_index, blk_index):
        return (token_index // span_len * blk_count + blk_index) * span_len + token_index % span_len

    query_places = head_places(jnp.arange(gathered_len, dtype=jnp.int32), blk_place)
    query_segment = segment_info(seg_lengths, query_places)[0]

    def key_info(key_index):
        key_places = head_places(key_index % gathered_len, key_index // gathered_len)
        return (key_places, segment_info(seg_lengths, key_places)[0])

    def allowed_mask(key_places, key_segment):
        same_segment = key_segment[:, None, None, :] == query_segment[:, None, :, None]
        causal = key_places[None, None, None, :] <= query_places[None, None, :, None]
        return same_segment & causal

    inputs = block_in.astype(jnp.float32).reshape(tokens_here, model_width)
    normed, scaled = normalize(inputs)
    attn_in = (normed * ln1_gain + ln1_bias).astype(jnp.bfloat16)
    qkv_full, out_full = (
        lax.all_gather(qkv_weight, "dp", axis=0, tiled=True),
        lax.all_gather(out_weight, "dp", axis=0, tiled=True),
    )
    joined = jnp.dot(attn_in, qkv_full, preferred_element_type=jnp.float32) + qkv_bias
    joined = joined.reshape(rows_here, span_len, 3, HEADS, HEAD_SIZE)
    query = rotate(joined[:, :, 0], own_offset, 1.0)
    keyed = rotate(joined[:, :, 1], own_offset, 1.0)
    packed = jnp.stack([query, keyed, joined[:, :, 2]], axis=2).astype(jnp.bfloat16)
    by_heads = lax.all_to_all(packed, "head", split_axis=3, concat_axis=1, tiled=True)
    query_h = by_heads[:, :, 0]
    key_h = by_heads[:, :, 1]
    value_h = by_heads[:, :, 2]
    running = jnp.full((rows_here, local_heads, gathered_len), NEG_FILL, jnp.float32)
    key_piece = lax.all_gather(key_h, "blk", axis=1, tiled=True)
    value_piece = lax.all_gather(value_h, "blk", axis=1, tiled=True)
    key_index = jnp.arange(key_piece.shape[1], dtype=jnp.int32)
    key_places, key_segment = key_info(key_index)
    scores = (
        jnp.einsum("rqhd,rkhd->rhqk", query_h, key_piece, preferred_element_type=jnp.float32)
        * score_scale
    )
    allowed = allowed_mask(key_places, key_segment)
    scores = jnp.where(allowed, scores, NEG_FILL)
    newest = jnp.maximum(running, jnp.max(scores, axis=-1))
    weights = jnp.where(allowed, jnp.exp(scores - newest[..., None]), 0.0)
    totals = jnp.sum(weights, axis=-1)
    accumulated = jnp.einsum(
        "rhqk,rkhd->rqhd",
        weights.astype(jnp.bfloat16),
        value_piece,
        preferred_element_type=jnp.float32,
    )
    running, totals, accumulated = (newest, totals, accumulated)
    log_total = running + jnp.log(totals)
    context_h = (accumulated / jnp.transpose(totals, (0, 2, 1))[..., None]).astype(jnp.bfloat16)
    context = lax.all_to_all(context_h, "head", split_axis=1, concat_axis=2, tiled=True).reshape(
        tokens_here, model_width
    )
    attn_out = jnp.dot(context, out_full, preferred_element_type=jnp.float32) + out_bias
    fc1_full, fc2_full = (
        lax.all_gather(fc1_weight, "dp", axis=0, tiled=True),
        lax.all_gather(fc2_weight, "dp", axis=0, tiled=True),
    )
    mlp_in = (normed * ln2_gain + ln2_bias).astype(jnp.bfloat16)
    hidden = jnp.dot(mlp_in, fc1_full, preferred_element_type=jnp.float32) + fc1_bias
    active, gelu_back = jax.vjp(exact_gelu, hidden)
    active = active.astype(jnp.bfloat16)
    mlp_out = (
        lax.dot_general(active, fc2_full, contract_last, preferred_element_type=jnp.float32)
        + fc2_bias
    )
    block_out = (
        (inputs + attn_out + mlp_out).astype(jnp.bfloat16).reshape(rows_here, span_len, model_width)
    )
    squares = jnp.stack([jnp.sum(attn_out * attn_out), jnp.sum(mlp_out * mlp_out)])
    upstream = cotangent.reshape(tokens_here, model_width)
    up_float = upstream.astype(jnp.float32)
    hidden_grad = gelu_back(jnp.dot(upstream, fc2_full, preferred_element_type=jnp.float32))[
        0
    ].astype(jnp.bfloat16)
    mlp_in_grad = lax.dot_general(
        hidden_grad, fc1_full, contract_last, preferred_element_type=jnp.float32
    )
    context_grad = lax.dot_general(
        upstream, out_full, contract_last, preferred_element_type=jnp.float32
    ).astype(jnp.bfloat16)
    grad_h = lax.all_to_all(
        context_grad.reshape(rows_here, span_len, HEADS, HEAD_SIZE),
        "head",
        split_axis=2,
        concat_axis=1,
        tiled=True,
    )
    key_all, value_all = (
        lax.all_gather(key_h, "blk", axis=1, tiled=True),
        lax.all_gather(value_h, "blk", axis=1, tiled=True),
    )
    key_places, key_segment = key_info(jnp.arange(key_all.shape[1], dtype=jnp.int32))
    allowed = allowed_mask(key_places, key_segment)
    scores = (
        jnp.einsum("rqhd,rkhd->rhqk", query_h, key_all, preferred_element_type=jnp.float32)
        * score_scale
    )
    probs_full = jnp.where(allowed, jnp.exp(scores - log_total[..., None]), 0.0)
    value_grad = jnp.einsum(
        "rhqk,rqhd->rkhd",
        probs_full.astype(jnp.bfloat16),
        grad_h,
        preferred_element_type=jnp.float32,
    )
    prob_grad = jnp.einsum("rqhd,rkhd->rhqk", grad_h, value_all, preferred_element_type=jnp.float32)
    score_grad = (
        probs_full * (prob_grad - jnp.sum(probs_full * prob_grad, axis=-1, keepdims=True))
    ).astype(jnp.bfloat16)
    query_grad = (
        jnp.einsum("rhqk,rkhd->rqhd", score_grad, key_all, preferred_element_type=jnp.float32)
        * score_scale
    )
    key_grad = (
        jnp.einsum("rhqk,rqhd->rkhd", score_grad, query_h, preferred_element_type=jnp.float32)
        * score_scale
    )
    key_own, value_own = (
        lax.psum_scatter(
            key_grad.astype(jnp.bfloat16), "blk", scatter_dimension=1, tiled=True
        ).astype(jnp.float32),
        lax.psum_scatter(
            value_grad.astype(jnp.bfloat16), "blk", scatter_dimension=1, tiled=True
        ).astype(jnp.float32),
    )
    back_pack = jnp.stack(
        [
            query_grad.astype(jnp.bfloat16),
            key_own.astype(jnp.bfloat16),
            value_own.astype(jnp.bfloat16),
        ],
        axis=2,
    )
    by_tokens = lax.all_to_all(back_pack, "head", split_axis=1, concat_axis=3, tiled=True).astype(
        jnp.float32
    )
    qkv_grad = jnp.stack(
        [
            rotate(by_tokens[:, :, 0], own_offset, -1.0),
            rotate(by_tokens[:, :, 1], own_offset, -1.0),
            by_tokens[:, :, 2],
        ],
        axis=2,
    )
    qkv_grad = qkv_grad.reshape(tokens_here, 3 * model_width).astype(jnp.bfloat16)
    attn_in_grad = lax.dot_general(
        qkv_grad, qkv_full, contract_last, preferred_element_type=jnp.float32
    )
    share_one, gain_one_grad, bias_one_grad = norm_back(normed, scaled, ln1_gain, attn_in_grad)
    share_two, gain_two_grad, bias_two_grad = norm_back(normed, scaled, ln2_gain, mlp_in_grad)
    input_grad = (
        (up_float + share_one + share_two)
        .astype(jnp.bfloat16)
        .reshape(rows_here, span_len, model_width)
    )
    contract = (((0,), (0,)), ((), ()))
    shard_rows = lax.psum_scatter(
        jnp.concatenate(
            [
                lax.dot_general(attn_in, qkv_grad, contract, preferred_element_type=jnp.float32),
                lax.dot_general(context, upstream, contract, preferred_element_type=jnp.float32),
                lax.dot_general(mlp_in, hidden_grad, contract, preferred_element_type=jnp.float32),
                lax.dot_general(upstream, active, contract, preferred_element_type=jnp.float32),
            ],
            axis=1,
        ).astype(jnp.bfloat16),
        "dp",
        scatter_dimension=0,
        tiled=True,
    ).astype(jnp.float32)
    shard_rows = lax.psum(shard_rows.astype(jnp.bfloat16), ("head", "blk")).astype(jnp.float32)
    bias_out_grad = jnp.sum(up_float, axis=0)
    reduced = lax.psum(
        (
            gain_one_grad,
            bias_one_grad,
            jnp.sum(qkv_grad.astype(jnp.float32), axis=0),
            bias_out_grad,
            gain_two_grad,
            bias_two_grad,
            jnp.sum(hidden_grad.astype(jnp.float32), axis=0),
            squares,
        ),
        ("dp", "head", "blk"),
    )
    entries = tokens_here * data_count * head_count * blk_count * model_width
    branch_rms = jnp.sqrt(reduced[7] / entries)
    qkv_part = shard_rows[:, : 3 * model_width]
    out_part = shard_rows[:, 3 * model_width : 4 * model_width]
    fc1_part = shard_rows[:, 4 * model_width : 4 * model_width + hidden_units]
    fc2_part = shard_rows[:, 4 * model_width + hidden_units :]
    return (
        block_out,
        input_grad,
        reduced[0],
        reduced[1],
        qkv_part,
        reduced[2],
        out_part,
        reduced[3],
        reduced[4],
        reduced[5],
        fc1_part,
        reduced[6],
        fc2_part,
        reduced[3],
        branch_rms[0],
        branch_rms[1],
    )


def solution(mesh):
    placed = (
        P("dp", ("head", "blk"), None),
        P("dp", ("head", "blk"), None),
        P("dp", None),
        P(),
        P(),
        P("dp", None),
        P(),
        P("dp", None),
        P(),
        P(),
        P(),
        P("dp", None),
        P(),
        P("dp", None),
        P(),
    )
    return jax.shard_map(
        body,
        mesh=mesh,
        in_specs=placed,
        out_specs=(
            P("dp", ("head", "blk"), None),
            P("dp", ("head", "blk"), None),
            P(),
            P(),
            P("dp", None),
            P(),
            P("dp", None),
            P(),
            P(),
            P(),
            P("dp", None),
            P(),
            P("dp", None),
            P(),
            P(),
            P(),
        ),
        check_vma=False,
    )
```

profile of v0, /device:TPU:0, one launch (start us, length us, event | category | flops | bytes accessed | tf_op | source)
XLA Modules:
  0.0 4040.2 jit_solution(9346358374026768)
XLA Ops:
  10.0 427.5 %all-gather.9.cloned.1.call-done = bf16[2048,6144]{1,0:T(8,128)(2,1)} async-done(((bf16[512,6144]{1,0:T(8,128)(2,1)}), bf16[2048,6144]{1,0:T(8,128)(2,1)}) %all-gather.9.cloned.1.call-update) | async-done | bytes 25165840 | tf_op jit(solution)/shard_map/all_gather | solution.py:116
  437.6 14.3 convolution_add_fusion.1
  451.9 6.6 copy.113
  460.2 2.7 slice_bitcast_fusion.3
  464.0 40.4 %all_to_all.57 = bf16[1,256,3,8,256]{1,4,2,0,3:T(8,128)(2,1)} all-to-all(bf16[1,256,3,8,256]{1,4,2,0,3:T(8,128)(2,1)S(1)} %copy.93), channel_id=1, replica_groups=mesh['dp'=4,'head'=4,'blk'=2] {'head'}, dimensions={3} | all-to-all | bytes 6291456 | tf_op jit(solution)/shard_map/all_to_all | solution.py:124
  504.4 4.6 copy.94
  509.0 3.0 fusion.132
  512.2 74.8 %all-gather.11.cloned.1.call-done = bf16[2048,2048]{1,0:T(8,128)(2,1)} async-done(((bf16[512,2048]{1,0:T(8,128)(2,1)}), bf16[2048,2048]{1,0:T(8,128)(2,1)}) %all-gather.11.cloned.1.call-update) | async-done | bytes 8388624 | tf_op jit(solution)/shard_map/all_gather | solution.py:117
  587.0 5.7 convolution_convert_fusion.3
  594.2 3.7 all-to-all-start.2
  598.0 3.5 compare_and_fusion
  601.5 10.4 all-to-all-done.2
  613.2 6.0 select_reduce_fusion
  619.2 7.3 fusion
  626.6 10.5 fusion.21
  637.4 14.5 multiply_reduce_fusion
  651.9 12.7 multiply_convert_fusion
  664.7 3.4 copy-done.3
  668.1 3.7 fusion.24
  673.3 11.7 fusion.58
  687.1 4.0 all-to-all-start.1
  691.0 10.3 fusion.68
  701.4 4.2 pad_maximum_fusion.2
  705.6 8.8 copy.104
  714.4 4.7 all-to-all-start.3
  721.8 7.4 convolution_convert_fusion.2
  729.2 12.3 copy.107
  741.4 13.3 all-to-all-done.3
  754.7 9.5 copy.105
  769.1 2.8 convert_reduce_fusion.1
  772.0 13.9 convolution_convert_fusion.1
  785.9 457.1 %all-gather.13.cloned.1.call-done = bf16[2048,8192]{1,0:T(8,128)(2,1)} async-done(((bf16[512,8192]{1,0:T(8,128)(2,1)}), bf16[2048,8192]{1,0:T(8,128)(2,1)}) %all-gather.13.cloned.1.call-update) | async-done | bytes 33554448 | tf_op jit(solution)/shard_map/all_gather | solution.py:156
  1242.9 32.4 multiply_convert_fusion.1
  1275.4 15.9 convert_bitcast_fusion
  1291.3 512.9 %all-gather.15.cloned.1.call-done = bf16[2048,8192]{1,0:T(8,128)(2,1)} async-done(((bf16[512,8192]{1,0:T(8,128)(2,1)}), bf16[2048,8192]{1,0:T(8,128)(2,1)}) %all-gather.15.cloned.1.call-update) | async-done | bytes 33554448 | tf_op jit(solution)/shard_map/all_gather | solution.py:157
  1804.1 33.4 convert_reduce_fusion
  1837.5 16.3 convolution_convert_fusion
  1853.8 65.7 %pad_maximum_fusion = bf16[2048,24576]{1,0:T(8,128)(2,1)} fusion(bf16[2048,8192]{1,0:T(8,128)(2,1)} %convert_bitcast_fusion, bf16[2048,8192]{1,0:T(8,128)(2,1)} %convolution_convert_fusion, bf16[2048,2048]{1,0:T(8,128)(2,1)} %copy.107, bf16[2048,6144]{1,0:T(8,128)(2,1)} %convolution_convert_fusion.1), kind=kLoop, calls=%fused_computation | loop fusion | flops 402653184 | bytes 201326592 | tf_op jit(solution)/shard_map/concatenate | solution.py:258
  1921.0 18.3 fusion.134
  1939.3 15.3 fusion.49
  1954.6 17.2 convolution_add_fusion.2
  1971.9 11.0 multiply_reduce_fusion.2
  1984.8 1566.9 %reduce-scatter.8.cloned.1.call-done = bf16[512,24576]{1,0:T(8,128)(2,1)} async-done(((bf16[2048,24576]{1,0:T(8,128)(2,1)}), bf16[512,24576]{1,0:T(8,128)(2,1)}) %reduce-scatter.8.cloned.1.call-update) | async-done | bytes 25165840 | tf_op jit(solution)/shard_map/reduce_scatter | solution.py:257
  3551.8 134.3 %all-reduce.6.cloned.1.call-done = (f32[2048]{0:T(1024)}, f32[2048]{0:T(1024)}, f32[6144]{0:T(1024)}, f32[2048]{0:T(1024)}, f32[2048]{0:T(1024)}, /*index=5*/f32[2048]{0:T(1024)}, f32[8192]{0:T(1024)}, f32[2]{0:T(128)}) async-done(((f32[2048]{0:T(1024)}, f32[2048]{0:T(1024)}, f32[6144]{0:T(1024)}, f32[2048]{0:T(1024)}, f32[2048]{0:T(1024)}, /*index=5*/f32[2048]{0:T(1024)}, f32[8192]{0:T(1024)}, ...) | async-done | bytes 98328 | tf_op jit(solution)/shard_map/psum | solution.py:273
  3687.3 310.7 %all-reduce.4.cloned.1.call-done = bf16[512,24576]{1,0:T(8,128)(2,1)} async-done(((bf16[512,24576]{1,0:T(8,128)(2,1)}), bf16[512,24576]{1,0:T(8,128)(2,1)}) %all-reduce.4.cloned.1.call-update) | async-done | bytes 25165840 | tf_op jit(solution)/shard_map/psum | solution.py:271
  3998.1 9.2 slice.132
  4007.3 4.1 slice.133
  4011.4 17.0 fusion.131
  (144 shorter events, 29.2 us)
Async XLA Ops:
  7.2 1.6 copy-start.22
  7.2 1.6 copy-start.17
  7.2 1.6 copy-start.23
  7.2 1.6 copy-start.28
  7.2 1.9 copy-start.1
  7.2 430.3 %all-gather.9.cloned.1.call-start = ((), (), s32[]{:S(2)}) async-start(), calls=%async_computation.7 | async-start | bytes 31457280 | tf_op jit(solution)/shard_map/all_gather | solution.py:116
  8.0 579.0 %all-gather.11.cloned.1.call-start = ((), (), s32[]{:S(2)}) async-start(), calls=%async_computation.8 | async-start | bytes 10485760 | tf_op jit(solution)/shard_map/all_gather | solution.py:117
  8.7 604.4 %all-gather.19.cloned.1.call-start = ((), (), s32[]{:S(2)}) async-start(), calls=%async_computation.16 | async-start | bytes 3145728 | tf_op jit(solution)/shard_map/all_gather | solution.py:129
  8.8 763.2 %copy-start.10 = (f32[2048]{0:T(1024)}, f32[2048]{0:T(1024)S(1)}, u32[]{:S(2)}) copy-start(f32[2048]{0:T(1024)S(1)} %convert_element_type.212) | copy-start | bytes 24580
  464.0 123.0 %copy-start.6 = (bf16[1,256,2048]{2,1,0:T(8,128)(2,1)S(1)}, bf16[1,256,2048]{2,1,0:T(8,128)(2,1)}, u32[]{:S(2)}) copy-start(bf16[1,256,2048]{2,1,0:T(8,128)(2,1)} %param.16) | copy-start | bytes 3145732
  594.2 17.6 all-to-all-start.2
  597.9 39.5 all-gather.17.cloned.1.call-start
  612.9 88.5 %reduce-scatter.6.cloned.1.call-start = ((), (), s32[]{:S(2)}) async-start(), calls=%async_computation.12 | async-start | bytes 3145728 | tf_op jit(solution)/shard_map/reduce_scatter | solution.py:222
  619.1 7.4 copy-start
  619.2 7.4 copy-start.9
  637.1 64.3 %reduce-scatter.4.cloned.1.call-start = ((), (), s32[]{:S(2)}) async-start(), calls=%async_computation.11 | async-start | bytes 3145728 | tf_op jit(solution)/shard_map/reduce_scatter | solution.py:219
  651.9 16.2 copy-start.2
  664.7 3.4 copy-start.3
  671.8 571.2 %all-gather.13.cloned.1.call-start = ((), (), s32[]{:S(2)}) async-start(), calls=%async_computation.9 | async-start | bytes 41943040 | tf_op jit(solution)/shard_map/all_gather | solution.py:156
  672.5 1131.6 %all-gather.15.cloned.1.call-start = ((), (), s32[]{:S(2)}) async-start(), calls=%async_computation.10 | async-start | bytes 41943040 | tf_op jit(solution)/shard_map/all_gather | solution.py:157
  687.1 27.3 all-to-all-start.1
  701.4 17.7 copy-start.16
  701.4 17.8 copy-start.24
  701.4 17.8 copy-start.25
  714.4 40.3 all-to-all-start.3
  719.0 2832.7 %reduce-scatter.8.cloned.1.call-start = ((), (), s32[]{:S(2)}) async-start(), calls=%async_computation.13 | async-start | bytes 125829120 | tf_op jit(solution)/shard_map/reduce_scatter | solution.py:257
  721.8 19.7 copy-start.4
  785.9 489.5 %copy-start.7 = (bf16[1,256,2048]{2,1,0:T(8,128)(2,1)S(1)}, bf16[1,256,2048]{2,1,0:T(8,128)(2,1)}, u32[]{:S(2)}) copy-start(bf16[1,256,2048]{2,1,0:T(8,128)(2,1)} %param.16) | copy-start | bytes 3145732
  1919.6 0.7 copy-start.26
  1919.6 0.7 copy-start.27
  1919.6 0.7 copy-start.12
  1919.6 1766.5 %all-reduce.6.cloned.1.call-start = ((), (), s32[]{:S(2)}) async-start(), calls=%async_computation.17 | async-start | bytes 197632 | tf_op jit(solution)/shard_map/psum | solution.py:273
  1921.0 18.3 copy-start.11
  1954.6 17.2 copy-start.5
  1954.6 17.2 copy-start.8
  1984.8 2013.3 %all-reduce.4.cloned.1.call-start = ((), (), s32[]{:S(2)}) async-start(), calls=%async_computation.14 | async-start | bytes 50331648 | tf_op jit(solution)/shard_map/psum | solution.py:271
  4011.4 17.0 copy-start.14
  4011.4 17.6 copy-start.21
  4011.4 18.2 copy-start.20
  4011.4 18.8 copy-start.15
  4011.4 20.0 copy-start.19
  4011.4 20.6 copy-start.18
  4011.4 21.2 copy-start.13
Sparse Core Ops, SparseCore 0:
  9.7 427.8 all-gather.8
  439.1 147.8 all-gather.10
  589.1 8.7 all-gather.18
  613.0 7.8 all-gather.16
  637.2 6.8 reduce-scatter.5
  671.9 6.7 reduce-scatter.3
  680.3 562.5 all-gather.12
  1244.5 559.5 all-gather.14
  1919.8 1631.9 reduce-scatter.7
  3560.3 125.7 all-reduce.5
  3689.8 308.1 all-reduce.3
where the time goes:
time: 4050 us; the launch traced here: 4040 us
  waiting for transfers between devices  3510 us (87%)
  matrix products  258 us (6%)
  local copies, waits for them, and re-layouts  102 us (3%)
  other arithmetic  101 us (2%)
    reduce_scatter x1, waiting for transfers between devices, body(): lax.psum_scatter(jnp.concatenate([lax.dot_general(attn_in, qkv_grad, cont...  1570 us
    all_gather x1, waiting for transfers between devices, body(): lax.all_gather(fc2_weight, 'dp', axis=0, tiled=True)  513 us
    all_gather x1, waiting for transfers between devices, body(): lax.all_gather(fc1_weight, 'dp', axis=0, tiled=True)  457 us
    all_gather x1, waiting for transfers between devices, body(): lax.all_gather(qkv_weight, 'dp', axis=0, tiled=True)  428 us
    psum x1, waiting for transfers between devices, body(): lax.psum(shard_rows.astype(jnp.bfloat16), ('head', 'blk'))  311 us
    psum x1, waiting for transfers between devices, body(): lax.psum((gain_one_grad, bias_one_grad, jnp.sum(qkv_grad.astype(jnp.float...  134 us
  transfers between devices with their start and end apart: 14, of which 9 were waited for; matrix products, arithmetic and copies ran while one was open for 8% of the time, Pallas kernels for 0%

commit v1 on v0

v1 whole, which is shorter than its diff:
```python
import functools

import jax
import jax.numpy as jnp
from jax import lax
from jax.experimental import pallas as pl
from jax.experimental.pallas import tpu as pltpu
from jax.sharding import PartitionSpec as P

HEADS = 8
HEAD_SIZE = 256
ROT = 64
NORM_EPS = 1e-05
NEG_FILL = -1e30
ROT_BASE = 10000.0
BF = jnp.bfloat16
F32 = jnp.float32


def across(values, offset):
    count = lax.axis_size("head")
    return lax.ppermute(values, "head", [(i, i ^ offset) for i in range(count)])


def other_core(values):
    return lax.ppermute(values, "blk", [(0, 1), (1, 0)])


def plane_gather(own):
    half = own.shape[0] // 2
    one = across(own, 1)
    two = across(own, 2)
    three = jnp.concatenate([across(one[:half], 2), across(two[half:], 1)], axis=0)
    near = [own, one, two, three]
    return near + [other_core(piece) for piece in near]


def plane_scatter(partial, span):
    count = lax.axis_size("head")
    width = partial.shape[1]
    side = width // 2
    near = count * span
    got = other_core(partial[near:])
    mine = (partial[:near].astype(F32) + got.astype(F32)).reshape(count, span, width)
    left, right = mine[:, :, :side], mine[:, :, side:]
    left_got = across(jnp.stack([left[1], left[3]]).astype(BF), 1).astype(F32)
    right_got = across(jnp.stack([right[2], right[3]]).astype(BF), 2).astype(F32)
    left_last = across((left[2] + left_got[1]).astype(BF), 2).astype(F32)
    right_last = across((right[1] + right_got[1]).astype(BF), 1).astype(F32)
    return jnp.concatenate(
        [left[0] + left_got[0] + left_last, right[0] + right_got[0] + right_last], axis=1
    )


def data_gather(own):
    count = lax.axis_size("dp")
    place = lax.axis_index("dp")
    rows = own.shape[0]
    up = down = own
    ups, downs = [], []
    for step in range(1, count):
        up = lax.ppermute(up, "dp", [(i, i + 1) for i in range(step - 1, count - 1)])
        down = lax.ppermute(down, "dp", [(i + 1, i) for i in range(count - step)])
        ups.append(up)
        downs.append(down)
    whole = jnp.zeros((count * rows,) + own.shape[1:], own.dtype)
    whole = lax.dynamic_update_slice_in_dim(whole, own, place * rows, 0)
    for step in range(1, count):
        piece = jnp.where(place + step < count, downs[step - 1], ups[count - step - 1])
        source = lax.rem(place + step, count)
        whole = lax.dynamic_update_slice_in_dim(whole, piece, source * rows, 0)
    return whole


def data_scatter(partial):
    count = lax.axis_size("dp")
    place = lax.axis_index("dp")
    rows = partial.shape[0] // count

    def chunk(offset):
        at = jnp.clip(place + offset, 0, count - 1)
        return lax.dynamic_slice_in_dim(partial, at * rows, rows, 0)

    up = chunk(count - 1)
    down = chunk(1 - count)
    for step in range(count - 1, 0, -1):
        up = lax.ppermute(up.astype(BF), "dp", [(i, i + 1) for i in range(count - step)])
        down = lax.ppermute(
            down.astype(BF), "dp", [(i + 1, i) for i in range(step - 1, count - 1)]
        )
        if step > 1:
            up = up.astype(F32) + chunk(step - 1).astype(F32)
            down = down.astype(F32) + chunk(1 - step).astype(F32)
    return chunk(0).astype(F32) + up.astype(F32) + down.astype(F32)


def spread_columns(piece, places, parts):
    rows, width = piece.shape
    each = width // parts
    pieces = plane_gather(piece)
    total = len(pieces)
    whole = jnp.zeros((rows, parts * total * each), F32)
    for relative, block in enumerate(pieces):
        for part in range(parts):
            whole = lax.dynamic_update_slice(
                whole,
                block[:, part * each : (part + 1) * each].astype(F32),
                (0, (part * total + places[relative]) * each),
            )
    return whole


def turn(values, cosine, sine):
    low = values[:, : cosine.shape[1]]
    lane = lax.broadcasted_iota(jnp.int32, low.shape, 1)
    half = ROT // 2
    partner = jnp.where(
        lane < half, pltpu.roll(low, low.shape[1] - half, 1), pltpu.roll(low, half, 1)
    )
    return jnp.concatenate([low * cosine + partner * sine, values[:, cosine.shape[1] :]], axis=1)


def attention_kernel(
    order, first, qkv, bias, upstream, cosine, sine, context, context_rel, grads, keys, values,
    score, prob_grad, key_sum, value_sum,
):
    step = pl.program_id(0)
    total = pl.num_programs(0)
    size = HEAD_SIZE
    span = qkv.shape[1]
    last = (((1,), (1,)), ((), ()))
    rows = (((0,), (0,)), ((), ()))
    mine = order[step]
    start = first[step]
    cos_here, sin_here = cosine[mine], sine[mine]
    joined = qkv[0] + bias[...]
    query = (turn(joined[:, :size], cos_here, sin_here) * (size**-0.5)).astype(BF)
    at = pl.ds(pl.multiple_of(step * span, span), span)
    keys[at, :] = turn(joined[:, size : 2 * size], cos_here, sin_here).astype(BF)
    values[at, :] = joined[:, 2 * size :].astype(BF)
    key_sum[at, :] = jnp.zeros((span, size), F32)
    value_sum[at, :] = jnp.zeros((span, size), F32)
    up = upstream[0]

    def one(count):
        blocks = [slice(i * span, (i + 1) * span) for i in range(count)]
        top = jnp.full((span, 1), NEG_FILL, F32)
        for i, block in enumerate(blocks):
            part = lax.dot_general(query, keys[block, :], last, preferred_element_type=F32)
            if i == count - 1:
                row = lax.broadcasted_iota(jnp.int32, part.shape, 0)
                column = lax.broadcasted_iota(jnp.int32, part.shape, 1)
                part = jnp.where(column <= row, part, NEG_FILL)
            else:
                part = part + jnp.where(i >= start, 0.0, NEG_FILL)
            score[:, block] = part
            top = jnp.maximum(top, jnp.max(part, axis=1, keepdims=True))
        norm = jnp.zeros((span, 1), F32)
        for block in blocks:
            part = jnp.exp(score[:, block] - top)
            score[:, block] = part
            norm = norm + jnp.sum(part, axis=1, keepdims=True)
        inverse = 1.0 / norm
        out = jnp.zeros((span, size), F32)
        inner = jnp.zeros((span, 1), F32)
        for block in blocks:
            probs = score[:, block] * inverse
            score[:, block] = probs
            grad = lax.dot_general(up, values[block, :], last, preferred_element_type=F32)
            prob_grad[:, block] = grad
            inner = inner + jnp.sum(probs * grad, axis=1, keepdims=True)
            low = probs.astype(BF)
            out = out + jnp.dot(low, values[block, :], preferred_element_type=F32)
            value_sum[block, :] += lax.dot_general(low, up, rows, preferred_element_type=F32)
        context[0] = out.astype(BF)
        context_rel[0] = out.astype(BF)
        query_grad = jnp.zeros((span, size), F32)
        for block in blocks:
            low = (score[:, block] * (prob_grad[:, block] - inner)).astype(BF)
            query_grad = query_grad + jnp.dot(low, keys[block, :], preferred_element_type=F32)
            key_sum[block, :] += lax.dot_general(low, query, rows, preferred_element_type=F32)
        query_grad = (query_grad * (size**-0.5)).astype(BF).astype(F32)
        grads[mine, :, :size] = turn(query_grad, cos_here, -sin_here).astype(BF)

    steps = keys.shape[0] // span
    for index in range(steps):
        pl.when(step == index)(functools.partial(one, index + 1))

    @pl.when(step == total - 1)
    def finish():
        def each(index, carry):
            place = order[index]
            block = pl.ds(pl.multiple_of(index * span, span), span)
            key_grad = key_sum[block, :].astype(BF).astype(F32)
            grads[place, :, size : 2 * size] = turn(key_grad, cosine[place], -sine[place]).astype(
                BF
            )
            grads[place, :, 2 * size :] = value_sum[block, :].astype(BF)
            return carry

        lax.fori_loop(0, total, each, 0)


def attention(order, first, qkv, bias, upstream, cosine, sine):
    count, span, width = qkv.shape
    size = HEAD_SIZE
    length = count * span
    whole = lambda *shape: pl.BlockSpec(shape, lambda i, o, f: (0,) * len(shape))
    taken = lambda *shape: pl.BlockSpec(
        (1,) + shape, lambda i, o, f: (o[i],) + (0,) * len(shape)
    )
    pairs = count * (count + 1) // 2
    return pl.pallas_call(
        attention_kernel,
        grid_spec=pltpu.PrefetchScalarGridSpec(
            num_scalar_prefetch=2,
            grid=(count,),
            in_specs=[
                taken(span, width),
                whole(1, width),
                taken(span, size),
                whole(count, span, cosine.shape[-1]),
                whole(count, span, cosine.shape[-1]),
            ],
            out_specs=[
                pl.BlockSpec((1, span, size), lambda i, o, f: (i, 0, 0)),
                taken(span, size),
                whole(count, span, width),
            ],
            scratch_shapes=[
                pltpu.VMEM((length, size), BF),
                pltpu.VMEM((length, size), BF),
                pltpu.VMEM((span, length), F32),
                pltpu.VMEM((span, length), F32),
                pltpu.VMEM((length, size), F32),
                pltpu.VMEM((length, size), F32),
            ],
        ),
        out_shape=[
            jax.ShapeDtypeStruct((count, span, size), BF),
            jax.ShapeDtypeStruct((count, span, size), BF),
            jax.ShapeDtypeStruct((count, span, width), BF),
        ],
        compiler_params=pltpu.CompilerParams(vmem_limit_bytes=40 * 2**20),
        cost_estimate=pl.CostEstimate(
            flops=pairs * span * span * size * 12 * 2,
            bytes_accessed=length * (width * 6 + size * 6 + 1024),
            transcendentals=pairs * span * span,
        ),
        name="attention",
    )(order, first, qkv, bias, upstream, cosine, sine)


def body(
    block_in,
    cotangent,
    seg_lengths,
    ln1_gain,
    ln1_bias,
    qkv_weight,
    qkv_bias,
    out_weight,
    out_bias,
    ln2_gain,
    ln2_bias,
    fc1_weight,
    fc1_bias,
    fc2_weight,
    fc2_bias,
):
    rows_here, span, width = block_in.shape
    shard, hidden_units = fc1_weight.shape
    data_count = lax.axis_size("dp")
    head_count = lax.axis_size("head")
    blk_count = lax.axis_size("blk")
    plane = head_count * blk_count
    head_place = lax.axis_index("head")
    blk_place = lax.axis_index("blk")
    place = head_place * blk_count + blk_place
    contract_last = (((1,), (1,)), ((), ()))
    contract = (((0,), (0,)), ((), ()))
    each = hidden_units // plane
    length = plane * span

    places = [
        (head_place ^ (r % head_count)) * blk_count + (blk_place ^ (r // head_count))
        for r in range(plane)
    ]
    absolute = jnp.arange(plane, dtype=jnp.int32)
    order = (absolute % blk_count ^ blk_place) * head_count + (absolute // blk_count ^ head_place)

    def columns(values, wide):
        return lax.dynamic_slice_in_dim(values, place * wide, wide, 1)

    out_mine = data_gather(columns(out_weight, HEAD_SIZE))
    qkv_mine = data_gather(
        jnp.concatenate(
            [
                columns(qkv_weight[:, part * width : (part + 1) * width], HEAD_SIZE)
                for part in range(3)
            ],
            axis=1,
        )
    )
    fc1_mine = data_gather(columns(fc1_weight, each))
    fc2_mine = data_gather(columns(fc2_weight, each))
    own_in = block_in.reshape(span, width)
    own_up = cotangent.reshape(span, width)
    tokens = jnp.concatenate(plane_gather(own_in), axis=0)
    upstream = jnp.concatenate(plane_gather(own_up), axis=0)

    lengths = seg_lengths.reshape(-1)
    starts = jnp.stack([jnp.sum(lengths[:i]) for i in range(lengths.shape[0])])
    block_at = absolute * span
    block_start = jnp.max(
        jnp.where(starts[None, :] <= block_at[:, None], starts[None, :], 0), axis=1
    ).astype(jnp.int32)
    first = block_start // span
    relative_at = jnp.stack(places)
    seg_at = jnp.max(
        jnp.where(starts[None, :] <= relative_at[:, None] * span, starts[None, :], 0), axis=1
    )
    offset = (relative_at * span - seg_at)[:, None] + jnp.arange(span, dtype=jnp.int32)[None, :]
    half = ROT // 2
    frequency = ROT_BASE ** (-(2.0 * jnp.arange(half, dtype=F32)) / ROT)
    angles = offset.astype(F32)[..., None] * frequency
    cosine, sine = jnp.cos(angles), jnp.sin(angles)
    rest = jnp.zeros((plane, span, 128 - ROT), F32)
    cosine = jnp.concatenate([cosine, cosine, rest + 1.0], axis=-1)
    sine = jnp.concatenate([-sine, sine, rest], axis=-1)

    inputs = tokens.astype(F32)
    centred = inputs - jnp.mean(inputs, axis=-1, keepdims=True)
    scaled = lax.rsqrt(jnp.mean(centred * centred, axis=-1, keepdims=True) + NORM_EPS)
    normed = centred * scaled
    attn_in = (normed * ln1_gain + ln1_bias).astype(BF)
    mlp_in = (normed * ln2_gain + ln2_bias).astype(BF)

    out_pieces = plane_gather(out_mine)
    out_full = jnp.zeros((width, width), BF)
    for relative, block in enumerate(out_pieces):
        out_full = lax.dynamic_update_slice(
            out_full, block, (0, places[relative] * HEAD_SIZE)
        )
    out_rows = lax.dynamic_slice_in_dim(out_full, place * HEAD_SIZE, HEAD_SIZE, 0)
    context_grad = lax.dot_general(
        upstream, out_rows, contract_last, preferred_element_type=F32
    ).astype(BF)
    joined = jnp.dot(attn_in, qkv_mine, preferred_element_type=F32)
    bias_mine = jnp.concatenate(
        [
            lax.dynamic_slice_in_dim(qkv_bias, part * width + place * HEAD_SIZE, HEAD_SIZE, 0)
            for part in range(3)
        ]
    ).astype(F32)
    context_abs, context, qkv_grad = attention(
        order.astype(jnp.int32),
        first,
        joined.reshape(plane, span, 3 * HEAD_SIZE),
        bias_mine[None, :],
        context_grad.reshape(plane, span, HEAD_SIZE),
        cosine,
        sine,
    )
    context = context.reshape(length, HEAD_SIZE)
    qkv_grad = qkv_grad.reshape(length, 3 * HEAD_SIZE)
    own_context = lax.all_to_all(
        context_abs.reshape(length, HEAD_SIZE),
        ("head", "blk"),
        split_axis=0,
        concat_axis=1,
        tiled=True,
    )
    attn_out = jnp.dot(own_context, out_full, preferred_element_type=F32) + out_bias
    out_grad = lax.dot_general(context, upstream, contract, preferred_element_type=F32).astype(BF)
    out_grad = lax.all_to_all(out_grad, ("head", "blk"), split_axis=1, concat_axis=0, tiled=True)
    qkv_w_grad = lax.dot_general(attn_in, qkv_grad, contract, preferred_element_type=F32).astype(BF)
    attn_in_grad = lax.dot_general(
        qkv_grad, qkv_mine, contract_last, preferred_element_type=F32
    )

    hidden = jnp.dot(mlp_in, fc1_mine, preferred_element_type=F32)
    hidden = hidden + lax.dynamic_slice_in_dim(fc1_bias, place * each, each, 0)
    phi = 0.5 * (1.0 + lax.erf(hidden * (0.5**0.5)))
    active = (hidden * phi).astype(BF)
    slope = phi + hidden * jnp.exp(-0.5 * hidden * hidden) * ((2.0 * jnp.pi) ** -0.5)
    fc2_grad = lax.dot_general(upstream, active, contract, preferred_element_type=F32).astype(BF)
    mlp_part = lax.dot_general(
        active, fc2_mine, contract_last, preferred_element_type=F32
    ).astype(BF)
    hidden_grad = (jnp.dot(upstream, fc2_mine, preferred_element_type=F32) * slope).astype(BF)
    fc1_grad = lax.dot_general(mlp_in, hidden_grad, contract, preferred_element_type=F32).astype(BF)
    mlp_in_grad = lax.dot_general(
        hidden_grad, fc1_mine, contract_last, preferred_element_type=F32
    )

    mlp_out = plane_scatter(mlp_part, span) + fc2_bias
    own_float = own_in.astype(F32)
    block_out = (own_float + attn_out + mlp_out).astype(BF).reshape(block_in.shape)

    share_part = (attn_in_grad * ln1_gain + mlp_in_grad * ln2_gain).astype(BF)
    share = plane_scatter(share_part, span)
    own_centred = own_float - jnp.mean(own_float, axis=-1, keepdims=True)
    own_scaled = lax.rsqrt(jnp.mean(own_centred * own_centred, axis=-1, keepdims=True) + NORM_EPS)
    own_normed = own_centred * own_scaled
    share = own_scaled * (
        share
        - jnp.mean(share, axis=-1, keepdims=True)
        - own_normed * jnp.mean(share * own_normed, axis=-1, keepdims=True)
    )
    input_grad = (own_up.astype(F32) + share).astype(BF).reshape(block_in.shape)

    fc2_out = spread_columns(data_scatter(fc2_grad).astype(BF), places, 1)
    fc1_out = spread_columns(data_scatter(fc1_grad).astype(BF), places, 1)
    out_out = spread_columns(data_scatter(out_grad).astype(BF), places, 1)
    qkv_out = spread_columns(data_scatter(qkv_w_grad).astype(BF), places, 3)

    qkv_bias_part = jnp.sum(qkv_grad.astype(F32), axis=0).reshape(3, 1, HEAD_SIZE)
    here = (jnp.arange(plane) == place).astype(F32)
    qkv_bias_part = (qkv_bias_part * here[None, :, None]).reshape(-1)
    fc1_bias_part = (
        here[:, None] * jnp.sum(hidden_grad.astype(F32), axis=0)[None, :]
    ).reshape(-1)
    reduced = lax.psum(
        (
            jnp.sum(attn_in_grad * normed, axis=0),
            jnp.sum(attn_in_grad, axis=0),
            qkv_bias_part,
            jnp.sum(own_up.astype(F32), axis=0),
            jnp.sum(mlp_in_grad * normed, axis=0),
            jnp.sum(mlp_in_grad, axis=0),
            fc1_bias_part,
            jnp.stack([jnp.sum(attn_out * attn_out), jnp.sum(mlp_out * mlp_out)]),
        ),
        ("dp", "head", "blk"),
    )
    entries = rows_here * length * data_count * width
    branch_rms = jnp.sqrt(reduced[7] / entries)
    return (
        block_out,
        input_grad,
        reduced[0],
        reduced[1],
        qkv_out,
        reduced[2],
        out_out,
        reduced[3],
        reduced[4],
        reduced[5],
        fc1_out,
        reduced[6],
        fc2_out,
        reduced[3],
        branch_rms[0],
        branch_rms[1],
    )


def solution(mesh):
    rows, tokens, whole = P("dp", None), P("dp", ("head", "blk"), None), P()
    return jax.shard_map(
        body,
        mesh=mesh,
        in_specs=(
            tokens,
            tokens,
            rows,
            whole,
            whole,
            rows,
            whole,
            rows,
            whole,
            whole,
            whole,
            rows,
            whole,
            rows,
            whole,
        ),
        out_specs=(
            tokens,
            tokens,
            whole,
            whole,
            rows,
            whole,
            rows,
            whole,
            whole,
            whole,
            rows,
            whole,
            rows,
            whole,
            whole,
            whole,
        ),
        check_vma=False,
    )
```

time: 4050 us -> 1030 us (0.25)
  waiting for transfers between devices: 3510 us -> 422 us
  starting transfers between devices: 13.1 us -> 173 us
  matrix products: 258 us -> 134 us
  other arithmetic: 101 us -> 156 us
    reduce_scatter x3 -> x0, waiting for transfers between devices: 1570 us -> none  [the longest x1 1570 us: body(): lax.psum_scatter(jnp.concatenate([lax.dot_general(attn_in, qkv_grad, cont...]
    all_gather x6 -> x0, waiting for transfers between devices: 1470 us -> none  [the longest x1 513 us: body(): lax.all_gather(fc2_weight, 'dp', axis=0, tiled=True)]
    psum x2 -> x1, waiting for transfers between devices: 445 us -> 121 us  [body(): lax.psum((jnp.sum(attn_in_grad * normed, axis=0), jnp.sum(attn_in_grad, a...]
    ppermute x0 -> x114, waiting for transfers between devices: none -> 301 us  [the longest x36 144 us: across(): return lax.ppermute(values, 'head', [(i, i ^ offset) for i in range(count)])]
    ppermute x0 -> x114, starting transfers between devices: none -> 165 us  [the longest x12 67.1 us: data_scatter(): lax.ppermute(up.astype(BF), 'dp', [(i, i + 1) for i in range(count - step)])]
    dot_general x18 -> x12, matrix products: 258 us -> 134 us  [the longest x1 23.2 us: body(): lax.dot_general(hidden_grad, fc1_mine, contract_last, preferred_element_t...]
    dynamic_update_slice x0 -> x60, other arithmetic: none -> 81.3 us  [the longest x48 71.8 us: spread_columns(): lax.dynamic_update_slice(whole, block[:, part * each:(part + 1) * each].a...]
    concatenate x1 -> x4, other arithmetic: 65.7 us -> 3.66 us  [the longest x1 2.52 us: body(): cosine = jnp.concatenate([cosine, cosine, rest + 1.0], axis=-1)]
  transfers between devices with their start and end apart: 14 -> 117, of which waited for: 9 -> 40; matrix products, arithmetic and copies ran while one was open for 8% -> 36% of each run, Pallas kernels for 0% -> 2%
where the time goes in v1:
time: 1030 us; the launch traced here: 1020 us
  waiting for transfers between devices  422 us (41%)
  starting transfers between devices  173 us (17%)
  other arithmetic  156 us (15%)
  matrix products  134 us (13%)
  local copies, waits for them, and re-layouts  99.2 us (10%)
  Pallas kernels  20.2 us (2%)
  between operations  16.3 us (2%)
    ppermute x36, waiting for transfers between devices, across(): return lax.ppermute(values, 'head', [(i, i ^ offset) for i in range(count)])  144 us
    psum x1, waiting for transfers between devices, body(): lax.psum((jnp.sum(attn_in_grad * normed, axis=0), jnp.sum(attn_in_grad, a...  121 us
    ppermute x12, waiting for transfers between devices, data_gather(): down = lax.ppermute(down, 'dp', [(i + 1, i) for i in range(count - step)])  90.6 us
    dynamic_update_slice x48, other arithmetic, spread_columns(): lax.dynamic_update_slice(whole, block[:, part * each:(part + 1) * each].a...  71.8 us
    ppermute x12, starting transfers between devices, data_scatter(): lax.ppermute(up.astype(BF), 'dp', [(i, i + 1) for i in range(count - step)])  67.1 us
    ppermute x12, waiting for transfers between devices, data_scatter(): lax.ppermute(up.astype(BF), 'dp', [(i, i + 1) for i in range(count - step)])  43 us
    ppermute x36, starting transfers between devices, across(): return lax.ppermute(values, 'head', [(i, i ^ offset) for i in range(count)])  35.9 us
    unnamed x159, local copies, waits for them, and re-layouts  30.8 us
  transfers between devices with their start and end apart: 117, of which 40 were waited for; matrix products, arithmetic and copies ran while one was open for 36% of the time, Pallas kernels for 2%

profile of v1, /device:TPU:0, one launch (start us, length us, event | category | flops | bytes accessed | tf_op | source)
XLA Modules:
  0.0 1021.0 jit_solution(6378973295635910925)
XLA Ops:
  32.9 6.0 fusion.64
  64.5 8.9 collective-permute-done.26
  76.4 6.5 collective-permute-done.27
  100.6 8.4 collective-permute-done.15
  110.6 9.6 collective-permute-done.2
  130.3 6.1 collective-permute-done.17
  139.4 19.1 %collective-permute-done.28 = bf16[2048,256]{1,0:T(8,128)(2,1)S(1)} collective-permute-done((bf16[2048,256]{1,0:T(8,128)(2,1)S(1)}, bf16[2048,256]{1,0:T(8,128)(2,1)S(1)}, u32[]{:S(2)}, u32[]{:S(2)}) %collective-permute-start.28) | collective-permute-done | bytes 1048608 | tf_op jit(solution)/shard_map/ppermute | solution.py:22
  166.3 8.8 collective-permute-done.30
  178.9 9.9 collective-permute-done.31
  188.8 5.5 collective-permute-start.37
  195.6 12.2 %collective-permute-done.12 = bf16[512,768]{1,0:T(8,128)(2,1)S(1)} collective-permute-done((bf16[512,768]{1,0:T(8,128)(2,1)S(1)}, bf16[512,768]{1,0:T(8,128)(2,1)S(1)}, u32[]{:S(2)}, u32[]{:S(2)}) %collective-permute-start.12) | collective-permute-done | bytes 786464 | tf_op jit(solution)/shard_map/ppermute | solution.py:63
  218.6 11.9 %collective-permute-done.42 = bf16[512,1024]{1,0:T(8,128)(2,1)} collective-permute-done((bf16[512,1024]{1,0:T(8,128)(2,1)S(1)}, bf16[512,1024]{1,0:T(8,128)(2,1)}, u32[]{:S(2)}, u32[]{:S(2)}) %collective-permute-start.42) | collective-permute-done | bytes 1048608 | tf_op jit(solution)/shard_map/ppermute | solution.py:63
  231.7 5.7 collective-permute-done.43
  238.6 8.6 collective-permute-done.13
  256.8 13.0 %collective-permute-done.40 = bf16[512,1024]{1,0:T(8,128)(2,1)} collective-permute-done((bf16[512,1024]{1,0:T(8,128)(2,1)}, bf16[512,1024]{1,0:T(8,128)(2,1)}, u32[]{:S(2)}, u32[]{:S(2)}) %collective-permute-start.40) | collective-permute-done | bytes 1048608 | tf_op jit(solution)/shard_map/ppermute | solution.py:63
  270.5 8.5 fusion.69
  282.6 9.6 collective-permute-done.46
  299.9 14.7 %collective-permute-done.41 = bf16[512,1024]{1,0:T(8,128)(2,1)S(1)} collective-permute-done((bf16[512,1024]{1,0:T(8,128)(2,1)}, bf16[512,1024]{1,0:T(8,128)(2,1)S(1)}, u32[]{:S(2)}, u32[]{:S(2)}) %collective-permute-start.41) | collective-permute-done | bytes 1048608 | tf_op jit(solution)/shard_map/ppermute | solution.py:63
  315.0 12.9 %multiply_convert_fusion = (bf16[2048,1024]{1,0:T(8,128)(2,1)}, f32[2048,1024]{1,0:T(8,128)}) fusion(f32[1024]{0:T(1024)S(1)} %dynamic-slice_convert_fusion, bf16[2048,1024]{1,0:T(8,128)(2,1)S(1)} %select_dynamic-update-slice_fusion.3, bf16[2048,2048]{1,0:T(8,128)(2,1)S(1)} %constant_dynamic-update-slice_fusion, f32[2048]{0:T(1024)S(1)} %convert_element_type.524, ...), kind=kOutput, calls=%fused_computation.26 | convolution fusion | flops 8627683328 | bytes 25202688 | tf_op jit(solution)/shard_map/dot_general | solution.py:382
  337.2 11.0 %convolution_convert_fusion = bf16[2048,2048]{1,0:T(8,128)(2,1)} fusion(bf16[2048,1024]{1,0:T(8,128)(2,1)S(1)} %copy-done.57, bf16[2048,1024]{1,0:T(8,128)(2,1)S(1)} %select_dynamic-update-slice_fusion), kind=kOutput, calls=%fused_computation.28 | convolution fusion | flops 8594128896 | bytes 16777216 | tf_op jit(solution)/shard_map/dot_general | solution.py:388
  348.2 16.2 %convert_reduce_fusion.1 = (f32[1024]{0:T(1024)S(1)}, bf16[2048,1024]{1,0:T(8,128)(2,1)}) fusion(f32[2048,1024]{1,0:T(8,128)} %get-tuple-element.109, f32[1024]{0:T(1024)S(1)} %dynamic-slice_convert_fusion, bf16[2048,2048]{1,0:T(8,128)(2,1)} %constant_dynamic-update-slice_fusion.9, bf16[2048,1024]{1,0:T(8,128)(2,1)S(1)} %select_dynamic-update-slice_fusion), kind=kOutput, calls=%fused_computation.23 | convolution fusion | flops 8617196544 | bytes 25174016 | tf_op jit(solution)/shard_map/dot_general | solution.py:391
  364.4 13.4 %convolution_convert_fusion.2 = bf16[2048,1024]{1,0:T(8,128)(2,1)S(1)} fusion(bf16[2048,1024]{1,0:T(8,128)(2,1)} %get-tuple-element.111, bf16[2048,2048]{1,0:T(8,128)(2,1)S(1)} %constant_dynamic-update-slice_fusion, f32[2048]{0:T(1024)S(1)} %convert_element_type.524, f32[2048]{0:T(1024)S(1)} %convert_element_type.523, f32[2048]{0:T(1024)S(1)} %add_rsqrt_fusion, ...), kind=kOutput, calls=%fused_computation.31 | convolution fusion | flops 8617197568 | bytes 16809984 | tf_op jit(solution)/shard_map/dot_general | solution.py:392
  377.8 13.1 %convolution_convert_fusion.1 = bf16[2048,1024]{1,0:T(8,128)(2,1)S(1)} fusion(bf16[2048,2048]{1,0:T(8,128)(2,1)} %constant_dynamic-update-slice_fusion.9, bf16[2048,1024]{1,0:T(8,128)(2,1)S(1)} %copy-done.57), kind=kOutput, calls=%fused_computation.30 | convolution fusion | flops 8592031744 | bytes 16777216 | tf_op jit(solution)/shard_map/dot_general | solution.py:387
  403.9 6.2 convolution_convert_fusion.5
  410.1 20.2 %attention.1 = (bf16[8,256,256]{2,1,0:T(8,128)(2,1)S(1)}, bf16[8,256,256]{2,1,0:T(8,128)(2,1)S(1)}, bf16[8,256,768]{2,1,0:T(8,128)(2,1)S(1)}) custom-call(s32[8]{0:T(128)S(1)} %get-tuple-element.113.order, s32[8]{0:T(128)S(1)} %get-tuple-element.112.first, f32[8,256,768]{2,1,0:T(8,128)} %bitcast.129, f32[1,768]{1,0:T(1,128)S(1)} %maximum_convert_fusion.bias, ...), custom_call_target="tpu_custom_call" | custom-call | flops 14495514624 | bytes 14680064 | tf_op jit(solution)/shard_map/attention/pallas_call | solution.py:213
  430.3 9.7 fusion.70
  440.0 7.4 convolution_convert_fusion.3
  452.6 5.7 convolution_convert_fusion.4
  463.8 23.2 %fusion.58 = (f32[2048]{0:T(1024)}, f32[2048]{0:T(1024)}, bf16[2048,2048]{1,0:T(8,128)(2,1)}, f32[2048]{0:T(1024)}, f32[2048]{0:T(1024)}) fusion(f32[2048]{0:T(1024)S(1)} %add_rsqrt_fusion, f32[2048]{0:T(1024)S(1)} %broadcast_multiply_fusion, bf16[2048,2048]{1,0:T(8,128)(2,1)} %copy-done.1, f32[2048]{0:T(1024)S(1)} %convert_element_type.523, ...), kind=kOutput, calls=%fused_computation.264 | convolution fusion | flops 8644452352 | bytes 42008576 | tf_op jit(solution)/shard_map/dot_general | solution.py:393
  520.4 19.3 %collective-permute-done.73 = bf16[512,256]{1,0:T(8,128)(2,1)S(1)} collective-permute-done((bf16[512,256]{1,0:T(8,128)(2,1)S(1)}, bf16[512,256]{1,0:T(8,128)(2,1)S(1)}, u32[]{:S(2)}, u32[]{:S(2)}) %collective-permute-start.73) | collective-permute-done | bytes 262176 | tf_op jit(solution)/shard_map/ppermute | solution.py:87
  544.9 7.5 collective-permute-start.87
  558.9 5.5 collective-permute-start.101
  569.1 22.0 %collective-permute-start.74 = (bf16[512,256]{1,0:T(8,128)(2,1)S(1)}, bf16[512,256]{1,0:T(8,128)(2,1)S(1)}, u32[]{:S(2)}, u32[]{:S(2)}) collective-permute-start(bf16[512,256]{1,0:T(8,128)(2,1)S(1)} %get-tuple-element.92), channel_id=1, source_target_pairs={{0,8},{8,16},{16,24},{1,9},{9,17},{17,25},{2,10},{10,18},{18,26},{... | collective-permute-start | bytes 786440 | tf_op jit(solution)/shard_map/ppermute | solution.py:87
  593.4 12.6 %collective-permute-done.74 = bf16[512,256]{1,0:T(8,128)(2,1)S(1)} collective-permute-done((bf16[512,256]{1,0:T(8,128)(2,1)S(1)}, bf16[512,256]{1,0:T(8,128)(2,1)S(1)}, u32[]{:S(2)}, u32[]{:S(2)}) %collective-permute-start.74) | collective-permute-done | bytes 262176 | tf_op jit(solution)/shard_map/ppermute | solution.py:87
  643.0 5.9 collective-permute-start.102
  652.7 7.0 collective-permute-done.91
  670.9 10.4 %collective-permute-done.105 = bf16[512,1024]{1,0:T(8,128)(2,1)} collective-permute-done((bf16[512,1024]{1,0:T(8,128)(2,1)}, bf16[512,1024]{1,0:T(8,128)(2,1)}, u32[]{:S(2)}, u32[]{:S(2)}) %collective-permute-start.105) | collective-permute-done | bytes 1048608 | tf_op jit(solution)/shard_map/ppermute | solution.py:88
  719.6 10.0 collective-permute-done.92
  729.6 5.7 convert_add_fusion.1
  740.5 10.3 %collective-permute-done.106 = bf16[512,1024]{1,0:T(8,128)(2,1)S(1)} collective-permute-done((bf16[512,1024]{1,0:T(8,128)(2,1)}, bf16[512,1024]{1,0:T(8,128)(2,1)S(1)}, u32[]{:S(2)}, u32[]{:S(2)}) %collective-permute-start.106) | collective-permute-done | bytes 1048608 | tf_op jit(solution)/shard_map/ppermute | solution.py:22
  768.6 5.5 convert_add_fusion
  784.1 10.6 %collective-permute-done.95 = bf16[256,1024]{1,0:T(8,128)(2,1)S(1)} collective-permute-done((bf16[256,1024]{1,0:T(8,128)(2,1)}, bf16[256,1024]{1,0:T(8,128)(2,1)S(1)}, u32[]{:S(2)}, u32[]{:S(2)}) %collective-permute-start.95) | collective-permute-done | bytes 524320 | tf_op jit(solution)/shard_map/ppermute | solution.py:22
  798.0 10.0 collective-permute-done.109
  832.8 11.6 %collective-permute-done.54 = bf16[2,256,1024]{2,1,0:T(8,128)(2,1)S(1)} collective-permute-done((bf16[2,256,1024]{2,1,0:T(8,128)(2,1)S(1)}, bf16[2,256,1024]{2,1,0:T(8,128)(2,1)S(1)}, u32[]{:S(2)}, u32[]{:S(2)}) %collective-permute-start.54) | collective-permute-done | bytes 1048608 | tf_op jit(solution)/shard_map/ppermute | solution.py:22
  855.4 5.9 collective-permute-done.50
  863.3 6.3 collective-permute-done.55
  870.1 6.6 multiply_reduce_fusion
  881.7 120.6 %all-reduce.3.cloned.1.call-done = (f32[2048]{0:T(1024)}, f32[2048]{0:T(1024)}, f32[6144]{0:T(1024)}, f32[2048]{0:T(1024)}, f32[2048]{0:T(1024)}, /*index=5*/f32[2048]{0:T(1024)}, f32[8192]{0:T(1024)}, f32[2]{0:T(128)}) async-done(((f32[2048]{0:T(1024)}, f32[2048]{0:T(1024)}, f32[6144]{0:T(1024)}, f32[2048]{0:T(1024)}, f32[2048]{0:T(1024)}, /*index=5*/f32[2048]{0:T(1024)}, f32[8192]{0:T(1024)}, ...) | async-done | bytes 98328 | tf_op jit(solution)/shard_map/psum | solution.py:424
  (554 shorter events, 399.2 us)
Async XLA Ops:
  7.2 81.9 %collective-permute-start = (bf16[256,2048]{1,0:T(8,128)(2,1)}, bf16[256,2048]{1,0:T(8,128)(2,1)}, u32[]{:S(2)}, u32[]{:S(2)}) collective-permute-start(bf16[256,2048]{1,0:T(8,128)(2,1)} %bitcast.111), channel_id=1, source_target_pairs={{0,2},{2,0},{4,6},{6,4},{1,3},{3,1},{5,7},{7,5},{8,10},{10,8},{12,... | collective-permute-start | bytes 3145736 | tf_op jit(solution)/shard_map/ppermute | solution.py:22
  10.2 82.4 %collective-permute-start.1 = (bf16[256,2048]{1,0:T(8,128)(2,1)}, bf16[256,2048]{1,0:T(8,128)(2,1)}, u32[]{:S(2)}, u32[]{:S(2)}) collective-permute-start(bf16[256,2048]{1,0:T(8,128)(2,1)} %bitcast.112), channel_id=1, source_target_pairs={{0,4},{2,6},{4,0},{6,2},{1,5},{3,7},{5,1},{7,3},{8,12},{10,14},{12... | collective-permute-start | bytes 3145736 | tf_op jit(solution)/shard_map/ppermute | solution.py:22
  11.7 111.6 %collective-permute-start.4 = (bf16[256,2048]{1,0:T(8,128)(2,1)}, bf16[256,2048]{1,0:T(8,128)(2,1)}, u32[]{:S(2)}, u32[]{:S(2)}) collective-permute-start(bf16[256,2048]{1,0:T(8,128)(2,1)} %bitcast.113), channel_id=1, source_target_pairs={{0,1},{1,0},{2,3},{3,2},{4,5},{5,4},{6,7},{7,6},{8,9},{9,8},{10,11... | collective-permute-start | bytes 3145736 | tf_op jit(solution)/shard_map/ppermute | solution.py:26
  13.5 47.3 %collective-permute-start.22 = (bf16[512,256]{1,0:T(8,128)(2,1)}, bf16[512,256]{1,0:T(8,128)(2,1)}, u32[]{:S(2)}, u32[]{:S(2)}) collective-permute-start(bf16[512,256]{1,0:T(8,128)(2,1)} %get-tuple-element.47), channel_id=1, source_target_pairs={{8,0},{16,8},{24,16},{9,1},{17,9},{25,17},{10,2},{18,10},{26,18},{... | collective-permute-start | bytes 786440 | tf_op jit(solution)/shard_map/ppermute | solution.py:63
  14.8 42.8 %collective-permute-start.23 = (bf16[512,256]{1,0:T(8,128)(2,1)}, bf16[512,256]{1,0:T(8,128)(2,1)}, u32[]{:S(2)}, u32[]{:S(2)}) collective-permute-start(bf16[512,256]{1,0:T(8,128)(2,1)} %get-tuple-element.47), channel_id=1, source_target_pairs={{0,8},{8,16},{16,24},{1,9},{9,17},{17,25},{2,10},{10,18},{18,26},{... | collective-permute-start | bytes 786440 | tf_op jit(solution)/shard_map/ppermute | solution.py:62
  89.1 32.6 %collective-permute-start.9 = (bf16[512,768]{1,0:T(8,128)(2,1)}, bf16[512,768]{1,0:T(8,128)(2,1)S(1)}, u32[]{:S(2)}, u32[]{:S(2)}) collective-permute-start(bf16[512,768]{1,0:T(8,128)(2,1)} %get-tuple-element.98), channel_id=1, source_target_pairs={{0,8},{8,16},{16,24},{1,9},{9,17},{17,25},{2,10},{10,18},{18,26},{... | collective-permute-start | bytes 2359304 | tf_op jit(solution)/shard_map/ppermute | solution.py:62
  123.3 35.2 %collective-permute-start.28 = (bf16[2048,256]{1,0:T(8,128)(2,1)S(1)}, bf16[2048,256]{1,0:T(8,128)(2,1)S(1)}, u32[]{:S(2)}, u32[]{:S(2)}) collective-permute-start(bf16[2048,256]{1,0:T(8,128)(2,1)S(1)} %select_dynamic-update-slice_fusion.9), channel_id=1, source_target_pairs={{0,2},{2,0},{4,6},{6,4},{1,3},{3,1},{5,7},{7,5},{8,10},{10,8},{12,... | collective-permute-start | bytes 3145736 | tf_op jit(solution)/shard_map/ppermute | solution.py:22
  163.9 50.0 %collective-permute-start.32 = (bf16[2048,256]{1,0:T(8,128)(2,1)S(1)}, bf16[2048,256]{1,0:T(8,128)(2,1)S(1)}, u32[]{:S(2)}, u32[]{:S(2)}) collective-permute-start(bf16[2048,256]{1,0:T(8,128)(2,1)S(1)} %select_dynamic-update-slice_fusion.9), channel_id=1, source_target_pairs={{0,1},{1,0},{2,3},{3,2},{4,5},{5,4},{6,7},{7,6},{8,9},{9,8},{10,11... | collective-permute-start | bytes 3145736 | tf_op jit(solution)/shard_map/ppermute | solution.py:26
  164.2 43.6 %collective-permute-start.12 = (bf16[512,768]{1,0:T(8,128)(2,1)S(1)}, bf16[512,768]{1,0:T(8,128)(2,1)S(1)}, u32[]{:S(2)}, u32[]{:S(2)}) collective-permute-start(bf16[512,768]{1,0:T(8,128)(2,1)S(1)} %collective-permute-done.8), channel_id=1, source_target_pairs={{8,0},{16,8},{9,1},{17,9},{10,2},{18,10},{11,3},{19,11},{12,4},{20... | collective-permute-start | bytes 2359304 | tf_op jit(solution)/shard_map/ppermute | solution.py:63
  165.6 48.3 %collective-permute-start.11 = (bf16[512,768]{1,0:T(8,128)(2,1)S(1)}, bf16[512,768]{1,0:T(8,128)(2,1)S(1)}, u32[]{:S(2)}, u32[]{:S(2)}) collective-permute-start(bf16[512,768]{1,0:T(8,128)(2,1)S(1)} %collective-permute-done.10), channel_id=1, source_target_pairs={{16,24},{17,25},{18,26},{19,27},{20,28},{21,29},{22,30},{23,31}} | collective-permute-start | bytes 2359304 | tf_op jit(solution)/shard_map/ppermute | solution.py:62
  194.3 36.1 %collective-permute-start.42 = (bf16[512,1024]{1,0:T(8,128)(2,1)S(1)}, bf16[512,1024]{1,0:T(8,128)(2,1)}, u32[]{:S(2)}, u32[]{:S(2)}) collective-permute-start(bf16[512,1024]{1,0:T(8,128)(2,1)S(1)} %copy-done.34), channel_id=1, source_target_pairs={{8,0},{16,8},{24,16},{9,1},{17,9},{25,17},{10,2},{18,10},{26,18},{... | collective-permute-start | bytes 3145736 | tf_op jit(solution)/shard_map/ppermute | solution.py:63
  213.9 34.8 %collective-permute-start.7 = (bf16[256,2048]{1,0:T(8,128)(2,1)S(1)}, bf16[256,2048]{1,0:T(8,128)(2,1)S(1)}, u32[]{:S(2)}, u32[]{:S(2)}) collective-permute-start(bf16[256,2048]{1,0:T(8,128)(2,1)S(1)} %pad_maximum_fusion), channel_id=1, source_target_pairs={{0,1},{1,0},{2,3},{3,2},{4,5},{5,4},{6,7},{7,6},{8,9},{9,8},{10,11... | collective-permute-start | bytes 3145736 | tf_op jit(solution)/shard_map/ppermute | solution.py:26
  214.0 33.2 %collective-permute-start.13 = (bf16[512,768]{1,0:T(8,128)(2,1)S(1)}, bf16[512,768]{1,0:T(8,128)(2,1)S(1)}, u32[]{:S(2)}, u32[]{:S(2)}) collective-permute-start(bf16[512,768]{1,0:T(8,128)(2,1)S(1)} %collective-permute-done.12), channel_id=1, source_target_pairs={{8,0},{9,1},{10,2},{11,3},{12,4},{13,5},{14,6},{15,7}} | collective-permute-start | bytes 2359304 | tf_op jit(solution)/shard_map/ppermute | solution.py:63
  216.9 39.3 %collective-permute-start.38 = (bf16[512,1024]{1,0:T(8,128)(2,1)}, bf16[512,1024]{1,0:T(8,128)(2,1)}, u32[]{:S(2)}, u32[]{:S(2)}) collective-permute-start(bf16[512,1024]{1,0:T(8,128)(2,1)} %collective-permute-done.37), channel_id=1, source_target_pairs={{8,16},{16,24},{9,17},{17,25},{10,18},{18,26},{11,19},{19,27},{12,... | collective-permute-start | bytes 3145736 | tf_op jit(solution)/shard_map/ppermute | solution.py:62
  230.4 39.3 %collective-permute-start.40 = (bf16[512,1024]{1,0:T(8,128)(2,1)}, bf16[512,1024]{1,0:T(8,128)(2,1)}, u32[]{:S(2)}, u32[]{:S(2)}) collective-permute-start(bf16[512,1024]{1,0:T(8,128)(2,1)} %collective-permute-done.36), channel_id=1, source_target_pairs={{8,0},{16,8},{9,1},{17,9},{10,2},{18,10},{11,3},{19,11},{12,4},{20... | collective-permute-start | bytes 3145736 | tf_op jit(solution)/shard_map/ppermute | solution.py:63
  237.4 44.0 %collective-permute-start.44 = (bf16[512,1024]{1,0:T(8,128)(2,1)}, bf16[512,1024]{1,0:T(8,128)(2,1)S(1)}, u32[]{:S(2)}, u32[]{:S(2)}) collective-permute-start(bf16[512,1024]{1,0:T(8,128)(2,1)} %collective-permute-done.43), channel_id=1, source_target_pairs={{8,16},{16,24},{9,17},{17,25},{10,18},{18,26},{11,19},{19,27},{12,... | collective-permute-start | bytes 3145736 | tf_op jit(solution)/shard_map/ppermute | solution.py:62
  247.2 45.0 %collective-permute-start.46 = (bf16[512,1024]{1,0:T(8,128)(2,1)}, bf16[512,1024]{1,0:T(8,128)(2,1)}, u32[]{:S(2)}, u32[]{:S(2)}) collective-permute-start(bf16[512,1024]{1,0:T(8,128)(2,1)} %collective-permute-done.42), channel_id=1, source_target_pairs={{8,0},{16,8},{9,1},{17,9},{10,2},{18,10},{11,3},{19,11},{12,4},{20... | collective-permute-start | bytes 3145736 | tf_op jit(solution)/shard_map/ppermute | solution.py:63
  256.2 36.7 %collective-permute-start.33 = (bf16[2048,256]{1,0:T(8,128)(2,1)S(1)}, bf16[2048,256]{1,0:T(8,128)(2,1)S(1)}, u32[]{:S(2)}, u32[]{:S(2)}) collective-permute-start(bf16[2048,256]{1,0:T(8,128)(2,1)S(1)} %collective-permute-done.28), channel_id=1, source_target_pairs={{0,1},{1,0},{2,3},{3,2},{4,5},{5,4},{6,7},{7,6},{8,9},{9,8},{10,11... | collective-permute-start | bytes 3145736 | tf_op jit(solution)/shard_map/ppermute | solution.py:26
  281.3 33.3 %collective-permute-start.41 = (bf16[512,1024]{1,0:T(8,128)(2,1)}, bf16[512,1024]{1,0:T(8,128)(2,1)S(1)}, u32[]{:S(2)}, u32[]{:S(2)}) collective-permute-start(bf16[512,1024]{1,0:T(8,128)(2,1)} %collective-permute-done.40), channel_id=1, source_target_pairs={{8,0},{9,1},{10,2},{11,3},{12,4},{13,5},{14,6},{15,7}} | collective-permute-start | bytes 3145736 | tf_op jit(solution)/shard_map/ppermute | solution.py:63
  292.2 35.7 %collective-permute-start.45 = (bf16[512,1024]{1,0:T(8,128)(2,1)S(1)}, bf16[512,1024]{1,0:T(8,128)(2,1)S(1)}, u32[]{:S(2)}, u32[]{:S(2)}) collective-permute-start(bf16[512,1024]{1,0:T(8,128)(2,1)S(1)} %collective-permute-done.44), channel_id=1, source_target_pairs={{16,24},{17,25},{18,26},{19,27},{20,28},{21,29},{22,30},{23,31}} | collective-permute-start | bytes 3145736 | tf_op jit(solution)/shard_map/ppermute | solution.py:62
  293.0 43.8 %collective-permute-start.47 = (bf16[512,1024]{1,0:T(8,128)(2,1)}, bf16[512,1024]{1,0:T(8,128)(2,1)S(1)}, u32[]{:S(2)}, u32[]{:S(2)}) collective-permute-start(bf16[512,1024]{1,0:T(8,128)(2,1)} %collective-permute-done.46), channel_id=1, source_target_pairs={{8,0},{9,1},{10,2},{11,3},{12,4},{13,5},{14,6},{15,7}} | collective-permute-start | bytes 3145736 | tf_op jit(solution)/shard_map/ppermute | solution.py:63
  295.4 107.4 %collective-permute-start.35 = (bf16[2048,256]{1,0:T(8,128)(2,1)S(1)}, bf16[2048,256]{1,0:T(8,128)(2,1)S(1)}, u32[]{:S(2)}, u32[]{:S(2)}) collective-permute-start(bf16[2048,256]{1,0:T(8,128)(2,1)S(1)} %constant_dynamic-update-slice_fusion.18), channel_id=1, source_target_pairs={{0,1},{1,0},{2,3},{3,2},{4,5},{5,4},{6,7},{7,6},{8,9},{9,8},{10,11... | collective-permute-start | bytes 3145736 | tf_op jit(solution)/shard_map/ppermute | solution.py:26
  395.8 120.2 %collective-permute-start.86 = (bf16[512,1024]{1,0:T(8,128)(2,1)}, bf16[512,1024]{1,0:T(8,128)(2,1)}, u32[]{:S(2)}, u32[]{:S(2)}) collective-permute-start(bf16[512,1024]{1,0:T(8,128)(2,1)} %get-tuple-element.76), channel_id=1, source_target_pairs={{0,8},{1,9},{2,10},{3,11},{4,12},{5,13},{6,14},{7,15}} | collective-permute-start | bytes 3145736 | tf_op jit(solution)/shard_map/ppermute | solution.py:87
  399.6 119.3 %collective-permute-start.89 = (bf16[512,1024]{1,0:T(8,128)(2,1)}, bf16[512,1024]{1,0:T(8,128)(2,1)}, u32[]{:S(2)}, u32[]{:S(2)}) collective-permute-start(bf16[512,1024]{1,0:T(8,128)(2,1)} %get-tuple-element.77), channel_id=1, source_target_pairs={{24,16},{25,17},{26,18},{27,19},{28,20},{29,21},{30,22},{31,23}} | collective-permute-start | bytes 3145736 | tf_op jit(solution)/shard_map/ppermute | solution.py:88
  448.9 51.1 %collective-permute-start.58 = (bf16[512,768]{1,0:T(8,128)(2,1)}, bf16[512,768]{1,0:T(8,128)(2,1)}, u32[]{:S(2)}, u32[]{:S(2)}) collective-permute-start(bf16[512,768]{1,0:T(8,128)(2,1)} %get-tuple-element.86), channel_id=1, source_target_pairs={{0,8},{1,9},{2,10},{3,11},{4,12},{5,13},{6,14},{7,15}} | collective-permute-start | bytes 2359304 | tf_op jit(solution)/shard_map/ppermute | solution.py:87
  451.1 61.4 %collective-permute-start.61 = (bf16[512,768]{1,0:T(8,128)(2,1)}, bf16[512,768]{1,0:T(8,128)(2,1)}, u32[]{:S(2)}, u32[]{:S(2)}) collective-permute-start(bf16[512,768]{1,0:T(8,128)(2,1)} %get-tuple-element.87), channel_id=1, source_target_pairs={{24,16},{25,17},{26,18},{27,19},{28,20},{29,21},{30,22},{31,23}} | collective-permute-start | bytes 2359304 | tf_op jit(solution)/shard_map/ppermute | solution.py:88
  491.9 74.9 %all-to-all-start = ((bf16[8,256,256]{2,1,0:T(8,128)(2,1)}), bf16[8,256,256]{2,1,0:T(8,128)(2,1)}, u32[]{:S(2)}, u32[]{:S(2)}) async-start(bf16[8,256,256]{2,1,0:T(8,128)(2,1)} %copy-done), calls=%async_computation | async-start | bytes 2097152 | tf_op jit(solution)/shard_map/all_to_all | solution.py:367
  496.1 506.1 %all-reduce.3.cloned.1.call-start = ((), (), s32[]{:S(2)}) async-start(), calls=%async_computation.2 | async-start | bytes 197632 | tf_op jit(solution)/shard_map/psum | solution.py:424
  505.9 47.6 %collective-permute-start.100 = (bf16[512,1024]{1,0:T(8,128)(2,1)}, bf16[512,1024]{1,0:T(8,128)(2,1)S(1)}, u32[]{:S(2)}, u32[]{:S(2)}) collective-permute-start(bf16[512,1024]{1,0:T(8,128)(2,1)} %get-tuple-element.70), channel_id=1, source_target_pairs={{0,8},{1,9},{2,10},{3,11},{4,12},{5,13},{6,14},{7,15}} | collective-permute-start | bytes 3145736 | tf_op jit(solution)/shard_map/ppermute | solution.py:87
  510.4 44.8 %collective-permute-start.103 = (bf16[512,1024]{1,0:T(8,128)(2,1)}, bf16[512,1024]{1,0:T(8,128)(2,1)S(1)}, u32[]{:S(2)}, u32[]{:S(2)}) collective-permute-start(bf16[512,1024]{1,0:T(8,128)(2,1)} %get-tuple-element.71), channel_id=1, source_target_pairs={{24,16},{25,17},{26,18},{27,19},{28,20},{29,21},{30,22},{31,23}} | collective-permute-start | bytes 3145736 | tf_op jit(solution)/shard_map/ppermute | solution.py:88
  516.0 42.8 %collective-permute-start.59 = (bf16[512,768]{1,0:T(8,128)(2,1)S(1)}, bf16[512,768]{1,0:T(8,128)(2,1)}, u32[]{:S(2)}, u32[]{:S(2)}) collective-permute-start(bf16[512,768]{1,0:T(8,128)(2,1)S(1)} %get-tuple-element.84), channel_id=1, source_target_pairs={{0,8},{8,16},{1,9},{9,17},{2,10},{10,18},{3,11},{11,19},{4,12},{12... | collective-permute-start | bytes 2359304 | tf_op jit(solution)/shard_map/ppermute | solution.py:87
  518.8 45.6 %collective-permute-start.62 = (bf16[512,768]{1,0:T(8,128)(2,1)S(1)}, bf16[512,768]{1,0:T(8,128)(2,1)}, u32[]{:S(2)}, u32[]{:S(2)}) collective-permute-start(bf16[512,768]{1,0:T(8,128)(2,1)S(1)} %get-tuple-element.85), channel_id=1, source_target_pairs={{16,8},{24,16},{17,9},{25,17},{18,10},{26,18},{19,11},{27,19},{20,... | collective-permute-start | bytes 2359304 | tf_op jit(solution)/shard_map/ppermute | solution.py:88
  544.9 66.7 %collective-permute-start.87 = (bf16[512,1024]{1,0:T(8,128)(2,1)}, bf16[512,1024]{1,0:T(8,128)(2,1)S(1)}, u32[]{:S(2)}, u32[]{:S(2)}) collective-permute-start(bf16[512,1024]{1,0:T(8,128)(2,1)} %get-tuple-element.74), channel_id=1, source_target_pairs={{0,8},{8,16},{1,9},{9,17},{2,10},{10,18},{3,11},{11,19},{4,12},{12... | collective-permute-start | bytes 3145736 | tf_op jit(solution)/shard_map/ppermute | solution.py:87
  553.6 63.1 %collective-permute-start.90 = (bf16[512,1024]{1,0:T(8,128)(2,1)}, bf16[512,1024]{1,0:T(8,128)(2,1)}, u32[]{:S(2)}, u32[]{:S(2)}) collective-permute-start(bf16[512,1024]{1,0:T(8,128)(2,1)} %get-tuple-element.75), channel_id=1, source_target_pairs={{16,8},{24,16},{17,9},{25,17},{18,10},{26,18},{19,11},{27,19},{20,... | collective-permute-start | bytes 3145736 | tf_op jit(solution)/shard_map/ppermute | solution.py:88
  558.9 61.6 %collective-permute-start.101 = (bf16[512,1024]{1,0:T(8,128)(2,1)}, bf16[512,1024]{1,0:T(8,128)(2,1)}, u32[]{:S(2)}, u32[]{:S(2)}) collective-permute-start(bf16[512,1024]{1,0:T(8,128)(2,1)} %get-tuple-element.68), channel_id=1, source_target_pairs={{0,8},{8,16},{1,9},{9,17},{2,10},{10,18},{3,11},{11,19},{4,12},{12... | collective-permute-start | bytes 3145736 | tf_op jit(solution)/shard_map/ppermute | solution.py:87
  564.4 57.6 %collective-permute-start.104 = (bf16[512,1024]{1,0:T(8,128)(2,1)}, bf16[512,1024]{1,0:T(8,128)(2,1)}, u32[]{:S(2)}, u32[]{:S(2)}) collective-permute-start(bf16[512,1024]{1,0:T(8,128)(2,1)} %get-tuple-element.69), channel_id=1, source_target_pairs={{16,8},{24,16},{17,9},{25,17},{18,10},{26,18},{19,11},{27,19},{20,... | collective-permute-start | bytes 3145736 | tf_op jit(solution)/shard_map/ppermute | solution.py:88
  569.1 36.9 %collective-permute-start.74 = (bf16[512,256]{1,0:T(8,128)(2,1)S(1)}, bf16[512,256]{1,0:T(8,128)(2,1)S(1)}, u32[]{:S(2)}, u32[]{:S(2)}) collective-permute-start(bf16[512,256]{1,0:T(8,128)(2,1)S(1)} %get-tuple-element.92), channel_id=1, source_target_pairs={{0,8},{8,16},{16,24},{1,9},{9,17},{17,25},{2,10},{10,18},{18,26},{... | collective-permute-start | bytes 786440 | tf_op jit(solution)/shard_map/ppermute | solution.py:87
  605.9 37.1 %collective-permute-start.63 = (bf16[512,768]{1,0:T(8,128)(2,1)S(1)}, bf16[512,768]{1,0:T(8,128)(2,1)S(1)}, u32[]{:S(2)}, u32[]{:S(2)}) collective-permute-start(bf16[512,768]{1,0:T(8,128)(2,1)S(1)} %get-tuple-element.83), channel_id=1, source_target_pairs={{8,0},{16,8},{24,16},{9,1},{17,9},{25,17},{10,2},{18,10},{26,18},{... | collective-permute-start | bytes 2359304 | tf_op jit(solution)/shard_map/ppermute | solution.py:88
  611.6 37.3 %collective-permute-start.60 = (bf16[512,768]{1,0:T(8,128)(2,1)S(1)}, bf16[512,768]{1,0:T(8,128)(2,1)S(1)}, u32[]{:S(2)}, u32[]{:S(2)}) collective-permute-start(bf16[512,768]{1,0:T(8,128)(2,1)S(1)} %get-tuple-element.82), channel_id=1, source_target_pairs={{0,8},{8,16},{16,24},{1,9},{9,17},{17,25},{2,10},{10,18},{18,26},{... | collective-permute-start | bytes 2359304 | tf_op jit(solution)/shard_map/ppermute | solution.py:87
  640.9 40.4 %collective-permute-start.105 = (bf16[512,1024]{1,0:T(8,128)(2,1)}, bf16[512,1024]{1,0:T(8,128)(2,1)}, u32[]{:S(2)}, u32[]{:S(2)}) collective-permute-start(bf16[512,1024]{1,0:T(8,128)(2,1)} %get-tuple-element.67), channel_id=1, source_target_pairs={{8,0},{16,8},{24,16},{9,1},{17,9},{25,17},{10,2},{18,10},{26,18},{... | collective-permute-start | bytes 3145736 | tf_op jit(solution)/shard_map/ppermute | solution.py:88
  643.0 42.1 %collective-permute-start.102 = (bf16[512,1024]{1,0:T(8,128)(2,1)}, bf16[512,1024]{1,0:T(8,128)(2,1)}, u32[]{:S(2)}, u32[]{:S(2)}) collective-permute-start(bf16[512,1024]{1,0:T(8,128)(2,1)} %get-tuple-element.66), channel_id=1, source_target_pairs={{0,8},{8,16},{16,24},{1,9},{9,17},{17,25},{2,10},{10,18},{18,26},{... | collective-permute-start | bytes 3145736 | tf_op jit(solution)/shard_map/ppermute | solution.py:87
  652.1 66.0 %collective-permute-start.48 = (bf16[1024,2048]{1,0:T(8,128)(2,1)}, bf16[1024,2048]{1,0:T(8,128)(2,1)}, u32[]{:S(2)}, u32[]{:S(2)}) collective-permute-start(bf16[1024,2048]{1,0:T(8,128)(2,1)} %slice.325), channel_id=1, source_target_pairs={{0,1},{1,0},{2,3},{3,2},{4,5},{5,4},{6,7},{7,6},{8,9},{9,8},{10,11... | collective-permute-start | bytes 12582920 | tf_op jit(solution)/shard_map/ppermute | solution.py:26
  681.3 86.7 %collective-permute-start.53 = (bf16[1024,2048]{1,0:T(8,128)(2,1)}, bf16[1024,2048]{1,0:T(8,128)(2,1)}, u32[]{:S(2)}, u32[]{:S(2)}) collective-permute-start(bf16[1024,2048]{1,0:T(8,128)(2,1)} %slice.337), channel_id=1, source_target_pairs={{0,1},{1,0},{2,3},{3,2},{4,5},{5,4},{6,7},{7,6},{8,9},{9,8},{10,11... | collective-permute-start | bytes 12582920 | tf_op jit(solution)/shard_map/ppermute | solution.py:26
  711.3 39.5 %collective-permute-start.106 = (bf16[512,1024]{1,0:T(8,128)(2,1)}, bf16[512,1024]{1,0:T(8,128)(2,1)S(1)}, u32[]{:S(2)}, u32[]{:S(2)}) collective-permute-start(bf16[512,1024]{1,0:T(8,128)(2,1)} %get-tuple-element.37), channel_id=1, source_target_pairs={{0,2},{2,0},{4,6},{6,4},{1,3},{3,1},{5,7},{7,5},{8,10},{10,8},{12,... | collective-permute-start | bytes 3145736 | tf_op jit(solution)/shard_map/ppermute | solution.py:22
  718.1 33.7 %collective-permute-start.107 = (bf16[512,1024]{1,0:T(8,128)(2,1)}, bf16[512,1024]{1,0:T(8,128)(2,1)S(1)}, u32[]{:S(2)}, u32[]{:S(2)}) collective-permute-start(bf16[512,1024]{1,0:T(8,128)(2,1)} %get-tuple-element.37), channel_id=1, source_target_pairs={{0,4},{2,6},{4,0},{6,2},{1,5},{3,7},{5,1},{7,3},{8,12},{10,14},{12... | collective-permute-start | bytes 3145736 | tf_op jit(solution)/shard_map/ppermute | solution.py:22
  750.8 58.9 %collective-permute-start.96 = (bf16[512,1024]{1,0:T(8,128)(2,1)}, bf16[512,1024]{1,0:T(8,128)(2,1)}, u32[]{:S(2)}, u32[]{:S(2)}) collective-permute-start(bf16[512,1024]{1,0:T(8,128)(2,1)} %get-tuple-element.39), channel_id=1, source_target_pairs={{0,1},{1,0},{2,3},{3,2},{4,5},{5,4},{6,7},{7,6},{8,9},{9,8},{10,11... | collective-permute-start | bytes 3145736 | tf_op jit(solution)/shard_map/ppermute | solution.py:26
  751.8 61.1 %collective-permute-start.110 = (bf16[512,1024]{1,0:T(8,128)(2,1)}, bf16[512,1024]{1,0:T(8,128)(2,1)}, u32[]{:S(2)}, u32[]{:S(2)}) collective-permute-start(bf16[512,1024]{1,0:T(8,128)(2,1)} %get-tuple-element.37), channel_id=1, source_target_pairs={{0,1},{1,0},{2,3},{3,2},{4,5},{5,4},{6,7},{7,6},{8,9},{9,8},{10,11... | collective-permute-start | bytes 3145736 | tf_op jit(solution)/shard_map/ppermute | solution.py:26
  757.8 58.0 %collective-permute-start.49 = (bf16[2,256,1024]{2,1,0:T(8,128)(2,1)}, bf16[2,256,1024]{2,1,0:T(8,128)(2,1)}, u32[]{:S(2)}, u32[]{:S(2)}) collective-permute-start(bf16[2,256,1024]{2,1,0:T(8,128)(2,1)} %pad_maximum_fusion.2), channel_id=1, source_target_pairs={{0,2},{2,0},{4,6},{6,4},{1,3},{3,1},{5,7},{7,5},{8,10},{10,8},{12,... | collective-permute-start | bytes 3145736 | tf_op jit(solution)/shard_map/ppermute | solution.py:22
  (133 other events, 2787.0 us)
Sparse Core Ops, SparseCore 0:
  878.7 123.4 all-reduce.2

commit v2 on v1

v2 whole, which is shorter than its diff:
```python
import functools

import jax
import jax.numpy as jnp
from jax import lax
from jax.experimental import pallas as pl
from jax.experimental.pallas import tpu as pltpu
from jax.sharding import PartitionSpec as P

HEADS = 8
HEAD_SIZE = 256
ROT = 64
NORM_EPS = 1e-05
NEG_FILL = -1e30
ROT_BASE = 10000.0
BF = jnp.bfloat16
F32 = jnp.float32
NN = (((1,), (0,)), ((), ()))
NT = (((1,), (1,)), ((), ()))
TN = (((0,), (0,)), ((), ()))
LIGHT = pl.CostEstimate(flops=10**9, bytes_accessed=10**6, transcendentals=0)
ROOM = pltpu.CompilerParams(vmem_limit_bytes=48 * 2**20)
MORE_ROOM = pltpu.CompilerParams(vmem_limit_bytes=48 * 2**20)


def across(values, offset):
    count = lax.axis_size("head")
    return lax.ppermute(values, "head", [(i, i ^ offset) for i in range(count)])


def other_core(values):
    return lax.ppermute(values, "blk", [(0, 1), (1, 0)])


def tie(*trees):
    leaves, form = jax.tree.flatten(trees)
    return jax.tree.unflatten(form, lax.optimization_barrier(leaves))


def gather_start(own):
    return own, across(own, 1), across(own, 2)


def gather_middle(own, one, two):
    half = own.shape[0] // 2
    return own, one, two, across(one[:half], 2), across(two[half:], 1)


def gather_end(*pieces):
    near = jnp.concatenate(pieces, axis=0)
    return near, other_core(near)


def data_gather(own):
    return lax.all_gather(own, "dp", axis=0, tiled=True)


def data_scatter(partial):
    return lax.psum_scatter(partial, "dp", scatter_dimension=0, tiled=True)


def hop_up(values):
    return lax.ppermute(values, "dp", [(0, 1), (1, 2), (2, 3)])


def hop_down(values):
    return lax.ppermute(values, "dp", [(3, 2), (2, 1), (1, 0)])


def part_of(sums, index):
    rows = sums.shape[0] // 4
    return lax.dynamic_slice_in_dim(sums, index * rows, rows, 0)


def exchange_one(own, sums):
    place = lax.axis_index("dp")
    return (
        hop_up(jnp.where(place == 0, part_of(sums, 3), own)),
        hop_down(jnp.where(place == 3, part_of(sums, 0), own)),
    )


def exchange_two(own, sums, up, down):
    place = lax.axis_index("dp")
    up = jnp.where(place == 0, own, jnp.where(place == 1, plus(part_of(sums, 3), up), up))
    down = jnp.where(place == 3, own, jnp.where(place == 2, plus(part_of(sums, 0), down), down))
    return hop_up(up), hop_down(down)


def exchange_three(sums, up, down):
    place = lax.axis_index("dp")
    more_up = plus(part_of(sums, 3), up)
    more_down = plus(part_of(sums, 0), down)
    up = jnp.where(place == 0, part_of(sums, 2), jnp.where(place == 2, more_up, up))
    down = jnp.where(place == 3, part_of(sums, 1), jnp.where(place == 1, more_down, down))
    return hop_up(up), hop_down(down)


def exchange_four(sums, up, down):
    place = lax.axis_index("dp")
    more_up = plus(part_of(sums, 2), up)
    more_down = plus(part_of(sums, 1), down)
    up = jnp.where(place == 0, part_of(sums, 1), jnp.where(place == 1, more_up, up))
    down = jnp.where(place == 3, part_of(sums, 2), jnp.where(place == 2, more_down, down))
    return hop_up(up), hop_down(down)


def exchange_end(own, sums, one, two, three, four):
    place = lax.axis_index("dp")
    rows = own.shape[0]

    def choose(*values):
        out = values[-1]
        for index in range(len(values) - 2, -1, -1):
            if values[index] is not out:
                out = jnp.where(place == index, values[index], out)
        return out

    up, down = 0, 1
    whole = jnp.zeros((4 * rows,) + own.shape[1:], own.dtype)
    for step, piece in enumerate(
        (
            own,
            jnp.where(place < 2, one[down], choose(two[down], two[down], two[down], four[up])),
            choose(two[down], three[down], three[up], two[up]),
            jnp.where(place >= 2, one[up], choose(four[down], two[up], two[up], two[up])),
        )
    ):
        whole = lax.dynamic_update_slice_in_dim(whole, piece, (place + step) % 4 * rows, 0)
    first = choose(three[down], four[up], four[up], three[up]).astype(F32)
    inner = (place == 1) | (place == 2)
    second = jnp.where(inner, four[down].astype(F32), 0.0)
    total = part_of(sums, place).astype(F32) + first + second
    return whole, total.astype(BF)


def plus(one, two):
    return (one.astype(F32) + two.astype(F32)).astype(BF)


def sum_moves():
    moves = []
    for axis in ("blk", "head", "dp"):
        count = lax.axis_size(axis)
        moves += [
            (axis, [(i, i ^ 2**k) for i in range(count)]) for k in range(count.bit_length() - 1)
        ]
    return moves


def sum_move(vector, move):
    return vector + lax.ppermute(vector, *move)


def whole(array):
    return pl.BlockSpec(array.shape, lambda i: (0,) * array.ndim)


def product(one, two, dims, tile=512, kind=BF):
    def kernel(left, right, out):
        out[...] = lax.dot_general(
            left[...], right[...], dims, preferred_element_type=F32
        ).astype(out.dtype)

    if dims == TN:
        rows, left_spec = one.shape[1], pl.BlockSpec((one.shape[0], tile), lambda i: (0, i))
    else:
        rows, left_spec = one.shape[0], pl.BlockSpec((tile, one.shape[1]), lambda i: (i, 0))
    columns = two.shape[0] if dims == NT else two.shape[1]
    return pl.pallas_call(
        kernel,
        grid=(rows // tile,),
        in_specs=[left_spec, whole(two)],
        out_specs=pl.BlockSpec((tile, columns), lambda i: (i, 0)),
        out_shape=jax.ShapeDtypeStruct((rows, columns), kind),
        compiler_params=ROOM,
        cost_estimate=LIGHT,
        name="product",
    )(one, two)


def wide_product(one, two, tile=512):
    def kernel(left, right, out):
        out[...] = lax.dot_general(
            left[...], right[...], TN, preferred_element_type=F32
        ).astype(BF)

    return pl.pallas_call(
        kernel,
        grid=(two.shape[1] // tile,),
        in_specs=[whole(one), pl.BlockSpec((two.shape[0], tile), lambda i: (0, i))],
        out_specs=pl.BlockSpec((one.shape[1], tile), lambda i: (0, i)),
        out_shape=jax.ShapeDtypeStruct((one.shape[1], two.shape[1]), BF),
        compiler_params=ROOM,
        cost_estimate=LIGHT,
        name="wide",
    )(one, two)


def hidden_kernel(tokens, weight, bias, active, slope):
    hidden = jnp.dot(tokens[...], weight[...], preferred_element_type=F32) + bias[...]
    phi = 0.5 * (1.0 + lax.erf(hidden * (0.5**0.5)))
    active[...] = (hidden * phi).astype(BF)
    density = jnp.exp(-0.5 * hidden * hidden) * ((2.0 * jnp.pi) ** -0.5)
    slope[...] = (phi + hidden * density).astype(BF)


def hidden_units_of(tokens, weight, bias, tile=512):
    rows, width = tokens.shape
    wide = weight.shape[1]
    out = pl.BlockSpec((tile, wide), lambda i: (i, 0))
    return pl.pallas_call(
        hidden_kernel,
        grid=(rows // tile,),
        in_specs=[pl.BlockSpec((tile, width), lambda i: (i, 0)), whole(weight), whole(bias)],
        out_specs=[out, out],
        out_shape=[jax.ShapeDtypeStruct((rows, wide), BF)] * 2,
        compiler_params=MORE_ROOM,
        cost_estimate=LIGHT,
        name="hidden",
    )(tokens, weight, bias)


def hidden_grad_kernel(upstream, weight, slope, grad, total):
    values = jnp.dot(upstream[...], weight[...], preferred_element_type=F32)
    low = (values * slope[...].astype(F32)).astype(BF)
    grad[...] = low

    @pl.when(pl.program_id(0) == 0)
    def clear():
        total[...] = jnp.zeros_like(total)

    total[...] += jnp.sum(low.astype(F32), axis=0, keepdims=True)


def hidden_grad_of(upstream, weight, slope, tile=512):
    rows, width = upstream.shape
    wide = weight.shape[1]
    out = pl.BlockSpec((tile, wide), lambda i: (i, 0))
    return pl.pallas_call(
        hidden_grad_kernel,
        grid=(rows // tile,),
        in_specs=[pl.BlockSpec((tile, width), lambda i: (i, 0)), whole(weight), out],
        out_specs=[out, pl.BlockSpec((1, wide), lambda i: (0, 0))],
        out_shape=[
            jax.ShapeDtypeStruct((rows, wide), BF),
            jax.ShapeDtypeStruct((1, wide), F32),
        ],
        compiler_params=MORE_ROOM,
        cost_estimate=LIGHT,
        name="hidden_grad",
    )(upstream, weight, slope)


def halves_product(one, two, tile=512):
    half = two.shape[1] // 2

    def kernel(left, right, low, high):
        values = lax.dot_general(left[...], right[...], TN, preferred_element_type=F32).astype(BF)
        low[...] = values[:, :half]
        high[...] = values[:, half:]

    rows = one.shape[1]
    out = pl.BlockSpec((tile, half), lambda i: (i, 0))
    return pl.pallas_call(
        kernel,
        grid=(rows // tile,),
        in_specs=[pl.BlockSpec((one.shape[0], tile), lambda i: (0, i)), whole(two)],
        out_specs=[out, out],
        out_shape=[jax.ShapeDtypeStruct((rows, half), BF)] * 2,
        compiler_params=ROOM,
        cost_estimate=LIGHT,
        name="halves_product",
    )(one, two)


def put_split(step, side, block, left_keep, left_send, right_keep, right_send):
    left, right = block[:, :side], block[:, side:]
    for index, out, at in ((0, left_keep, 0), (1, left_send, 0), (2, left_keep, 1), (3, left_send, 1)):

        @pl.when(step == index)
        def write_left(out=out, at=at):
            out[at] = left

    for index, out, at in ((0, right_keep, 0), (1, right_keep, 1), (2, right_send, 0), (3, right_send, 1)):

        @pl.when(step == index)
        def write_right(out=out, at=at):
            out[at] = right


def split_shapes(span, width):
    return [jax.ShapeDtypeStruct((2, span, width // 2), BF)] * 4


def split_specs(span, width):
    return [pl.BlockSpec((2, span, width // 2), lambda i: (0, 0, 0))] * 4


def collect_start(left_keep, left_send, right_keep, right_send):
    return across(left_send, 1), across(right_send, 2)


def collect_middle(parts, got):
    (left_keep, _, right_keep, _), (left, right) = parts, got
    left_last = across(plus(left_keep[1], left[1]), 2)
    right_last = across(plus(right_keep[1], right[1]), 1)
    return (left_keep[0], left[0], left_last), (right_keep[0], right[0], right_last)


def collect_end(*sides):
    return jnp.concatenate(
        [sum(term.astype(F32) for term in terms[1:]) + terms[0].astype(F32) for terms in sides],
        axis=1,
    )


def product_far(one, two, tile=512):
    rows = one.shape[0] // 2

    def kernel(left, right, out):
        out[...] = lax.dot_general(
            left[...], right[...], NT, preferred_element_type=F32
        ).astype(BF)

    return pl.pallas_call(
        kernel,
        grid=(rows // tile,),
        in_specs=[
            pl.BlockSpec((tile, one.shape[1]), lambda i: (i + rows // tile, 0)),
            whole(two),
        ],
        out_specs=pl.BlockSpec((tile, two.shape[0]), lambda i: (i, 0)),
        out_shape=jax.ShapeDtypeStruct((rows, two.shape[0]), BF),
        compiler_params=ROOM,
        cost_estimate=LIGHT,
        name="far",
    )(one, two)


def product_near(one, two, got, span):
    width = two.shape[0]

    def kernel(left, right, more, *outs):
        values = lax.dot_general(left[...], right[...], NT, preferred_element_type=F32)
        block = (values + more[...].astype(F32)).astype(BF)
        put_split(pl.program_id(0), width // 2, block, *outs)

    return pl.pallas_call(
        kernel,
        grid=(one.shape[0] // 2 // span,),
        in_specs=[
            pl.BlockSpec((span, one.shape[1]), lambda i: (i, 0)),
            whole(two),
            pl.BlockSpec((span, width), lambda i: (i, 0)),
        ],
        out_specs=split_specs(span, width),
        out_shape=split_shapes(span, width),
        compiler_params=MORE_ROOM,
        cost_estimate=LIGHT,
        name="near",
    )(one, two, got)


def share_kernel(near, qkv, qkv_weight, hidden, weight, gain_one, gain_two, normed, *rest):
    outs, sums = rest[-5:-1] if near else rest[:1], rest[-1]
    one = lax.dot_general(qkv[...], qkv_weight[...], NT, preferred_element_type=F32)
    two = lax.dot_general(hidden[...], weight[...], NT, preferred_element_type=F32)
    scaled = normed[...].astype(F32)

    @pl.when(pl.program_id(0) == 0)
    def clear():
        sums[...] = jnp.zeros_like(sums)

    for row, values in enumerate((one * scaled, one, two * scaled, two)):
        sums[row : row + 1, :] += jnp.sum(values, axis=0, keepdims=True)
    share = one * gain_one[...] + two * gain_two[...]
    if near:
        block = (share + rest[0][...].astype(F32)).astype(BF)
        put_split(pl.program_id(0), share.shape[1] // 2, block, *outs)
    else:
        outs[0][...] = share.astype(BF)


def shares(near, qkv, qkv_weight, hidden, weight, gains, normed, span, got=None):
    rows, width = normed.shape
    steps = rows // 2 // span
    offset = 0 if near else steps

    def rows_of(array):
        return pl.BlockSpec((span, array.shape[1]), lambda i: (i + offset, 0))

    extra = [got] if near else []
    block = pl.BlockSpec((span, width), lambda i: (i, 0))
    return pl.pallas_call(
        functools.partial(share_kernel, near),
        grid=(steps,),
        in_specs=[
            rows_of(qkv),
            whole(qkv_weight),
            rows_of(hidden),
            whole(weight),
            whole(gains[0]),
            whole(gains[1]),
            rows_of(normed),
        ]
        + [block] * len(extra),
        out_specs=(split_specs(span, width) if near else [block])
        + [pl.BlockSpec((8, width), lambda i: (0, 0))],
        out_shape=(
            split_shapes(span, width) if near else [jax.ShapeDtypeStruct((rows // 2, width), BF)]
        )
        + [jax.ShapeDtypeStruct((8, width), F32)],
        compiler_params=MORE_ROOM,
        cost_estimate=LIGHT,
        name="share_near" if near else "share_far",
    )(qkv, qkv_weight, hidden, weight, *gains, normed, *extra)


def norm_kernel(near, far, gain_one, bias_one, gain_two, bias_two, normed, attn_in, mlp_in):
    half = pl.num_programs(0) // 2

    def write(block):
        values = block[...].astype(F32)
        centred = values - jnp.mean(values, axis=1, keepdims=True)
        spread = jnp.mean(centred * centred, axis=1, keepdims=True)
        scaled = centred * lax.rsqrt(spread + NORM_EPS)
        normed[...] = scaled.astype(BF)
        attn_in[...] = (scaled * gain_one[...] + bias_one[...]).astype(BF)
        mlp_in[...] = (scaled * gain_two[...] + bias_two[...]).astype(BF)

    pl.when(pl.program_id(0) < half)(lambda: write(near))
    pl.when(pl.program_id(0) >= half)(lambda: write(far))


def norms(near, far, span, *vectors):
    rows, width = near.shape
    half = rows // span
    vector = pl.BlockSpec((1, width), lambda i: (0, 0))
    block = pl.BlockSpec((span, width), lambda i: (i, 0))
    return pl.pallas_call(
        norm_kernel,
        grid=(2 * half,),
        in_specs=[
            pl.BlockSpec((span, width), lambda i: (jnp.minimum(i, half - 1), 0)),
            pl.BlockSpec((span, width), lambda i: (jnp.maximum(i - half, 0), 0)),
        ]
        + [vector] * 4,
        out_specs=[block] * 3,
        out_shape=[jax.ShapeDtypeStruct((2 * rows, width), BF)] * 3,
        compiler_params=ROOM,
        cost_estimate=LIGHT,
        name="norms",
    )(near, far, *[v.astype(F32)[None, :] for v in vectors])


def spread_kernel(parts, places, near, far, *outs):
    count = near.shape[0]
    each = near.shape[2] // sum(parts)
    for relative in range(2 * count):
        source = near if relative < count else far
        at = 0
        for out, part in zip(outs, parts):
            for index in range(part):
                where = (index * 2 * count + places[relative]) * each
                out[:, pl.ds(pl.multiple_of(where, each), each)] = source[
                    relative % count, :, at * each : (at + 1) * each
                ].astype(F32)
                at += 1


def spread_columns(near, far, places, parts):
    count = lax.axis_size("head")
    rows = near.shape[0] // count
    width = near.shape[1]
    step = min(rows, 64)
    each = width // sum(parts)
    taken = pl.BlockSpec((count, step, width), lambda i, p: (0, i, 0))
    wide = [2 * count * each * part for part in parts]
    return pl.pallas_call(
        functools.partial(spread_kernel, parts),
        grid_spec=pltpu.PrefetchScalarGridSpec(
            num_scalar_prefetch=1,
            grid=(rows // step,),
            in_specs=[taken, taken],
            out_specs=[pl.BlockSpec((step, w), lambda i, p: (i, 0)) for w in wide],
        ),
        out_shape=[jax.ShapeDtypeStruct((rows, w), F32) for w in wide],
        compiler_params=ROOM,
        cost_estimate=LIGHT,
        name="spread",
    )(places, near.reshape(count, rows, width), far.reshape(count, rows, width))


def halves_kernel(places, near, far, *rest):
    count = pl.num_programs(0) // 2
    out = rest[-1]

    def write(source):
        out[...] = source[...].astype(F32)

    pl.when(pl.program_id(0) < count)(lambda: write(near))
    pl.when(pl.program_id(0) >= count)(lambda: write(far))


def spread_half(near, far, places, side, first_column, begun=None):
    count = lax.axis_size("head")
    rows = near.shape[0] // count
    width = near.shape[1] - first_column
    column = first_column // width
    specs = [
        pl.BlockSpec((rows, width), lambda r, p: (jnp.minimum(r, count - 1), column)),
        pl.BlockSpec((rows, width), lambda r, p: (jnp.maximum(r - count, 0), column)),
    ]
    extra = () if begun is None else (begun,)
    return pl.pallas_call(
        halves_kernel,
        grid_spec=pltpu.PrefetchScalarGridSpec(
            num_scalar_prefetch=1,
            grid=(2 * count,),
            in_specs=specs + [pl.BlockSpec(memory_space=pl.ANY) for _ in extra],
            out_specs=pl.BlockSpec((rows, width), lambda r, p: (0, 2 * p[r] + side)),
        ),
        out_shape=jax.ShapeDtypeStruct((rows, 4 * count * width), F32),
        input_output_aliases={3: 0} if extra else {},
        compiler_params=ROOM,
        cost_estimate=LIGHT,
        name="halves",
    )(places, near, far, *extra)


def turn(values, cosine, sine):
    low = values[:, : cosine.shape[1]]
    lane = lax.broadcasted_iota(jnp.int32, low.shape, 1)
    half = ROT // 2
    partner = jnp.where(
        lane < half, pltpu.roll(low, low.shape[1] - half, 1), pltpu.roll(low, half, 1)
    )
    return jnp.concatenate([low * cosine + partner * sine, values[:, cosine.shape[1] :]], axis=1)


def attention_kernel(
    order, first, qkv, bias, upstream, cosine, sine, context, context_rel, grads, keys, values,
    score, prob_grad, key_sum, value_sum,
):
    step = pl.program_id(0)
    total = pl.num_programs(0)
    size = HEAD_SIZE
    span = qkv.shape[1]
    last = (((1,), (1,)), ((), ()))
    rows = (((0,), (0,)), ((), ()))
    mine = order[step]
    start = first[step]
    cos_here, sin_here = cosine[mine], sine[mine]
    joined = qkv[0].astype(F32) + bias[...]
    query = (turn(joined[:, :size], cos_here, sin_here) * (size**-0.5)).astype(BF)
    at = pl.ds(pl.multiple_of(step * span, span), span)
    keys[at, :] = turn(joined[:, size : 2 * size], cos_here, sin_here).astype(BF)
    values[at, :] = joined[:, 2 * size :].astype(BF)
    key_sum[at, :] = jnp.zeros((span, size), F32)
    value_sum[at, :] = jnp.zeros((span, size), F32)
    up = upstream[0]

    def one(count):
        blocks = [slice(i * span, (i + 1) * span) for i in range(count)]
        top = jnp.full((span, 1), NEG_FILL, F32)
        for i, block in enumerate(blocks):
            part = lax.dot_general(query, keys[block, :], last, preferred_element_type=F32)
            if i == count - 1:
                row = lax.broadcasted_iota(jnp.int32, part.shape, 0)
                column = lax.broadcasted_iota(jnp.int32, part.shape, 1)
                part = jnp.where(column <= row, part, NEG_FILL)
            else:
                part = part + jnp.where(i >= start, 0.0, NEG_FILL)
            score[:, block] = part
            top = jnp.maximum(top, jnp.max(part, axis=1, keepdims=True))
        norm = jnp.zeros((span, 1), F32)
        for block in blocks:
            part = jnp.exp(score[:, block] - top)
            score[:, block] = part
            norm = norm + jnp.sum(part, axis=1, keepdims=True)
        inverse = 1.0 / norm
        out = jnp.zeros((span, size), F32)
        inner = jnp.zeros((span, 1), F32)
        for block in blocks:
            probs = score[:, block] * inverse
            score[:, block] = probs
            grad = lax.dot_general(up, values[block, :], last, preferred_element_type=F32)
            prob_grad[:, block] = grad
            inner = inner + jnp.sum(probs * grad, axis=1, keepdims=True)
            low = probs.astype(BF)
            out = out + jnp.dot(low, values[block, :], preferred_element_type=F32)
            value_sum[block, :] += lax.dot_general(low, up, rows, preferred_element_type=F32)
        context[0] = out.astype(BF)
        context_rel[0] = out.astype(BF)
        query_grad = jnp.zeros((span, size), F32)
        for block in blocks:
            low = (score[:, block] * (prob_grad[:, block] - inner)).astype(BF)
            query_grad = query_grad + jnp.dot(low, keys[block, :], preferred_element_type=F32)
            key_sum[block, :] += lax.dot_general(low, query, rows, preferred_element_type=F32)
        query_grad = (query_grad * (size**-0.5)).astype(BF).astype(F32)
        grads[mine, :, :size] = turn(query_grad, cos_here, -sin_here).astype(BF)

    steps = keys.shape[0] // span
    for index in range(steps):
        pl.when(step == index)(functools.partial(one, index + 1))

    @pl.when(step == total - 1)
    def finish():
        def each(index, carry):
            place = order[index]
            block = pl.ds(pl.multiple_of(index * span, span), span)
            key_grad = key_sum[block, :].astype(BF).astype(F32)
            grads[place, :, size : 2 * size] = turn(key_grad, cosine[place], -sine[place]).astype(
                BF
            )
            grads[place, :, 2 * size :] = value_sum[block, :].astype(BF)
            return carry

        lax.fori_loop(0, total, each, 0)


def attention(order, first, qkv, bias, upstream, cosine, sine):
    count, span, width = qkv.shape
    size = HEAD_SIZE
    length = count * span
    whole = lambda *shape: pl.BlockSpec(shape, lambda i, o, f: (0,) * len(shape))
    taken = lambda *shape: pl.BlockSpec(
        (1,) + shape, lambda i, o, f: (o[i],) + (0,) * len(shape)
    )
    pairs = count * (count + 1) // 2
    return pl.pallas_call(
        attention_kernel,
        grid_spec=pltpu.PrefetchScalarGridSpec(
            num_scalar_prefetch=2,
            grid=(count,),
            in_specs=[
                taken(span, width),
                whole(1, width),
                taken(span, size),
                whole(count, span, cosine.shape[-1]),
                whole(count, span, cosine.shape[-1]),
            ],
            out_specs=[
                pl.BlockSpec((1, span, size), lambda i, o, f: (i, 0, 0)),
                taken(span, size),
                whole(count, span, width),
            ],
            scratch_shapes=[
                pltpu.VMEM((length, size), BF),
                pltpu.VMEM((length, size), BF),
                pltpu.VMEM((span, length), F32),
                pltpu.VMEM((span, length), F32),
                pltpu.VMEM((length, size), F32),
                pltpu.VMEM((length, size), F32),
            ],
        ),
        out_shape=[
            jax.ShapeDtypeStruct((count, span, size), BF),
            jax.ShapeDtypeStruct((count, span, size), BF),
            jax.ShapeDtypeStruct((count, span, width), BF),
        ],
        compiler_params=ROOM,
        cost_estimate=LIGHT,
        name="attention",
    )(order, first, qkv, bias, upstream, cosine, sine)


def segment_start(lengths, at):
    lengths = lengths.reshape(-1)
    starts = jnp.stack([jnp.sum(lengths[:i]) for i in range(lengths.shape[0])])
    return jnp.max(jnp.where(starts[None, :] <= at[:, None], starts[None, :], 0), axis=1).astype(
        jnp.int32
    )


def rotary_tables(lengths, places, span):
    at = places * span
    offset = (at - segment_start(lengths, at))[:, None] + jnp.arange(span, dtype=jnp.int32)[None, :]
    half = ROT // 2
    frequency = ROT_BASE ** (-(2.0 * jnp.arange(half, dtype=F32)) / ROT)
    angles = offset.astype(F32)[..., None] * frequency
    cosine, sine = jnp.cos(angles), jnp.sin(angles)
    rest = jnp.zeros(offset.shape + (128 - ROT,), F32)
    return (
        jnp.concatenate([cosine, cosine, rest + 1.0], axis=-1),
        jnp.concatenate([-sine, sine, rest], axis=-1),
    )


def body(
    block_in,
    cotangent,
    seg_lengths,
    ln1_gain,
    ln1_bias,
    qkv_weight,
    qkv_bias,
    out_weight,
    out_bias,
    ln2_gain,
    ln2_bias,
    fc1_weight,
    fc1_bias,
    fc2_weight,
    fc2_bias,
):
    rows_here, span, width = block_in.shape
    shard, hidden_units = fc1_weight.shape
    data_count = lax.axis_size("dp")
    head_count = lax.axis_size("head")
    blk_count = lax.axis_size("blk")
    plane = head_count * blk_count
    head_place = lax.axis_index("head")
    blk_place = lax.axis_index("blk")
    place = head_place * blk_count + blk_place
    each = hidden_units // plane
    length = plane * span

    places = [
        (head_place ^ (r % head_count)) * blk_count + (blk_place ^ (r // head_count))
        for r in range(plane)
    ]
    absolute = jnp.arange(plane, dtype=jnp.int32)
    order = (absolute % blk_count ^ blk_place) * head_count + (absolute // blk_count ^ head_place)

    def columns(values, wide):
        return lax.dynamic_slice_in_dim(values, place * wide, wide, 1)

    own_in = block_in.reshape(span, width)
    own_up = cotangent.reshape(span, width)
    att_shard = jnp.concatenate(
        [
            columns(qkv_weight[:, part * width : (part + 1) * width], HEAD_SIZE)
            for part in range(3)
        ]
        + [columns(out_weight, HEAD_SIZE)],
        axis=1,
    )
    att_shard, own_in = tie(att_shard, own_in)
    att_mine = data_gather(att_shard)
    tokens_begun = gather_start(own_in)
    tokens_begun, own_up = tie(tokens_begun, own_up)
    upstream_begun = gather_start(own_up)
    tokens_near, tokens_far = gather_end(*gather_middle(*tokens_begun))
    fc1_shard, tokens_near = tie(columns(fc1_weight, each), tokens_near)
    fc1_mine = data_gather(fc1_shard)
    upstream_begun, tokens_near, tokens_far = tie(upstream_begun, tokens_near, tokens_far)
    upstream_begun = gather_middle(*upstream_begun)
    cosine, sine = rotary_tables(seg_lengths, jnp.stack(places), span)
    normed, attn_in, mlp_in = norms(
        tokens_near, tokens_far, span, ln1_gain, ln1_bias, ln2_gain, ln2_bias
    )
    upstream_begun, attn_in, cosine, sine = tie(upstream_begun, attn_in, cosine, sine)
    upstream_near, upstream_far = gather_end(*upstream_begun)
    upstream_near, att_mine, attn_in = tie(upstream_near, att_mine, attn_in)

    first = segment_start(seg_lengths, absolute * span) // span

    qkv_mine, out_mine = att_mine[:, : 3 * HEAD_SIZE], att_mine[:, 3 * HEAD_SIZE :]
    out_rows = lax.all_to_all(out_mine, ("head", "blk"), split_axis=0, concat_axis=1, tiled=True)
    joined = product(attn_in, qkv_mine, NN, kind=F32)
    upstream_near, upstream_far, joined = tie(upstream_near, upstream_far, joined)
    upstream = jnp.concatenate([upstream_near, upstream_far], axis=0)
    context_grad = product(upstream, out_rows, NT)
    bias_mine = jnp.concatenate(
        [
            lax.dynamic_slice_in_dim(qkv_bias, part * width + place * HEAD_SIZE, HEAD_SIZE, 0)
            for part in range(3)
        ]
    ).astype(F32)
    context_abs, context, qkv_grad = attention(
        order.astype(jnp.int32),
        first,
        joined.reshape(plane, span, 3 * HEAD_SIZE),
        bias_mine[None, :],
        context_grad.reshape(plane, span, HEAD_SIZE),
        cosine,
        sine,
    )
    context = context.reshape(length, HEAD_SIZE)
    qkv_grad = qkv_grad.reshape(length, 3 * HEAD_SIZE)
    out_grad = wide_product(context, upstream)
    out_grad = lax.all_to_all(out_grad, ("head", "blk"), split_axis=1, concat_axis=0, tiled=True)
    qkv_w_grad = product(attn_in, qkv_grad, TN)
    att_grad = jnp.concatenate([qkv_w_grad, out_grad], axis=1)

    fc1_mine, att_grad, context_abs, out_mine, fc2_shard = tie(
        fc1_mine, att_grad, context_abs, out_mine, columns(fc2_weight, each)
    )
    chain = data_count == 4
    if chain:
        move_one = exchange_one(fc2_shard, att_grad)
    else:
        fc2_mine, att_sum = data_gather(fc2_shard), data_scatter(att_grad)
    out_moved = gather_start(out_mine)
    fc1_bias_mine = lax.dynamic_slice_in_dim(fc1_bias, place * each, each, 0).astype(F32)
    active, slope = hidden_units_of(mlp_in, fc1_mine, fc1_bias_mine[None, :])
    if chain:
        move_one, out_moved, fc2_shard, att_grad, active = tie(
            move_one, out_moved, fc2_shard, att_grad, active
        )
        move_two = exchange_two(fc2_shard, att_grad, *move_one)
    out_moved = gather_middle(*out_moved)
    fc2_grad = product(upstream, active, TN)
    if chain:
        move_two, out_moved, att_grad, fc2_grad, context_abs = tie(
            move_two, out_moved, att_grad, fc2_grad, context_abs
        )
        move_three = exchange_three(att_grad, *move_two)
    own_context = lax.all_to_all(
        context_abs.reshape(length, HEAD_SIZE),
        ("head", "blk"),
        split_axis=0,
        concat_axis=1,
        tiled=True,
    )
    if chain:
        move_three, att_grad, own_context, out_moved = tie(
            move_three, att_grad, own_context, out_moved
        )
        move_four = exchange_four(att_grad, *move_three)
    out_pieces = gather_end(*out_moved)
    attn_out = jnp.zeros((span, width), F32)
    for half, pieces in enumerate(out_pieces):
        for index in range(head_count):
            attn_out = lax.dynamic_update_slice(
                attn_out,
                jnp.dot(
                    own_context,
                    pieces[index * width : (index + 1) * width],
                    preferred_element_type=F32,
                ),
                (0, places[half * head_count + index] * HEAD_SIZE),
            )
    attn_out = attn_out + out_bias
    if chain:
        move_four, fc2_grad, attn_out = tie(move_four, fc2_grad, attn_out)
        fc2_mine, att_sum = exchange_end(
            fc2_shard, att_grad, move_one, move_two, move_three, move_four
        )
    fc2_sum = data_scatter(fc2_grad)

    att_moved = gather_start(att_sum)
    mlp_far = product_far(active, fc2_mine)
    mlp_got = other_core(mlp_far)
    hidden_grad, fc1_bias_part = hidden_grad_of(upstream, fc2_mine, slope)
    att_moved, mlp_got, hidden_grad, active = tie(att_moved, mlp_got, hidden_grad, active)
    att_moved = gather_middle(*att_moved)
    mlp_parts = product_near(active, fc2_mine, mlp_got, span)
    att_moved, mlp_parts, hidden_grad = tie(att_moved, mlp_parts, hidden_grad)
    mlp_got = collect_start(*mlp_parts)
    gains = (ln1_gain.astype(F32)[None, :], ln2_gain.astype(F32)[None, :])
    share_far, sums_far = shares(
        False, qkv_grad, qkv_mine, hidden_grad, fc1_mine, gains, normed, span
    )
    mlp_got, share_far, hidden_grad = tie(mlp_got, share_far, hidden_grad)
    mlp_done = collect_middle(mlp_parts, mlp_got)
    share_got = other_core(share_far)
    fc1_low, fc1_high = halves_product(mlp_in, hidden_grad)
    mlp_done, share_got, fc1_low, fc1_high, hidden_grad, fc2_sum = tie(
        mlp_done, share_got, fc1_low, fc1_high, hidden_grad, fc2_sum
    )
    low_sum = data_scatter(fc1_low)
    high_sum = data_scatter(fc1_high)
    fc2_moved = gather_start(fc2_sum)
    *share_parts, sums_near = shares(
        True, qkv_grad, qkv_mine, hidden_grad, fc1_mine, gains, normed, span, share_got
    )
    fc2_moved, share_parts, att_moved = tie(fc2_moved, share_parts, att_moved)
    share_got = collect_start(*share_parts)
    fc2_moved = gather_middle(*fc2_moved)
    place_list = jnp.stack(places).astype(jnp.int32)
    qkv_out, out_out = spread_columns(*gather_end(*att_moved), place_list, (3, 1))
    mlp_out = collect_end(*mlp_done) + fc2_bias
    own_float = own_in.astype(F32)
    block_out = (own_float + attn_out + mlp_out).astype(BF).reshape(block_in.shape)

    moves = sum_moves()
    qkv_bias_part = jnp.sum(qkv_grad.astype(F32), axis=0).reshape(3, 1, HEAD_SIZE)
    here = (jnp.arange(plane) == place).astype(F32)
    norm_sums = sums_far + sums_near
    terms = (
        norm_sums[0],
        norm_sums[1],
        (qkv_bias_part * here[None, :, None]).reshape(-1),
        jnp.sum(own_up.astype(F32), axis=0),
        norm_sums[2],
        norm_sums[3],
        (here[:, None] * fc1_bias_part).reshape(-1),
        jnp.stack([jnp.sum(attn_out * attn_out), jnp.sum(mlp_out * mlp_out)]),
    )
    sizes = [term.shape[0] for term in terms]
    vector = jnp.concatenate(terms + (jnp.zeros((-sum(sizes) % 1024,), F32),)).reshape(-1, 128)
    vector = sum_move(vector, moves[0])

    share_got, fc2_moved, vector, low_sum, qkv_out, out_out = tie(
        share_got, fc2_moved, vector, low_sum, qkv_out, out_out
    )
    share_done = collect_middle(share_parts, share_got)
    low_moved = gather_start(low_sum)
    fc2_moved = gather_end(*fc2_moved)
    vector = sum_move(vector, moves[1])
    share_done, fc2_moved, vector, low_moved, high_sum = tie(
        share_done, fc2_moved, vector, low_moved, high_sum
    )

    share = collect_end(*share_done)
    own_centred = own_float - jnp.mean(own_float, axis=-1, keepdims=True)
    own_scaled = lax.rsqrt(jnp.mean(own_centred * own_centred, axis=-1, keepdims=True) + NORM_EPS)
    own_normed = own_centred * own_scaled
    share = own_scaled * (
        share
        - jnp.mean(share, axis=-1, keepdims=True)
        - own_normed * jnp.mean(share * own_normed, axis=-1, keepdims=True)
    )
    input_grad = (own_up.astype(F32) + share).astype(BF).reshape(block_in.shape)

    low_moved = gather_middle(*low_moved)
    high_moved = gather_start(high_sum)
    vector = sum_move(vector, moves[2])
    [fc2_out] = spread_columns(*fc2_moved, place_list, (1,))
    low_moved, high_moved, vector, fc2_out, input_grad = tie(
        low_moved, high_moved, vector, fc2_out, input_grad
    )
    low_moved = gather_end(*low_moved)
    high_moved = gather_middle(*high_moved)
    vector = sum_move(vector, moves[3])
    low_moved, high_moved, vector = tie(low_moved, high_moved, vector)
    high_moved = gather_end(*high_moved)
    for move in moves[4:]:
        vector = sum_move(vector, move)
    fc1_begun = spread_half(*low_moved, place_list, 0, 0)
    fc1_out = spread_half(*high_moved, place_list, 1, 0, fc1_begun)
    reduced = [
        vector.reshape(-1)[sum(sizes[:i]) : sum(sizes[: i + 1])] for i in range(len(sizes))
    ]
    entries = rows_here * length * data_count * width
    branch_rms = jnp.sqrt(reduced[7] / entries)
    return (
        block_out,
        input_grad,
        reduced[0],
        reduced[1],
        qkv_out,
        reduced[2],
        out_out,
        reduced[3],
        reduced[4],
        reduced[5],
        fc1_out,
        reduced[6],
        fc2_out,
        reduced[3],
        branch_rms[0],
        branch_rms[1],
    )


def solution(mesh):
    rows, tokens, whole = P("dp", None), P("dp", ("head", "blk"), None), P()
    return jax.shard_map(
        body,
        mesh=mesh,
        in_specs=(
            tokens,
            tokens,
            rows,
            whole,
            whole,
            rows,
            whole,
            rows,
            whole,
            whole,
            whole,
            rows,
            whole,
            rows,
            whole,
        ),
        out_specs=(
            tokens,
            tokens,
            whole,
            whole,
            rows,
            whole,
            rows,
            whole,
            whole,
            whole,
            rows,
            whole,
            rows,
            whole,
            whole,
            whole,
        ),
        check_vma=False,
    )
```

time: 1030 us -> 646 us (0.63)
  waiting for transfers between devices: 422 us -> 148 us
  Pallas kernels: 20.2 us -> 218 us
  matrix products: 134 us -> 10.2 us
  starting transfers between devices: 173 us -> 69.2 us
  other arithmetic: 156 us -> 55.7 us
  blocking collectives: 0 us -> 18.7 us
    pallas_call x0 -> x17, Pallas kernels: none -> 190 us  [the longest x4 38.6 us: product(): pl.pallas_call(kernel, grid=(rows // tile,), in_specs=[left_spec, whole(t...]
    dot_general x12 -> x8, matrix products: 134 us -> 10.2 us  [body(): jnp.dot(own_context, pieces[index * width:(index + 1) * width], preferred...]
    psum x1 -> x0, waiting for transfers between devices: 121 us -> none  [body(): lax.psum((jnp.sum(attn_in_grad * normed, axis=0), jnp.sum(attn_in_grad, a...]
    ppermute x48 -> x13, waiting for transfers between devices: 157 us -> 42.9 us  [the longest x4 15.4 us: hop_down(): return lax.ppermute(values, 'dp', [(3, 2), (2, 1), (1, 0)])]
    ppermute x48 -> x13, starting transfers between devices: 124 us -> 23.7 us  [the longest x4 15.5 us: hop_up(): return lax.ppermute(values, 'dp', [(0, 1), (1, 2), (2, 3)])]
    dynamic_update_slice x60 -> x3, other arithmetic: 81.3 us -> 4.52 us  [exchange_end(): lax.dynamic_update_slice_in_dim(whole, piece, (place + step) % 4 * rows, 0)]
    ppermute x36, waiting for transfers between devices: 144 us -> 102 us  [across(): return lax.ppermute(values, 'head', [(i, i ^ offset) for i in range(count)])]
    convert_element_type x25 -> x8, other arithmetic: 33.8 us -> 7.6 us  [the longest x4 4.44 us: plus(): return (one.astype(F32) + two.astype(F32)).astype(BF)]
  transfers between devices with their start and end apart: 117 -> 65, of which waited for: 40 -> 32; matrix products, arithmetic and copies ran while one was open for 36% -> 17% of each run, Pallas kernels for 2% -> 32%
where the time goes in v2:
time: 646 us; the launch traced here: 634 us
  Pallas kernels  218 us (34%)
  waiting for transfers between devices  148 us (23%)
  local copies, waits for them, and re-layouts  98.3 us (15%)
  starting transfers between devices  69.2 us (11%)
  other arithmetic  55.7 us (9%)
  blocking collectives  18.7 us (3%)
  between operations  15.3 us (2%)
  matrix products  10.2 us (2%)
    ppermute x36, waiting for transfers between devices, across(): return lax.ppermute(values, 'head', [(i, i ^ offset) for i in range(count)])  102 us
    unnamed x160, local copies, waits for them, and re-layouts  49.2 us
    pallas_call x4, Pallas kernels, product(): pl.pallas_call(kernel, grid=(rows // tile,), in_specs=[left_spec, whole(t...  38.6 us
    pallas_call x2, Pallas kernels, shares(): pl.pallas_call(functools.partial(share_kernel, near), grid=(steps,), in_s...  38.1 us
    ppermute x36, starting transfers between devices, across(): return lax.ppermute(values, 'head', [(i, i ^ offset) for i in range(count)])  36.4 us
    pallas_call x1, Pallas kernels, attention(): pl.pallas_call(attention_kernel, grid_spec=pltpu.PrefetchScalarGridSpec(n...  28.7 us
    pallas_call x2, Pallas kernels, spread_columns(): pl.pallas_call(functools.partial(spread_kernel, parts), grid_spec=pltpu.P...  21.8 us
    all_to_all x1, blocking collectives, body(): lax.all_to_all(context_abs.reshape(length, HEAD_SIZE), ('head', 'blk'), s...  18.7 us
  transfers between devices with their start and end apart: 65, of which 32 were waited for; matrix products, arithmetic and copies ran while one was open for 17% of the time, Pallas kernels for 32%

profile of v2, /device:TPU:0, one launch (start us, length us, event | category | flops | bytes accessed | tf_op | source)
XLA Modules:
  0.0 634.0 jit_solution(2467970854637893000)
XLA Ops:
  7.2 5.8 fusion.49
  20.9 21.6 %collective-permute-done = bf16[256,2048]{1,0:T(8,128)(2,1)S(1)} collective-permute-done((bf16[256,2048]{1,0:T(8,128)(2,1)S(1)}, bf16[256,2048]{1,0:T(8,128)(2,1)S(1)}, u32[]{:S(2)}, u32[]{:S(2)}) %collective-permute-start) | collective-permute-done | bytes 1048608 | tf_op jit(solution)/shard_map/ppermute | solution.py:28
  49.4 7.2 %collective-permute-done.2 = bf16[128,2048]{1,0:T(8,128)(2,1)S(1)} collective-permute-done((bf16[128,2048]{1,0:T(8,128)(2,1)S(1)}, bf16[128,2048]{1,0:T(8,128)(2,1)S(1)}, u32[]{:S(2)}, u32[]{:S(2)}) %collective-permute-start.2) | collective-permute-done | bytes 524320 | tf_op jit(solution)/shard_map/ppermute | solution.py:28
  66.5 20.3 %collective-permute-done.4 = bf16[256,2048]{1,0:T(8,128)(2,1)S(1)} collective-permute-done((bf16[256,2048]{1,0:T(8,128)(2,1)S(1)}, bf16[256,2048]{1,0:T(8,128)(2,1)S(1)}, u32[]{:S(2)}, u32[]{:S(2)}) %collective-permute-start.4) | collective-permute-done | bytes 1048608 | tf_op jit(solution)/shard_map/ppermute | solution.py:28
  89.2 3.7 fusion.39
  93.6 15.3 %norms.1 = (bf16[2048,2048]{1,0:T(8,128)(2,1)}, bf16[2048,2048]{1,0:T(8,128)(2,1)}, bf16[2048,2048]{1,0:T(8,128)(2,1)}) custom-call(bf16[1024,2048]{1,0:T(8,128)(2,1)} %constant_dynamic-update-slice_fusion.near, bf16[1024,2048]{1,0:T(8,128)(2,1)} %collective-permute-done.6.far, f32[1,2048]{1,0:T(1,128)S(1)} %bitcast.120, f32[1,2048]{1,0:T(1,128)S(1)} %bitcast.126, ...), custom_call_target="tpu_custom_call" | custom-call | flops 1000000000 | bytes 1000000 | tf_op jit(solution)/shard_map/norms/pallas_call | solution.py:441
  116.1 4.5 all-to-all-start
  123.9 10.7 %product.4 = f32[2048,768]{1,0:T(8,128)} custom-call(bf16[2048,2048]{1,0:T(8,128)(2,1)} %get-tuple-element.210.left, bf16[2048,768]{1,0:T(8,128)(2,1)S(1)} %slice.210.right.qkv_weight), custom_call_target="tpu_custom_call" | custom-call | flops 1000000000 | bytes 1000000 | tf_op jit(solution)/shard_map/product/pallas_call | solution.py:170
  143.1 3.3 copy-done.10
  146.5 5.6 product.5
  152.1 28.7 %attention.1 = (bf16[8,256,256]{2,1,0:T(8,128)(2,1)S(1)}, bf16[8,256,256]{2,1,0:T(8,128)(2,1)S(1)}, bf16[8,256,768]{2,1,0:T(8,128)(2,1)}) custom-call(s32[8]{0:T(128)S(1)} %get-tuple-element.404.order, s32[8]{0:T(128)S(1)} %get-tuple-element.403.first, f32[8,256,768]{2,1,0:T(8,128)} %bitcast.145, f32[1,768]{1,0:T(1,128)S(1)} %maximum_convert_fusion.bias, ...), custom_call_target="tpu_custom_call" | custom-call | flops 1000000000 | bytes 1000000 | tf_op jit(solution)/shard_map/attention/pallas_call | solution.py:632
  181.9 5.6 wide.1
  188.5 4.3 all-to-all-start.1
  195.1 9.9 %product.6 = bf16[2048,768]{1,0:T(8,128)(2,1)S(1)} custom-call(bf16[2048,2048]{1,0:T(8,128)(2,1)} %get-tuple-element.210.left, bf16[2048,768]{1,0:T(8,128)(2,1)} %bitcast.113), custom_call_target="tpu_custom_call" | custom-call | flops 1000000000 | bytes 1000000 | tf_op jit(solution)/shard_map/product/pallas_call | solution.py:170
  205.1 3.1 all-to-all-done.1
  208.2 3.8 pad_maximum_fusion
  212.0 3.4 slice_select_fusion
  215.4 3.5 collective-permute-start.10
  222.1 16.1 %hidden.1 = (bf16[2048,1024]{1,0:T(8,128)(2,1)S(1)}, bf16[2048,1024]{1,0:T(8,128)(2,1)}) custom-call(bf16[2048,2048]{1,0:T(8,128)(2,1)} %get-tuple-element.224.tokens.left, bf16[2048,1024]{1,0:T(8,128)(2,1)} %all-gather.3.cloned.1.call-done.weight, f32[1,1024]{1,0:T(1,128)S(1)} %bitcast.128), custom_call_target="tpu_custom_call" | custom-call | flops 1000000000 | bytes 1000000 | tf_op jit(solution)/shard_map/hidden/pallas_call | solution.py:212
  239.0 4.2 collective-permute-done.11
  246.1 4.5 fusion.24
  250.6 4.3 collective-permute-start.14
  259.7 12.3 %product.7 = bf16[2048,1024]{1,0:T(8,128)(2,1)S(1)} custom-call(bf16[2048,2048]{1,0:T(8,128)(2,1)} %copy-done.10, bf16[2048,1024]{1,0:T(8,128)(2,1)} %copy-done.3), custom_call_target="tpu_custom_call" | custom-call | flops 1000000000 | bytes 1000000 | tf_op jit(solution)/shard_map/product/pallas_call | solution.py:170
  276.1 4.1 collective-permute-done.15
  280.2 5.0 fusion.22
  285.2 5.1 collective-permute-start.18
  291.6 18.7 %all_to_all.54 = bf16[8,256,256]{2,1,0:T(8,128)(2,1)} all-to-all(bf16[8,256,256]{2,1,0:T(8,128)(2,1)S(1)} %copy-done.7), channel_id=1, replica_groups=mesh['dp'=4,'head'=4,'blk'=2] {'head','blk'}, dimensions={0} | all-to-all | bytes 2097152 | tf_op jit(solution)/shard_map/all_to_all | solution.py:811
  322.1 4.4 fusion.20
  342.7 9.3 %collective-permute-done.20 = bf16[512,1024]{1,0:T(8,128)(2,1)S(1)} collective-permute-done((bf16[512,1024]{1,0:T(8,128)(2,1)S(1)}, bf16[512,1024]{1,0:T(8,128)(2,1)S(1)}, u32[]{:S(2)}, u32[]{:S(2)}) %collective-permute-start.20) | collective-permute-done | bytes 1048608 | tf_op jit(solution)/shard_map/ppermute | solution.py:63
  352.0 4.3 collective-permute-done.21
  363.0 8.6 %far.1 = bf16[1024,2048]{1,0:T(8,128)(2,1)} custom-call(bf16[2048,1024]{1,0:T(8,128)(2,1)} %copy-done.3, bf16[2048,1024]{1,0:T(8,128)(2,1)} %copy-done.13), custom_call_target="tpu_custom_call" | custom-call | flops 1000000000 | bytes 1000000 | tf_op jit(solution)/shard_map/far/pallas_call | solution.py:326
  373.2 3.1 add_convert_fusion
  377.3 13.6 %hidden_grad.1 = (bf16[2048,1024]{1,0:T(8,128)(2,1)S(1)}, f32[1,1024]{1,0:T(1,128)S(1)}) custom-call(bf16[2048,2048]{1,0:T(8,128)(2,1)} %copy-done.10, bf16[2048,1024]{1,0:T(8,128)(2,1)} %copy-done.13, bf16[2048,1024]{1,0:T(8,128)(2,1)} %get-tuple-element.258.slope), custom_call_target="tpu_custom_call" | custom-call | flops 1000000000 | bytes 1000000 | tf_op jit(solution)/shard_map/hidden_grad/pallas_call | solution.py:240
  392.9 7.8 %collective-permute-done.23 = bf16[512,1024]{1,0:T(8,128)(2,1)S(1)} collective-permute-done((bf16[512,1024]{1,0:T(8,128)(2,1)S(1)}, bf16[512,1024]{1,0:T(8,128)(2,1)S(1)}, u32[]{:S(2)}, u32[]{:S(2)}) %collective-permute-start.23) | collective-permute-done | bytes 1048608 | tf_op jit(solution)/shard_map/ppermute | solution.py:28
  403.6 8.7 %near.1 = (bf16[2,256,1024]{2,1,0:T(8,128)(2,1)S(1)}, bf16[2,256,1024]{2,1,0:T(8,128)(2,1)S(1)}, bf16[2,256,1024]{2,1,0:T(8,128)(2,1)S(1)}, bf16[2,256,1024]{2,1,0:T(8,128)(2,1)S(1)}) custom-call(bf16[2048,1024]{1,0:T(8,128)(2,1)} %copy-done.3, bf16[2048,1024]{1,0:T(8,128)(2,1)} %copy-done.13, bf16[1024,2048]{1,0:T(8,128)(2,1)} %collective-permute-done.25.more), custom_call_target="tpu_custom_call" | custom-call | flops 1000000000 | bytes 1000000 | tf_op jit(solution)/shard_map/near/pallas_call | solution.py:349
  417.3 16.8 %share_far.1 = (bf16[1024,2048]{1,0:T(8,128)(2,1)}, f32[8,2048]{1,0:T(8,128)S(1)}) custom-call(bf16[2048,768]{1,0:T(8,128)(2,1)S(1)} %bitcast.115, bf16[2048,768]{1,0:T(8,128)(2,1)} %copy-done.2, bf16[2048,1024]{1,0:T(8,128)(2,1)} %copy-done.4, bf16[2048,1024]{1,0:T(8,128)(2,1)} %all-gather.3.cloned.1.call-done.weight, f32[1,2048]{1,0:T(1,128)S(1)} %bitcast.121, ...), custom_call_target="tpu_custom_call" | custom-call | flops 1000000000 | bytes 1000000 | tf_op jit(solution)/shard_map/share_far/pallas_call | solution.py:395
  434.1 3.8 collective-permute-done.28
  442.4 13.1 %halves_product.1 = (bf16[2048,512]{1,0:T(8,128)(2,1)}, bf16[2048,512]{1,0:T(8,128)(2,1)}) custom-call(bf16[2048,2048]{1,0:T(8,128)(2,1)} %get-tuple-element.224.tokens.left, bf16[2048,1024]{1,0:T(8,128)(2,1)} %copy-done.4), custom_call_target="tpu_custom_call" | custom-call | flops 1000000000 | bytes 1000000 | tf_op jit(solution)/shard_map/halves_product/pallas_call | solution.py:265
  459.9 21.3 %share_near.1 = (bf16[2,256,1024]{2,1,0:T(8,128)(2,1)S(1)}, bf16[2,256,1024]{2,1,0:T(8,128)(2,1)}, bf16[2,256,1024]{2,1,0:T(8,128)(2,1)S(1)}, bf16[2,256,1024]{2,1,0:T(8,128)(2,1)S(1)}, f32[8,2048]{1,0:T(8,128)S(1)}) custom-call(bf16[2048,768]{1,0:T(8,128)(2,1)} %bitcast.114, bf16[2048,768]{1,0:T(8,128)(2,1)} %copy-done.2, bf16[2048,1024]{1,0:T(8,128)(2,1)} %copy-done.4, ...), custom_call_target="tpu_custom_call" | custom-call | flops 1000000000 | bytes 1000000 | tf_op jit(solution)/shard_map/share_near/pallas_call | solution.py:395
  504.6 11.1 %spread.2 = (f32[512,6144]{1,0:T(8,128)}, f32[512,2048]{1,0:T(8,128)}) custom-call(s32[8]{0:T(128)S(1)} %stack.64.places, bf16[4,512,1024]{2,1,0:T(8,128)(2,1)} %bitcast.44.near, bf16[4,512,1024]{2,1,0:T(8,128)(2,1)} %bitcast.45.far), custom_call_target="tpu_custom_call" | custom-call | flops 1000000000 | bytes 1000000 | tf_op jit(solution)/shard_map/spread/pallas_call | solution.py:480
  515.7 17.2 %collective-permute-done.37 = bf16[256,1024]{1,0:T(8,128)(2,1)} collective-permute-done((bf16[256,1024]{1,0:T(8,128)(2,1)}, bf16[256,1024]{1,0:T(8,128)(2,1)}, u32[]{:S(2)}, u32[]{:S(2)}) %collective-permute-start.37) | collective-permute-done | bytes 524320 | tf_op jit(solution)/shard_map/ppermute | solution.py:28
  552.2 8.6 %collective-permute-done.44 = f32[200,128]{1,0:T(8,128)S(1)} collective-permute-done((f32[200,128]{1,0:T(8,128)S(1)}, f32[200,128]{1,0:T(8,128)S(1)}, u32[]{:S(2)}, u32[]{:S(2)}) %collective-permute-start.44) | collective-permute-done | bytes 102432 | tf_op jit(solution)/shard_map/ppermute | solution.py:152
  564.5 7.2 %collective-permute-done.42 = bf16[256,1024]{1,0:T(8,128)(2,1)} collective-permute-done((bf16[256,1024]{1,0:T(8,128)(2,1)}, bf16[256,1024]{1,0:T(8,128)(2,1)}, u32[]{:S(2)}, u32[]{:S(2)}) %collective-permute-start.42) | collective-permute-done | bytes 524320 | tf_op jit(solution)/shard_map/ppermute | solution.py:28
  587.1 10.7 %spread.3 = f32[512,8192]{1,0:T(8,128)} custom-call(s32[8]{0:T(128)S(1)} %stack.64.places, bf16[4,512,1024]{2,1,0:T(8,128)(2,1)} %bitcast.51.near, bf16[4,512,1024]{2,1,0:T(8,128)(2,1)} %bitcast.52.far), custom_call_target="tpu_custom_call" | custom-call | flops 1000000000 | bytes 1000000 | tf_op jit(solution)/shard_map/spread/pallas_call | solution.py:480
  604.2 3.6 collective-permute-done.55
  610.9 5.1 halves.2.rest_0_
  615.9 3.2 collective-permute-done.56
  621.6 5.1 halves.3
  (392 shorter events, 197.5 us)
Async XLA Ops:
  7.2 106.6 %all-gather.5.cloned.1.call-start = ((), (), s32[]{:S(2)}) async-start(), calls=%async_computation.7 | async-start | bytes 5242880 | tf_op jit(solution)/shard_map/all_gather | solution.py:55
  16.3 26.1 %collective-permute-start = (bf16[256,2048]{1,0:T(8,128)(2,1)S(1)}, bf16[256,2048]{1,0:T(8,128)(2,1)S(1)}, u32[]{:S(2)}, u32[]{:S(2)}) collective-permute-start(bf16[256,2048]{1,0:T(8,128)(2,1)S(1)} %bitcast.138), channel_id=1, source_target_pairs={{0,2},{2,0},{4,6},{6,4},{1,3},{3,1},{5,7},{7,5},{8,10},{10,8},{12,... | collective-permute-start | bytes 3145736 | tf_op jit(solution)/shard_map/ppermute | solution.py:28
  19.3 24.6 %collective-permute-start.1 = (bf16[256,2048]{1,0:T(8,128)(2,1)S(1)}, bf16[256,2048]{1,0:T(8,128)(2,1)S(1)}, u32[]{:S(2)}, u32[]{:S(2)}) collective-permute-start(bf16[256,2048]{1,0:T(8,128)(2,1)S(1)} %bitcast.139), channel_id=1, source_target_pairs={{0,4},{2,6},{4,0},{6,2},{1,5},{3,7},{5,1},{7,3},{8,12},{10,14},{12... | collective-permute-start | bytes 3145736 | tf_op jit(solution)/shard_map/ppermute | solution.py:28
  20.8 191.2 %all-gather.3.cloned.1.call-start = ((), (), s32[]{:S(2)}) async-start(), calls=%async_computation.6 | async-start | bytes 5242880 | tf_op jit(solution)/shard_map/all_gather | solution.py:55
  59.9 27.2 %collective-permute-start.6 = (bf16[1024,2048]{1,0:T(8,128)(2,1)}, bf16[1024,2048]{1,0:T(8,128)(2,1)}, u32[]{:S(2)}, u32[]{:S(2)}) collective-permute-start(bf16[1024,2048]{1,0:T(8,128)(2,1)} %constant_dynamic-update-slice_fusion.near), channel_id=1, source_target_pairs={{0,1},{1,0},{2,3},{3,2},{4,5},{5,4},{6,7},{7,6},{8,9},{9,8},{10,11... | collective-permute-start | bytes 12582920 | tf_op jit(solution)/shard_map/ppermute | solution.py:32
  61.2 25.6 %collective-permute-start.4 = (bf16[256,2048]{1,0:T(8,128)(2,1)S(1)}, bf16[256,2048]{1,0:T(8,128)(2,1)S(1)}, u32[]{:S(2)}, u32[]{:S(2)}) collective-permute-start(bf16[256,2048]{1,0:T(8,128)(2,1)S(1)} %bitcast.146), channel_id=1, source_target_pairs={{0,2},{2,0},{4,6},{6,4},{1,3},{3,1},{5,7},{7,5},{8,10},{10,8},{12,... | collective-permute-start | bytes 3145736 | tf_op jit(solution)/shard_map/ppermute | solution.py:28
  61.8 25.3 %collective-permute-start.5 = (bf16[256,2048]{1,0:T(8,128)(2,1)S(1)}, bf16[256,2048]{1,0:T(8,128)(2,1)S(1)}, u32[]{:S(2)}, u32[]{:S(2)}) collective-permute-start(bf16[256,2048]{1,0:T(8,128)(2,1)S(1)} %bitcast.147), channel_id=1, source_target_pairs={{0,4},{2,6},{4,0},{6,2},{1,5},{3,7},{5,1},{7,3},{8,12},{10,14},{12... | collective-permute-start | bytes 3145736 | tf_op jit(solution)/shard_map/ppermute | solution.py:28
  87.1 21.7 %collective-permute-start.7 = (bf16[128,2048]{1,0:T(8,128)(2,1)S(1)}, bf16[128,2048]{1,0:T(8,128)(2,1)S(1)}, u32[]{:S(2)}, u32[]{:S(2)}) collective-permute-start(bf16[128,2048]{1,0:T(8,128)(2,1)S(1)} %slice.204), channel_id=1, source_target_pairs={{0,4},{2,6},{4,0},{6,2},{1,5},{3,7},{5,1},{7,3},{8,12},{10,14},{12... | collective-permute-start | bytes 1572872 | tf_op jit(solution)/shard_map/ppermute | solution.py:28
  87.7 21.1 %collective-permute-start.8 = (bf16[128,2048]{1,0:T(8,128)(2,1)S(1)}, bf16[128,2048]{1,0:T(8,128)(2,1)S(1)}, u32[]{:S(2)}, u32[]{:S(2)}) collective-permute-start(bf16[128,2048]{1,0:T(8,128)(2,1)S(1)} %slice.205), channel_id=1, source_target_pairs={{0,2},{2,0},{4,6},{6,4},{1,3},{3,1},{5,7},{7,5},{8,10},{10,8},{12,... | collective-permute-start | bytes 1572872 | tf_op jit(solution)/shard_map/ppermute | solution.py:28
  113.8 23.8 %collective-permute-start.9 = (bf16[1024,2048]{1,0:T(8,128)(2,1)}, bf16[1024,2048]{1,0:T(8,128)(2,1)}, u32[]{:S(2)}, u32[]{:S(2)}) collective-permute-start(bf16[1024,2048]{1,0:T(8,128)(2,1)} %constant_dynamic-update-slice_fusion.5), channel_id=1, source_target_pairs={{0,1},{1,0},{2,3},{3,2},{4,5},{5,4},{6,7},{7,6},{8,9},{9,8},{10,11... | collective-permute-start | bytes 12582920 | tf_op jit(solution)/shard_map/ppermute | solution.py:32
  116.1 20.1 %all-to-all-start = ((bf16[8,256,256]{2,1,0:T(8,128)(2,1)}), bf16[8,256,256]{2,1,0:T(8,128)(2,1)}, u32[]{:S(2)}, u32[]{:S(2)}) async-start(bf16[8,256,256]{2,1,0:T(8,128)(2,1)} %bitcast.18), calls=%async_computation | async-start | bytes 2097152 | tf_op jit(solution)/shard_map/all_to_all | solution.py:761
  188.5 19.7 %all-to-all-start.1 = ((bf16[256,8,256]{2,0,1:T(8,128)(2,1)}), bf16[256,8,256]{2,0,1:T(8,128)(2,1)}, u32[]{:S(2)}, u32[]{:S(2)}) async-start(bf16[256,8,256]{2,0,1:T(8,128)(2,1)} %bitcast.110), calls=%async_computation.1 | async-start | bytes 2097152 | tf_op jit(solution)/shard_map/all_to_all | solution.py:784
  192.8 264.5 %reduce-scatter.4.cloned.1.call-start = ((), (), s32[]{:S(2)}) async-start(), calls=%async_computation.8 | async-start | bytes 5242880 | tf_op jit(solution)/shard_map/reduce_scatter | solution.py:59
  215.4 23.6 %collective-permute-start.10 = (bf16[512,1024]{1,0:T(8,128)(2,1)}, bf16[512,1024]{1,0:T(8,128)(2,1)S(1)}, u32[]{:S(2)}, u32[]{:S(2)}) collective-permute-start(bf16[512,1024]{1,0:T(8,128)(2,1)} %get-tuple-element.376), channel_id=1, source_target_pairs={{0,8},{8,16},{16,24},{1,9},{9,17},{17,25},{2,10},{10,18},{18,26},{... | collective-permute-start | bytes 3145736 | tf_op jit(solution)/shard_map/ppermute | solution.py:63
  218.9 24.3 %collective-permute-start.11 = (bf16[512,1024]{1,0:T(8,128)(2,1)}, bf16[512,1024]{1,0:T(8,128)(2,1)}, u32[]{:S(2)}, u32[]{:S(2)}) collective-permute-start(bf16[512,1024]{1,0:T(8,128)(2,1)} %get-tuple-element.375), channel_id=1, source_target_pairs={{24,16},{16,8},{8,0},{25,17},{17,9},{9,1},{26,18},{18,10},{10,2},{... | collective-permute-start | bytes 3145736 | tf_op jit(solution)/shard_map/ppermute | solution.py:67
  220.2 23.9 %collective-permute-start.12 = (bf16[2048,256]{1,0:T(8,128)(2,1)}, bf16[2048,256]{1,0:T(8,128)(2,1)S(1)}, u32[]{:S(2)}, u32[]{:S(2)}) collective-permute-start(bf16[2048,256]{1,0:T(8,128)(2,1)} %slice.211), channel_id=1, source_target_pairs={{0,2},{2,0},{4,6},{6,4},{1,3},{3,1},{5,7},{7,5},{8,10},{10,8},{12,... | collective-permute-start | bytes 3145736 | tf_op jit(solution)/shard_map/ppermute | solution.py:28
  220.8 24.8 %collective-permute-start.13 = (bf16[2048,256]{1,0:T(8,128)(2,1)}, bf16[2048,256]{1,0:T(8,128)(2,1)S(1)}, u32[]{:S(2)}, u32[]{:S(2)}) collective-permute-start(bf16[2048,256]{1,0:T(8,128)(2,1)} %slice.211), channel_id=1, source_target_pairs={{0,4},{2,6},{4,0},{6,2},{1,5},{3,7},{5,1},{7,3},{8,12},{10,14},{12... | collective-permute-start | bytes 3145736 | tf_op jit(solution)/shard_map/ppermute | solution.py:28
  250.6 25.5 %collective-permute-start.14 = (bf16[512,1024]{1,0:T(8,128)(2,1)}, bf16[512,1024]{1,0:T(8,128)(2,1)S(1)}, u32[]{:S(2)}, u32[]{:S(2)}) collective-permute-start(bf16[512,1024]{1,0:T(8,128)(2,1)} %get-tuple-element.374), channel_id=1, source_target_pairs={{0,8},{8,16},{16,24},{1,9},{9,17},{17,25},{2,10},{10,18},{18,26},{... | collective-permute-start | bytes 3145736 | tf_op jit(solution)/shard_map/ppermute | solution.py:63
  255.0 25.2 %collective-permute-start.15 = (bf16[512,1024]{1,0:T(8,128)(2,1)}, bf16[512,1024]{1,0:T(8,128)(2,1)S(1)}, u32[]{:S(2)}, u32[]{:S(2)}) collective-permute-start(bf16[512,1024]{1,0:T(8,128)(2,1)} %get-tuple-element.373), channel_id=1, source_target_pairs={{24,16},{16,8},{8,0},{25,17},{17,9},{9,1},{26,18},{18,10},{10,2},{... | collective-permute-start | bytes 3145736 | tf_op jit(solution)/shard_map/ppermute | solution.py:67
  257.1 17.0 %collective-permute-start.16 = (bf16[1024,256]{1,0:T(8,128)(2,1)}, bf16[1024,256]{1,0:T(8,128)(2,1)S(1)}, u32[]{:S(2)}, u32[]{:S(2)}) collective-permute-start(bf16[1024,256]{1,0:T(8,128)(2,1)} %slice.212), channel_id=1, source_target_pairs={{0,4},{2,6},{4,0},{6,2},{1,5},{3,7},{5,1},{7,3},{8,12},{10,14},{12... | collective-permute-start | bytes 1572872 | tf_op jit(solution)/shard_map/ppermute | solution.py:28
  285.2 26.6 %collective-permute-start.18 = (bf16[512,1024]{1,0:T(8,128)(2,1)}, bf16[512,1024]{1,0:T(8,128)(2,1)}, u32[]{:S(2)}, u32[]{:S(2)}) collective-permute-start(bf16[512,1024]{1,0:T(8,128)(2,1)} %get-tuple-element.380), channel_id=1, source_target_pairs={{0,8},{8,16},{16,24},{1,9},{9,17},{17,25},{2,10},{10,18},{18,26},{... | collective-permute-start | bytes 3145736 | tf_op jit(solution)/shard_map/ppermute | solution.py:63
  290.3 24.4 %collective-permute-start.19 = (bf16[512,1024]{1,0:T(8,128)(2,1)}, bf16[512,1024]{1,0:T(8,128)(2,1)}, u32[]{:S(2)}, u32[]{:S(2)}) collective-permute-start(bf16[512,1024]{1,0:T(8,128)(2,1)} %get-tuple-element.379), channel_id=1, source_target_pairs={{24,16},{16,8},{8,0},{25,17},{17,9},{9,1},{26,18},{18,10},{10,2},{... | collective-permute-start | bytes 3145736 | tf_op jit(solution)/shard_map/ppermute | solution.py:67
  326.5 25.5 %collective-permute-start.20 = (bf16[512,1024]{1,0:T(8,128)(2,1)S(1)}, bf16[512,1024]{1,0:T(8,128)(2,1)S(1)}, u32[]{:S(2)}, u32[]{:S(2)}) collective-permute-start(bf16[512,1024]{1,0:T(8,128)(2,1)S(1)} %get-tuple-element.378), channel_id=1, source_target_pairs={{0,8},{8,16},{16,24},{1,9},{9,17},{17,25},{2,10},{10,18},{18,26},{... | collective-permute-start | bytes 3145736 | tf_op jit(solution)/shard_map/ppermute | solution.py:63
  329.1 27.3 %collective-permute-start.21 = (bf16[512,1024]{1,0:T(8,128)(2,1)S(1)}, bf16[512,1024]{1,0:T(8,128)(2,1)S(1)}, u32[]{:S(2)}, u32[]{:S(2)}) collective-permute-start(bf16[512,1024]{1,0:T(8,128)(2,1)S(1)} %get-tuple-element.377), channel_id=1, source_target_pairs={{24,16},{16,8},{8,0},{25,17},{17,9},{9,1},{26,18},{18,10},{10,2},{... | collective-permute-start | bytes 3145736 | tf_op jit(solution)/shard_map/ppermute | solution.py:67
  371.7 29.8 %collective-permute-start.25 = (bf16[1024,2048]{1,0:T(8,128)(2,1)}, bf16[1024,2048]{1,0:T(8,128)(2,1)}, u32[]{:S(2)}, u32[]{:S(2)}) collective-permute-start(bf16[1024,2048]{1,0:T(8,128)(2,1)} %far.1), channel_id=1, source_target_pairs={{0,1},{1,0},{2,3},{3,2},{4,5},{5,4},{6,7},{7,6},{8,9},{9,8},{10,11... | collective-permute-start | bytes 12582920 | tf_op jit(solution)/shard_map/ppermute | solution.py:32
  371.7 161.3 %reduce-scatter.6.cloned.1.call-start = ((), (), s32[]{:S(2)}) async-start(), calls=%async_computation.9 | async-start | bytes 2621440 | tf_op jit(solution)/shard_map/reduce_scatter | solution.py:59
  376.3 24.5 %collective-permute-start.23 = (bf16[512,1024]{1,0:T(8,128)(2,1)S(1)}, bf16[512,1024]{1,0:T(8,128)(2,1)S(1)}, u32[]{:S(2)}, u32[]{:S(2)}) collective-permute-start(bf16[512,1024]{1,0:T(8,128)(2,1)S(1)} %add_convert_fusion), channel_id=1, source_target_pairs={{0,2},{2,0},{4,6},{6,4},{1,3},{3,1},{5,7},{7,5},{8,10},{10,8},{12,... | collective-permute-start | bytes 3145736 | tf_op jit(solution)/shard_map/ppermute | solution.py:28
  377.3 24.1 %collective-permute-start.24 = (bf16[512,1024]{1,0:T(8,128)(2,1)S(1)}, bf16[512,1024]{1,0:T(8,128)(2,1)S(1)}, u32[]{:S(2)}, u32[]{:S(2)}) collective-permute-start(bf16[512,1024]{1,0:T(8,128)(2,1)S(1)} %add_convert_fusion), channel_id=1, source_target_pairs={{0,4},{2,6},{4,0},{6,2},{1,5},{3,7},{5,1},{7,3},{8,12},{10,14},{12... | collective-permute-start | bytes 3145736 | tf_op jit(solution)/shard_map/ppermute | solution.py:28
  415.4 22.5 %collective-permute-start.28 = (bf16[2,256,1024]{2,1,0:T(8,128)(2,1)S(1)}, bf16[2,256,1024]{2,1,0:T(8,128)(2,1)S(1)}, u32[]{:S(2)}, u32[]{:S(2)}) collective-permute-start(bf16[2,256,1024]{2,1,0:T(8,128)(2,1)S(1)} %get-tuple-element.271), channel_id=1, source_target_pairs={{0,2},{2,0},{4,6},{6,4},{1,3},{3,1},{5,7},{7,5},{8,10},{10,8},{12,... | collective-permute-start | bytes 3145736 | tf_op jit(solution)/shard_map/ppermute | solution.py:28
  416.4 22.2 %collective-permute-start.29 = (bf16[2,256,1024]{2,1,0:T(8,128)(2,1)S(1)}, bf16[2,256,1024]{2,1,0:T(8,128)(2,1)S(1)}, u32[]{:S(2)}, u32[]{:S(2)}) collective-permute-start(bf16[2,256,1024]{2,1,0:T(8,128)(2,1)S(1)} %get-tuple-element.272), channel_id=1, source_target_pairs={{0,4},{2,6},{4,0},{6,2},{1,5},{3,7},{5,1},{7,3},{8,12},{10,14},{12... | collective-permute-start | bytes 3145736 | tf_op jit(solution)/shard_map/ppermute | solution.py:28
  438.6 18.7 %collective-permute-start.32 = (bf16[1024,2048]{1,0:T(8,128)(2,1)}, bf16[1024,2048]{1,0:T(8,128)(2,1)}, u32[]{:S(2)}, u32[]{:S(2)}) collective-permute-start(bf16[1024,2048]{1,0:T(8,128)(2,1)} %get-tuple-element.279), channel_id=1, source_target_pairs={{0,1},{1,0},{2,3},{3,2},{4,5},{5,4},{6,7},{7,6},{8,9},{9,8},{10,11... | collective-permute-start | bytes 12582920 | tf_op jit(solution)/shard_map/ppermute | solution.py:32
  440.5 16.8 %collective-permute-start.31 = (bf16[256,1024]{1,0:T(8,128)(2,1)S(1)}, bf16[256,1024]{1,0:T(8,128)(2,1)}, u32[]{:S(2)}, u32[]{:S(2)}) collective-permute-start(bf16[256,1024]{1,0:T(8,128)(2,1)S(1)} %fusion.36), channel_id=1, source_target_pairs={{0,2},{2,0},{4,6},{6,4},{1,3},{3,1},{5,7},{7,5},{8,10},{10,8},{12,... | collective-permute-start | bytes 1572872 | tf_op jit(solution)/shard_map/ppermute | solution.py:28
  457.3 25.4 %collective-permute-start.33 = (bf16[512,1024]{1,0:T(8,128)(2,1)}, bf16[512,1024]{1,0:T(8,128)(2,1)}, u32[]{:S(2)}, u32[]{:S(2)}) collective-permute-start(bf16[512,1024]{1,0:T(8,128)(2,1)} %reduce-scatter.4.cloned.1.call-done), channel_id=1, source_target_pairs={{0,2},{2,0},{4,6},{6,4},{1,3},{3,1},{5,7},{7,5},{8,10},{10,8},{12,... | collective-permute-start | bytes 3145736 | tf_op jit(solution)/shard_map/ppermute | solution.py:28
  458.4 25.0 %collective-permute-start.34 = (bf16[512,1024]{1,0:T(8,128)(2,1)}, bf16[512,1024]{1,0:T(8,128)(2,1)}, u32[]{:S(2)}, u32[]{:S(2)}) collective-permute-start(bf16[512,1024]{1,0:T(8,128)(2,1)} %reduce-scatter.4.cloned.1.call-done), channel_id=1, source_target_pairs={{0,4},{2,6},{4,0},{6,2},{1,5},{3,7},{5,1},{7,3},{8,12},{10,14},{12... | collective-permute-start | bytes 3145736 | tf_op jit(solution)/shard_map/ppermute | solution.py:28
  459.9 104.7 %reduce-scatter.8.cloned.1.call-start = ((), (), s32[]{:S(2)}) async-start(), calls=%async_computation.10 | async-start | bytes 2621440 | tf_op jit(solution)/shard_map/reduce_scatter | solution.py:59
  488.3 16.3 %collective-permute-start.40 = (bf16[2048,1024]{1,0:T(8,128)(2,1)}, bf16[2048,1024]{1,0:T(8,128)(2,1)}, u32[]{:S(2)}, u32[]{:S(2)}) collective-permute-start(bf16[2048,1024]{1,0:T(8,128)(2,1)} %constant_dynamic-update-slice_fusion.17), channel_id=1, source_target_pairs={{0,1},{1,0},{2,3},{3,2},{4,5},{5,4},{6,7},{7,6},{8,9},{9,8},{10,11... | collective-permute-start | bytes 12582920 | tf_op jit(solution)/shard_map/ppermute | solution.py:32
  495.3 37.6 %collective-permute-start.35 = (bf16[2,256,1024]{2,1,0:T(8,128)(2,1)}, bf16[2,256,1024]{2,1,0:T(8,128)(2,1)}, u32[]{:S(2)}, u32[]{:S(2)}) collective-permute-start(bf16[2,256,1024]{2,1,0:T(8,128)(2,1)} %get-tuple-element.303), channel_id=1, source_target_pairs={{0,2},{2,0},{4,6},{6,4},{1,3},{3,1},{5,7},{7,5},{8,10},{10,8},{12,... | collective-permute-start | bytes 3145736 | tf_op jit(solution)/shard_map/ppermute | solution.py:28
  496.3 36.6 %collective-permute-start.36 = (bf16[2,256,1024]{2,1,0:T(8,128)(2,1)S(1)}, bf16[2,256,1024]{2,1,0:T(8,128)(2,1)}, u32[]{:S(2)}, u32[]{:S(2)}) collective-permute-start(bf16[2,256,1024]{2,1,0:T(8,128)(2,1)S(1)} %copy-done.9), channel_id=1, source_target_pairs={{0,4},{2,6},{4,0},{6,2},{1,5},{3,7},{5,1},{7,3},{8,12},{10,14},{12... | collective-permute-start | bytes 3145736 | tf_op jit(solution)/shard_map/ppermute | solution.py:28
  501.0 31.9 %collective-permute-start.37 = (bf16[256,1024]{1,0:T(8,128)(2,1)}, bf16[256,1024]{1,0:T(8,128)(2,1)}, u32[]{:S(2)}, u32[]{:S(2)}) collective-permute-start(bf16[256,1024]{1,0:T(8,128)(2,1)} %slice.229), channel_id=1, source_target_pairs={{0,4},{2,6},{4,0},{6,2},{1,5},{3,7},{5,1},{7,3},{8,12},{10,14},{12... | collective-permute-start | bytes 1572872 | tf_op jit(solution)/shard_map/ppermute | solution.py:28
  503.5 29.4 %collective-permute-start.38 = (bf16[256,1024]{1,0:T(8,128)(2,1)}, bf16[256,1024]{1,0:T(8,128)(2,1)}, u32[]{:S(2)}, u32[]{:S(2)}) collective-permute-start(bf16[256,1024]{1,0:T(8,128)(2,1)} %slice.230), channel_id=1, source_target_pairs={{0,2},{2,0},{4,6},{6,4},{1,3},{3,1},{5,7},{7,5},{8,10},{10,8},{12,... | collective-permute-start | bytes 1572872 | tf_op jit(solution)/shard_map/ppermute | solution.py:28
  543.5 30.7 %collective-permute-start.43 = (bf16[2048,1024]{1,0:T(8,128)(2,1)}, bf16[2048,1024]{1,0:T(8,128)(2,1)}, u32[]{:S(2)}, u32[]{:S(2)}) collective-permute-start(bf16[2048,1024]{1,0:T(8,128)(2,1)} %constant_dynamic-update-slice_fusion.22), channel_id=1, source_target_pairs={{0,1},{1,0},{2,3},{3,2},{4,5},{5,4},{6,7},{7,6},{8,9},{9,8},{10,11... | collective-permute-start | bytes 12582920 | tf_op jit(solution)/shard_map/ppermute | solution.py:32
  543.6 30.7 %collective-permute-start.45 = (bf16[512,512]{1,0:T(8,128)(2,1)}, bf16[512,512]{1,0:T(8,128)(2,1)}, u32[]{:S(2)}, u32[]{:S(2)}) collective-permute-start(bf16[512,512]{1,0:T(8,128)(2,1)} %reduce-scatter.6.cloned.1.call-done), channel_id=1, source_target_pairs={{0,2},{2,0},{4,6},{6,4},{1,3},{3,1},{5,7},{7,5},{8,10},{10,8},{12,... | collective-permute-start | bytes 1572872 | tf_op jit(solution)/shard_map/ppermute | solution.py:28
  544.7 29.6 %collective-permute-start.46 = (bf16[512,512]{1,0:T(8,128)(2,1)}, bf16[512,512]{1,0:T(8,128)(2,1)}, u32[]{:S(2)}, u32[]{:S(2)}) collective-permute-start(bf16[512,512]{1,0:T(8,128)(2,1)} %reduce-scatter.6.cloned.1.call-done), channel_id=1, source_target_pairs={{0,4},{2,6},{4,0},{6,2},{1,5},{3,7},{5,1},{7,3},{8,12},{10,14},{12... | collective-permute-start | bytes 1572872 | tf_op jit(solution)/shard_map/ppermute | solution.py:28
  549.1 22.6 %collective-permute-start.42 = (bf16[256,1024]{1,0:T(8,128)(2,1)}, bf16[256,1024]{1,0:T(8,128)(2,1)}, u32[]{:S(2)}, u32[]{:S(2)}) collective-permute-start(bf16[256,1024]{1,0:T(8,128)(2,1)} %fusion.38), channel_id=1, source_target_pairs={{0,2},{2,0},{4,6},{6,4},{1,3},{3,1},{5,7},{7,5},{8,10},{10,8},{12,... | collective-permute-start | bytes 1572872 | tf_op jit(solution)/shard_map/ppermute | solution.py:28
  574.3 23.6 %collective-permute-start.49 = (bf16[512,512]{1,0:T(8,128)(2,1)}, bf16[512,512]{1,0:T(8,128)(2,1)S(1)}, u32[]{:S(2)}, u32[]{:S(2)}) collective-permute-start(bf16[512,512]{1,0:T(8,128)(2,1)} %reduce-scatter.8.cloned.1.call-done), channel_id=1, source_target_pairs={{0,2},{2,0},{4,6},{6,4},{1,3},{3,1},{5,7},{7,5},{8,10},{10,8},{12,... | collective-permute-start | bytes 1572872 | tf_op jit(solution)/shard_map/ppermute | solution.py:28
  575.4 22.5 %collective-permute-start.50 = (bf16[512,512]{1,0:T(8,128)(2,1)}, bf16[512,512]{1,0:T(8,128)(2,1)S(1)}, u32[]{:S(2)}, u32[]{:S(2)}) collective-permute-start(bf16[512,512]{1,0:T(8,128)(2,1)} %reduce-scatter.8.cloned.1.call-done), channel_id=1, source_target_pairs={{0,4},{2,6},{4,0},{6,2},{1,5},{3,7},{5,1},{7,3},{8,12},{10,14},{12... | collective-permute-start | bytes 1572872 | tf_op jit(solution)/shard_map/ppermute | solution.py:28
  580.1 17.7 %collective-permute-start.51 = (f32[200,128]{1,0:T(8,128)S(1)}, f32[200,128]{1,0:T(8,128)S(1)}, u32[]{:S(2)}, u32[]{:S(2)}) collective-permute-start(f32[200,128]{1,0:T(8,128)S(1)} %add.326), channel_id=1, source_target_pairs={{0,4},{2,6},{4,0},{6,2},{1,5},{3,7},{5,1},{7,3},{8,12},{10,14},{12... | collective-permute-start | bytes 307208 | tf_op jit(solution)/shard_map/ppermute | solution.py:152
  581.7 16.1 %collective-permute-start.47 = (bf16[256,512]{1,0:T(8,128)(2,1)S(1)}, bf16[256,512]{1,0:T(8,128)(2,1)S(1)}, u32[]{:S(2)}, u32[]{:S(2)}) collective-permute-start(bf16[256,512]{1,0:T(8,128)(2,1)S(1)} %slice.242), channel_id=1, source_target_pairs={{0,4},{2,6},{4,0},{6,2},{1,5},{3,7},{5,1},{7,3},{8,12},{10,14},{12... | collective-permute-start | bytes 786440 | tf_op jit(solution)/shard_map/ppermute | solution.py:28
  (81 other events, 644.0 us)
Sparse Core Ops, SparseCore 0:
  21.0 80.1 all-gather.4
  113.9 81.2 all-gather.2
  371.8 74.4 reduce-scatter.3
  460.0 41.1 reduce-scatter.5
  504.7 41.9 reduce-scatter.7

commit v3 on v2

--- a/solution.py
+++ b/solution.py
@@ -47,7 +47,7 @@
 
 
 def gather_end(*pieces):
-    near = jnp.concatenate(pieces, axis=0)
+    near = join(*pieces)
     return near, other_core(near)
 
 
@@ -116,6 +116,11 @@
                 out = jnp.where(place == index, values[index], out)
         return out
 
+    first = choose(three[1], four[0], four[0], three[0]).astype(F32)
+    inner = (place == 1) | (place == 2)
+    second = jnp.where(inner, four[1].astype(F32), 0.0)
+    total = part_of(sums, place).astype(F32) + first + second
+    total, own, one, two, three, four = tie(total.astype(BF), own, one, two, three, four)
     up, down = 0, 1
     whole = jnp.zeros((4 * rows,) + own.shape[1:], own.dtype)
     for step, piece in enumerate(
@@ -127,11 +132,7 @@
         )
     ):
         whole = lax.dynamic_update_slice_in_dim(whole, piece, (place + step) % 4 * rows, 0)
-    first = choose(three[down], four[up], four[up], three[up]).astype(F32)
-    inner = (place == 1) | (place == 2)
-    second = jnp.where(inner, four[down].astype(F32), 0.0)
-    total = part_of(sums, place).astype(F32) + first + second
-    return whole, total.astype(BF)
+    return total, whole
 
 
 def plus(one, two):
@@ -250,28 +251,6 @@
         cost_estimate=LIGHT,
         name="hidden_grad",
     )(upstream, weight, slope)
-
-
-def halves_product(one, two, tile=512):
-    half = two.shape[1] // 2
-
-    def kernel(left, right, low, high):
-        values = lax.dot_general(left[...], right[...], TN, preferred_element_type=F32).astype(BF)
-        low[...] = values[:, :half]
-        high[...] = values[:, half:]
-
-    rows = one.shape[1]
-    out = pl.BlockSpec((tile, half), lambda i: (i, 0))
-    return pl.pallas_call(
-        kernel,
-        grid=(rows // tile,),
-        in_specs=[pl.BlockSpec((one.shape[0], tile), lambda i: (0, i)), whole(two)],
-        out_specs=[out, out],
-        out_shape=[jax.ShapeDtypeStruct((rows, half), BF)] * 2,
-        compiler_params=ROOM,
-        cost_estimate=LIGHT,
-        name="halves_product",
-    )(one, two)
 
 
 def put_split(step, side, block, left_keep, left_send, right_keep, right_send):
@@ -454,6 +433,67 @@
     )(near, far, *[v.astype(F32)[None, :] for v in vectors])
 
 
+def join_kernel(own, one, two, low, high, out):
+    half = low.shape[0]
+    for index, source in enumerate((own, one, two)):
+
+        @pl.when(pl.program_id(0) == index)
+        def copy(source=source):
+            out[...] = source[...]
+
+    @pl.when(pl.program_id(0) == 3)
+    def last():
+        out[:half, :] = low[...]
+        out[half:, :] = high[...]
+
+
+def join(*pieces):
+    rows, width = pieces[0].shape
+    return pl.pallas_call(
+        join_kernel,
+        grid=(4,),
+        in_specs=[whole(piece) for piece in pieces],
+        out_specs=pl.BlockSpec((rows, width), lambda i: (i, 0)),
+        out_shape=jax.ShapeDtypeStruct((4 * rows, width), BF),
+        compiler_params=ROOM,
+        cost_estimate=LIGHT,
+        name="join",
+    )(*pieces)
+
+
+def columns_kernel(places, values, near, far, out):
+    count = pl.num_programs(0) // 2
+
+    def write(source):
+        out[...] = jnp.dot(values[...], source[...], preferred_element_type=F32)
+
+    pl.when(pl.program_id(0) < count)(lambda: write(near))
+    pl.when(pl.program_id(0) >= count)(lambda: write(far))
+
+
+def columns_product(values, near, far, places):
+    count = lax.axis_size("head")
+    rows, depth = values.shape
+    width = near.shape[1]
+    return pl.pallas_call(
+        columns_kernel,
+        grid_spec=pltpu.PrefetchScalarGridSpec(
+            num_scalar_prefetch=1,
+            grid=(2 * count,),
+            in_specs=[
+                pl.BlockSpec((rows, depth), lambda r, p: (0, 0)),
+                pl.BlockSpec((depth, width), lambda r, p: (jnp.minimum(r, count - 1), 0)),
+                pl.BlockSpec((depth, width), lambda r, p: (jnp.maximum(r - count, 0), 0)),
+            ],
+            out_specs=pl.BlockSpec((rows, width), lambda r, p: (0, p[r])),
+        ),
+        out_shape=jax.ShapeDtypeStruct((rows, 2 * count * width), F32),
+        compiler_params=ROOM,
+        cost_estimate=LIGHT,
+        name="columns",
+    )(places, values, near, far)
+
+
 def spread_kernel(parts, places, near, far, *outs):
     count = near.shape[0]
     each = near.shape[2] // sum(parts)
@@ -492,41 +532,29 @@
     )(places, near.reshape(count, rows, width), far.reshape(count, rows, width))
 
 
-def halves_kernel(places, near, far, *rest):
-    count = pl.num_programs(0) // 2
-    out = rest[-1]
-
-    def write(source):
-        out[...] = source[...].astype(F32)
-
-    pl.when(pl.program_id(0) < count)(lambda: write(near))
-    pl.when(pl.program_id(0) >= count)(lambda: write(far))
-
-
-def spread_half(near, far, places, side, first_column, begun=None):
+def place_kernel(places, blocks, *rest):
+    rest[-1][...] = blocks[...].astype(F32)
+
+
+def place_blocks(blocks, places, begun=None):
     count = lax.axis_size("head")
-    rows = near.shape[0] // count
-    width = near.shape[1] - first_column
-    column = first_column // width
-    specs = [
-        pl.BlockSpec((rows, width), lambda r, p: (jnp.minimum(r, count - 1), column)),
-        pl.BlockSpec((rows, width), lambda r, p: (jnp.maximum(r - count, 0), column)),
-    ]
+    rows, width = blocks.shape[0] // count, blocks.shape[1]
     extra = () if begun is None else (begun,)
     return pl.pallas_call(
-        halves_kernel,
+        place_kernel,
         grid_spec=pltpu.PrefetchScalarGridSpec(
             num_scalar_prefetch=1,
-            grid=(2 * count,),
-            in_specs=specs + [pl.BlockSpec(memory_space=pl.ANY) for _ in extra],
-            out_specs=pl.BlockSpec((rows, width), lambda r, p: (0, 2 * p[r] + side)),
+            grid=(count,),
+            in_specs=[pl.BlockSpec((rows, width), lambda r, p: (r, 0))]
+            + [pl.BlockSpec(memory_space=pl.ANY) for _ in extra],
+            out_specs=pl.BlockSpec((rows, width), lambda r, p: (0, p[r])),
         ),
-        out_shape=jax.ShapeDtypeStruct((rows, 4 * count * width), F32),
-        input_output_aliases={3: 0} if extra else {},
+        out_shape=jax.ShapeDtypeStruct((rows, 2 * count * width), F32),
+        input_output_aliases={2: 0} if extra else {},
         compiler_params=ROOM,
         cost_estimate=LIGHT,
-        name="halves",
-    )(places, near, far, *extra)
+        name="place",
+    )(places, blocks, *extra)
 
 
 def turn(values, cosine, sine):
@@ -721,6 +749,7 @@
         (head_place ^ (r % head_count)) * blk_count + (blk_place ^ (r // head_count))
         for r in range(plane)
     ]
+    place_list = jnp.stack(places).astype(jnp.int32)
     absolute = jnp.arange(plane, dtype=jnp.int32)
     order = (absolute % blk_count ^ blk_place) * head_count + (absolute // blk_count ^ head_place)
 
@@ -729,38 +758,40 @@
 
     own_in = block_in.reshape(span, width)
     own_up = cotangent.reshape(span, width)
-    att_shard = jnp.concatenate(
+    out_shard = columns(out_weight, HEAD_SIZE)
+    qkv_shard = jnp.concatenate(
         [
             columns(qkv_weight[:, part * width : (part + 1) * width], HEAD_SIZE)
             for part in range(3)
-        ]
-        + [columns(out_weight, HEAD_SIZE)],
+        ],
         axis=1,
     )
-    att_shard, own_in = tie(att_shard, own_in)
-    att_mine = data_gather(att_shard)
+    out_shard, own_in = tie(out_shard, own_in)
+    out_mine = data_gather(out_shard)
     tokens_begun = gather_start(own_in)
-    tokens_begun, own_up = tie(tokens_begun, own_up)
+    tokens_begun, own_up, qkv_shard = tie(tokens_begun, own_up, qkv_shard)
+    qkv_mine = data_gather(qkv_shard)
     upstream_begun = gather_start(own_up)
     tokens_near, tokens_far = gather_end(*gather_middle(*tokens_begun))
     fc1_shard, tokens_near = tie(columns(fc1_weight, each), tokens_near)
     fc1_mine = data_gather(fc1_shard)
-    upstream_begun, tokens_near, tokens_far = tie(upstream_begun, tokens_near, tokens_far)
-    upstream_begun = gather_middle(*upstream_begun)
     cosine, sine = rotary_tables(seg_lengths, jnp.stack(places), span)
     normed, attn_in, mlp_in = norms(
         tokens_near, tokens_far, span, ln1_gain, ln1_bias, ln2_gain, ln2_bias
     )
-    upstream_begun, attn_in, cosine, sine = tie(upstream_begun, attn_in, cosine, sine)
-    upstream_near, upstream_far = gather_end(*upstream_begun)
-    upstream_near, att_mine, attn_in = tie(upstream_near, att_mine, attn_in)
+    upstream_begun, attn_in, cosine, sine, out_mine = tie(
+        upstream_begun, attn_in, cosine, sine, out_mine
+    )
+    out_rows = lax.all_to_all(out_mine, ("head", "blk"), split_axis=0, concat_axis=1, tiled=True)
+    upstream_near, upstream_far = gather_end(*gather_middle(*upstream_begun))
+    upstream_near, qkv_mine, attn_in = tie(upstream_near, qkv_mine, attn_in)
 
     first = segment_start(seg_lengths, absolute * span) // span
 
-    qkv_mine, out_mine = att_mine[:, : 3 * HEAD_SIZE], att_mine[:, 3 * HEAD_SIZE :]
-    out_rows = lax.all_to_all(out_mine, ("head", "blk"), split_axis=0, concat_axis=1, tiled=True)
     joined = product(attn_in, qkv_mine, NN, kind=F32)
-    upstream_near, upstream_far, joined = tie(upstream_near, upstream_far, joined)
+    upstream_near, upstream_far, joined, out_rows = tie(
+        upstream_near, upstream_far, joined, out_rows
+    )
     upstream = jnp.concatenate([upstream_near, upstream_far], axis=0)
     context_grad = product(upstream, out_rows, NT)
     bias_mine = jnp.concatenate(
@@ -820,23 +851,9 @@
             move_three, att_grad, own_context, out_moved
         )
         move_four = exchange_four(att_grad, *move_three)
-    out_pieces = gather_end(*out_moved)
-    attn_out = jnp.zeros((span, width), F32)
-    for half, pieces in enumerate(out_pieces):
-        for index in range(head_count):
-            attn_out = lax.dynamic_update_slice(
-                attn_out,
-                jnp.dot(
-                    own_context,
-                    pieces[index * width : (index + 1) * width],
-                    preferred_element_type=F32,
-                ),
-                (0, places[half * head_count + index] * HEAD_SIZE),
-            )
-    attn_out = attn_out + out_bias
     if chain:
-        move_four, fc2_grad, attn_out = tie(move_four, fc2_grad, attn_out)
-        fc2_mine, att_sum = exchange_end(
+        move_four, fc2_grad = tie(move_four, fc2_grad)
+        att_sum, fc2_mine = exchange_end(
             fc2_shard, att_grad, move_one, move_two, move_three, move_four
         )
     fc2_sum = data_scatter(fc2_grad)
@@ -850,28 +867,31 @@
     mlp_parts = product_near(active, fc2_mine, mlp_got, span)
     att_moved, mlp_parts, hidden_grad = tie(att_moved, mlp_parts, hidden_grad)
     mlp_got = collect_start(*mlp_parts)
+    fc1_grad = product(mlp_in, hidden_grad, TN)
+    att_near, out_near = join(*att_moved), join(*out_moved)
+    mlp_got, fc1_grad, hidden_grad, fc2_sum, att_near, out_near = tie(
+        mlp_got, fc1_grad, hidden_grad, fc2_sum, att_near, out_near
+    )
+    fc1_sum = data_scatter(fc1_grad)
+    mlp_done = collect_middle(mlp_parts, mlp_got)
+    att_far, out_far = other_core(att_near), other_core(out_near)
     gains = (ln1_gain.astype(F32)[None, :], ln2_gain.astype(F32)[None, :])
     share_far, sums_far = shares(
         False, qkv_grad, qkv_mine, hidden_grad, fc1_mine, gains, normed, span
     )
-    mlp_got, share_far, hidden_grad = tie(mlp_got, share_far, hidden_grad)
-    mlp_done = collect_middle(mlp_parts, mlp_got)
+    mlp_done, share_far, att_far, out_far, fc2_sum = tie(
+        mlp_done, share_far, att_far, out_far, fc2_sum
+    )
     share_got = other_core(share_far)
-    fc1_low, fc1_high = halves_product(mlp_in, hidden_grad)
-    mlp_done, share_got, fc1_low, fc1_high, hidden_grad, fc2_sum = tie(
-        mlp_done, share_got, fc1_low, fc1_high, hidden_grad, fc2_sum
-    )
-    low_sum = data_scatter(fc1_low)
-    high_sum = data_scatter(fc1_high)
     fc2_moved = gather_start(fc2_sum)
     *share_parts, sums_near = shares(
         True, qkv_grad, qkv_mine, hidden_grad, fc1_mine, gains, normed, span, share_got
     )
-    fc2_moved, share_parts, att_moved = tie(fc2_moved, share_parts, att_moved)
+    fc2_moved, share_parts, att_far, out_far = tie(fc2_moved, share_parts, att_far, out_far)
     share_got = collect_start(*share_parts)
     fc2_moved = gather_middle(*fc2_moved)
-    place_list = jnp.stack(places).astype(jnp.int32)
-    qkv_out, out_out = spread_columns(*gather_end(*att_moved), place_list, (3, 1))
+    attn_out = columns_product(own_context, out_near, out_far, place_list) + out_bias
+    qkv_out, out_out = spread_columns(att_near, att_far, place_list, (3, 1))
     mlp_out = collect_end(*mlp_done) + fc2_bias
     own_float = own_in.astype(F32)
     block_out = (own_float + attn_out + mlp_out).astype(BF).reshape(block_in.shape)
@@ -892,18 +912,16 @@
     )
     sizes = [term.shape[0] for term in terms]
     vector = jnp.concatenate(terms + (jnp.zeros((-sum(sizes) % 1024,), F32),)).reshape(-1, 128)
+    share_got, fc2_moved, vector, block_out, qkv_out, out_out, fc1_sum = tie(
+        share_got, fc2_moved, vector, block_out, qkv_out, out_out, fc1_sum
+    )
+    share_done = collect_middle(share_parts, share_got)
+    fc1_moved = gather_start(fc1_sum)
     vector = sum_move(vector, moves[0])
-
-    share_got, fc2_moved, vector, low_sum, qkv_out, out_out = tie(
-        share_got, fc2_moved, vector, low_sum, qkv_out, out_out
-    )
-    share_done = collect_middle(share_parts, share_got)
-    low_moved = gather_start(low_sum)
-    fc2_moved = gather_end(*fc2_moved)
-    vector = sum_move(vector, moves[1])
-    share_done, fc2_moved, vector, low_moved, high_sum = tie(
-        share_done, fc2_moved, vector, low_moved, high_sum
-    )
+    share_done, fc1_moved, vector, fc2_moved = tie(share_done, fc1_moved, vector, fc2_moved)
+    fc1_moved = gather_middle(*fc1_moved)
+    fc2_near, fc2_far = gather_end(*fc2_moved)
+    vector = sum_move(sum_move(vector, moves[1]), moves[2])
 
     share = collect_end(*share_done)
     own_centred = own_float - jnp.mean(own_float, axis=-1, keepdims=True)
@@ -916,22 +934,17 @@
     )
     input_grad = (own_up.astype(F32) + share).astype(BF).reshape(block_in.shape)
 
-    low_moved = gather_middle(*low_moved)
-    high_moved = gather_start(high_sum)
-    vector = sum_move(vector, moves[2])
-    [fc2_out] = spread_columns(*fc2_moved, place_list, (1,))
-    low_moved, high_moved, vector, fc2_out, input_grad = tie(
-        low_moved, high_moved, vector, fc2_out, input_grad
-    )
-    low_moved = gather_end(*low_moved)
-    high_moved = gather_middle(*high_moved)
-    vector = sum_move(vector, moves[3])
-    low_moved, high_moved, vector = tie(low_moved, high_moved, vector)
-    high_moved = gather_end(*high_moved)
-    for move in moves[4:]:
+    fc1_moved, vector, fc2_near, fc2_far, input_grad = tie(
+        fc1_moved, vector, fc2_near, fc2_far, input_grad
+    )
+    fc1_near, fc1_far = gather_end(*fc1_moved)
+    fc2_out = place_blocks(fc2_near, place_list[:head_count])
+    fc2_out = place_blocks(fc2_far, place_list[head_count:], fc2_out)
+    fc1_out = place_blocks(fc1_near, place_list[:head_count])
+    for move in moves[3:]:
         vector = sum_move(vector, move)
-    fc1_begun = spread_half(*low_moved, place_list, 0, 0)
-    fc1_out = spread_half(*high_moved, place_list, 1, 0, fc1_begun)
+    fc1_far, fc1_out, fc2_out, vector = tie(fc1_far, fc1_out, fc2_out, vector)
+    fc1_out = place_blocks(fc1_far, place_list[head_count:], fc1_out)
     reduced = [
         vector.reshape(-1)[sum(sizes[:i]) : sum(sizes[: i + 1])] for i in range(len(sizes))
     ]

time: 646 us -> 620 us (0.960)
  local copies, waits for them, and re-layouts: 98.3 us -> 68.1 us
  Pallas kernels: 218 us -> 242 us
  matrix products: 10.2 us -> 0 us
    pallas_call x3 -> x11, Pallas kernels: 23.3 us -> 46.6 us  [the longest x6 19.2 us: join(): pl.pallas_call(join_kernel, grid=(4,), in_specs=[whole(piece) for piece i...]
    ppermute x36 -> x32, waiting for transfers between devices: 102 us -> 87 us  [across(): return lax.ppermute(values, 'head', [(i, i ^ offset) for i in range(count)])]
    pallas_call x4 -> x5, Pallas kernels: 38.6 us -> 51.5 us  [product(): pl.pallas_call(kernel, grid=(rows // tile,), in_specs=[left_spec, whole(t...]
    unnamed x160 -> x176, local copies, waits for them, and re-layouts: 49.2 us -> 36.7 us
    pallas_call x2 -> x1, Pallas kernels: 21.8 us -> 9.71 us  [spread_columns(): pl.pallas_call(functools.partial(spread_kernel, parts), grid_spec=pltpu.P...]
    all_gather x2 -> x3, waiting for transfers between devices: 0.02 us -> 11.1 us  [data_gather(): return lax.all_gather(own, 'dp', axis=0, tiled=True)]
    dot_general x8 -> x0, matrix products: 10.2 us -> none  [body(): jnp.dot(own_context, pieces[index * width:(index + 1) * width], preferred...]
    ppermute x4, waiting for transfers between devices: 12.1 us -> 20.4 us  [hop_up(): return lax.ppermute(values, 'dp', [(0, 1), (1, 2), (2, 3)])]
  transfers between devices with their start and end apart: 65 -> 60, of which waited for: 32 -> 27; matrix products, arithmetic and copies ran while one was open for 17% -> 11% of each run, Pallas kernels for 32% -> 37%
where the time goes in v3:
time: 620 us; the launch traced here: 612 us
  Pallas kernels  242 us (39%)
  waiting for transfers between devices  150 us (24%)
  local copies, waits for them, and re-layouts  68.1 us (11%)
  starting transfers between devices  65.9 us (11%)
  other arithmetic  53.1 us (9%)
  blocking collectives  18.2 us (3%)
  between operations  15.4 us (2%)
    ppermute x32, waiting for transfers between devices, across(): return lax.ppermute(values, 'head', [(i, i ^ offset) for i in range(count)])  87 us
    pallas_call x5, Pallas kernels, product(): pl.pallas_call(kernel, grid=(rows // tile,), in_specs=[left_spec, whole(t...  51.5 us
    pallas_call x2, Pallas kernels, shares(): pl.pallas_call(functools.partial(share_kernel, near), grid=(steps,), in_s...  37.8 us
    unnamed x176, local copies, waits for them, and re-layouts  36.7 us
    ppermute x32, starting transfers between devices, across(): return lax.ppermute(values, 'head', [(i, i ^ offset) for i in range(count)])  35.3 us
    pallas_call x1, Pallas kernels, attention(): pl.pallas_call(attention_kernel, grid_spec=pltpu.PrefetchScalarGridSpec(n...  29.5 us
    ppermute x4, waiting for transfers between devices, hop_up(): return lax.ppermute(values, 'dp', [(0, 1), (1, 2), (2, 3)])  20.4 us
    pallas_call x6, Pallas kernels, join(): pl.pallas_call(join_kernel, grid=(4,), in_specs=[whole(piece) for piece i...  19.2 us
  transfers between devices with their start and end apart: 60, of which 27 were waited for; matrix products, arithmetic and copies ran while one was open for 11% of the time, Pallas kernels for 37%

profile of v3, /device:TPU:0, one launch (start us, length us, event | category | flops | bytes accessed | tf_op | source)
XLA Modules:
  0.0 612.0 jit_solution(12735989487390230238)
XLA Ops:
  14.0 4.0 fusion.41
  19.1 16.7 %collective-permute-done.one = bf16[256,2048]{1,0:T(8,128)(2,1)S(1)} collective-permute-done((bf16[256,2048]{1,0:T(8,128)(2,1)}, bf16[256,2048]{1,0:T(8,128)(2,1)S(1)}, u32[]{:S(2)}, u32[]{:S(2)}) %collective-permute-start) | collective-permute-done | bytes 1048608 | tf_op jit(solution)/shard_map/ppermute | solution.py:28
  39.6 10.4 %collective-permute-done.2.low = bf16[128,2048]{1,0:T(8,128)(2,1)S(1)} collective-permute-done((bf16[128,2048]{1,0:T(8,128)(2,1)S(1)}, bf16[128,2048]{1,0:T(8,128)(2,1)S(1)}, u32[]{:S(2)}, u32[]{:S(2)}) %collective-permute-start.2) | collective-permute-done | bytes 524320 | tf_op jit(solution)/shard_map/ppermute | solution.py:28
  62.3 3.7 fusion.32
  69.0 14.2 %norms.1 = (bf16[2048,2048]{1,0:T(8,128)(2,1)}, bf16[2048,2048]{1,0:T(8,128)(2,1)}, bf16[2048,2048]{1,0:T(8,128)(2,1)}) custom-call(bf16[1024,2048]{1,0:T(8,128)(2,1)S(1)} %copy-done.10, bf16[1024,2048]{1,0:T(8,128)(2,1)} %collective-permute-done.6.far, f32[1,2048]{1,0:T(1,128)S(1)} %bitcast.121, f32[1,2048]{1,0:T(1,128)S(1)} %bitcast.127, ...), custom_call_target="tpu_custom_call" | custom-call | flops 1000000000 | bytes 1000000 | tf_op jit(solution)/shard_map/norms/pallas_call | solution.py:420
  87.9 9.5 %collective-permute-done.7.low = bf16[128,2048]{1,0:T(8,128)(2,1)S(1)} collective-permute-done((bf16[128,2048]{1,0:T(8,128)(2,1)S(1)}, bf16[128,2048]{1,0:T(8,128)(2,1)S(1)}, u32[]{:S(2)}, u32[]{:S(2)}) %collective-permute-start.7) | collective-permute-done | bytes 524320 | tf_op jit(solution)/shard_map/ppermute | solution.py:28
  99.4 3.7 join.7
  103.1 3.8 all-to-all-start
  107.8 11.1 %all-gather.8.cloned.1.call-done.right.qkv_weight = bf16[2048,768]{1,0:T(8,128)(2,1)} async-done(((bf16[512,768]{1,0:T(8,128)(2,1)}), bf16[2048,768]{1,0:T(8,128)(2,1)}) %all-gather.8.cloned.1.call-update) | async-done | bytes 3145744 | tf_op jit(solution)/shard_map/all_gather | solution.py:55
  120.7 10.6 %product.5 = f32[2048,768]{1,0:T(8,128)} custom-call(bf16[2048,2048]{1,0:T(8,128)(2,1)} %get-tuple-element.203.left, bf16[2048,768]{1,0:T(8,128)(2,1)S(1)} %copy-done.5), custom_call_target="tpu_custom_call" | custom-call | flops 1000000000 | bytes 1000000 | tf_op jit(solution)/shard_map/product/pallas_call | solution.py:171
  136.5 3.3 copy-done.53
  139.9 5.8 product.6
  145.7 29.5 %attention.1 = (bf16[8,256,256]{2,1,0:T(8,128)(2,1)S(1)}, bf16[8,256,256]{2,1,0:T(8,128)(2,1)S(1)}, bf16[8,256,768]{2,1,0:T(8,128)(2,1)}) custom-call(s32[8]{0:T(128)S(1)} %get-tuple-element.401.order, s32[8]{0:T(128)S(1)} %get-tuple-element.400.first, f32[8,256,768]{2,1,0:T(8,128)} %bitcast.131, f32[1,768]{1,0:T(1,128)S(1)} %maximum_convert_fusion.bias, ...), custom_call_target="tpu_custom_call" | custom-call | flops 1000000000 | bytes 1000000 | tf_op jit(solution)/shard_map/attention/pallas_call | solution.py:660
  175.1 6.0 wide.1
  182.2 3.6 all-to-all-start.1
  187.2 10.3 %product.7 = bf16[2048,768]{1,0:T(8,128)(2,1)S(1)} custom-call(bf16[2048,2048]{1,0:T(8,128)(2,1)} %get-tuple-element.203.left, bf16[2048,768]{1,0:T(8,128)(2,1)} %bitcast.100), custom_call_target="tpu_custom_call" | custom-call | flops 1000000000 | bytes 1000000 | tf_op jit(solution)/shard_map/product/pallas_call | solution.py:171
  201.2 4.5 pad_maximum_fusion
  205.7 3.0 slice_select_fusion
  214.5 16.2 %hidden.1 = (bf16[2048,1024]{1,0:T(8,128)(2,1)S(1)}, bf16[2048,1024]{1,0:T(8,128)(2,1)}) custom-call(bf16[2048,2048]{1,0:T(8,128)(2,1)} %get-tuple-element.219.tokens.left, bf16[2048,1024]{1,0:T(8,128)(2,1)} %all-gather.4.cloned.1.call-done.weight, f32[1,1024]{1,0:T(1,128)S(1)} %bitcast.129), custom_call_target="tpu_custom_call" | custom-call | flops 1000000000 | bytes 1000000 | tf_op jit(solution)/shard_map/hidden/pallas_call | solution.py:213
  231.5 5.2 collective-permute-done.11
  238.2 5.4 fusion.24
  243.6 5.2 collective-permute-start.14
  254.2 12.3 %product.8 = bf16[2048,1024]{1,0:T(8,128)(2,1)S(1)} custom-call(bf16[2048,2048]{1,0:T(8,128)(2,1)} %copy-done.53, bf16[2048,1024]{1,0:T(8,128)(2,1)} %copy-done.3), custom_call_target="tpu_custom_call" | custom-call | flops 1000000000 | bytes 1000000 | tf_op jit(solution)/shard_map/product/pallas_call | solution.py:171
  269.4 5.1 collective-permute-done.15
  274.5 5.4 fusion.22
  283.0 18.2 %all_to_all.54 = bf16[8,256,256]{2,1,0:T(8,128)(2,1)S(1)} all-to-all(bf16[8,256,256]{2,1,0:T(8,128)(2,1)S(1)} %copy-done.43), channel_id=1, replica_groups=mesh['dp'=4,'head'=4,'blk'=2] {'head','blk'}, dimensions={0} | all-to-all | bytes 2097152 | tf_op jit(solution)/shard_map/all_to_all | solution.py:842
  302.3 3.7 collective-permute-done.19
  311.2 18.7 %collective-permute-done.20 = bf16[512,1024]{1,0:T(8,128)(2,1)S(1)} collective-permute-done((bf16[512,1024]{1,0:T(8,128)(2,1)S(1)}, bf16[512,1024]{1,0:T(8,128)(2,1)S(1)}, u32[]{:S(2)}, u32[]{:S(2)}) %collective-permute-start.20) | collective-permute-done | bytes 1048608 | tf_op jit(solution)/shard_map/ppermute | solution.py:63
  330.0 4.2 collective-permute-done.21
  335.1 3.7 add_convert_fusion.own
  349.8 7.3 %far.1 = bf16[1024,2048]{1,0:T(8,128)(2,1)S(1)} custom-call(bf16[2048,1024]{1,0:T(8,128)(2,1)} %copy-done.3, bf16[2048,1024]{1,0:T(8,128)(2,1)} %copy-done.54), custom_call_target="tpu_custom_call" | custom-call | flops 1000000000 | bytes 1000000 | tf_op jit(solution)/shard_map/far/pallas_call | solution.py:305
  359.2 13.2 %hidden_grad.1 = (bf16[2048,1024]{1,0:T(8,128)(2,1)S(1)}, f32[1,1024]{1,0:T(1,128)S(1)}) custom-call(bf16[2048,2048]{1,0:T(8,128)(2,1)} %copy-done.53, bf16[2048,1024]{1,0:T(8,128)(2,1)} %copy-done.54, bf16[2048,1024]{1,0:T(8,128)(2,1)} %get-tuple-element.256.slope), custom_call_target="tpu_custom_call" | custom-call | flops 1000000000 | bytes 1000000 | tf_op jit(solution)/shard_map/hidden_grad/pallas_call | solution.py:241
  374.4 8.4 %collective-permute-done.22.one = bf16[512,1024]{1,0:T(8,128)(2,1)S(1)} collective-permute-done((bf16[512,1024]{1,0:T(8,128)(2,1)S(1)}, bf16[512,1024]{1,0:T(8,128)(2,1)S(1)}, u32[]{:S(2)}, u32[]{:S(2)}) %collective-permute-start.22) | collective-permute-done | bytes 1048608 | tf_op jit(solution)/shard_map/ppermute | solution.py:28
  385.5 9.9 %near.1 = (bf16[2,256,1024]{2,1,0:T(8,128)(2,1)S(1)}, bf16[2,256,1024]{2,1,0:T(8,128)(2,1)}, bf16[2,256,1024]{2,1,0:T(8,128)(2,1)S(1)}, bf16[2,256,1024]{2,1,0:T(8,128)(2,1)}) custom-call(bf16[2048,1024]{1,0:T(8,128)(2,1)} %copy-done.3, bf16[2048,1024]{1,0:T(8,128)(2,1)} %copy-done.54, bf16[1024,2048]{1,0:T(8,128)(2,1)} %collective-permute-done.24.more), custom_call_target="tpu_custom_call" | custom-call | flops 1000000000 | bytes 1000000 | tf_op jit(solution)/shard_map/near/pallas_call | solution.py:328
  400.1 4.0 join.9.near
  404.2 12.5 %product.9 = bf16[2048,1024]{1,0:T(8,128)(2,1)S(1)} custom-call(bf16[2048,2048]{1,0:T(8,128)(2,1)} %get-tuple-element.219.tokens.left, bf16[2048,1024]{1,0:T(8,128)(2,1)} %copy-done.4), custom_call_target="tpu_custom_call" | custom-call | flops 1000000000 | bytes 1000000 | tf_op jit(solution)/shard_map/product/pallas_call | solution.py:171
  432.0 16.9 %share_far.1 = (bf16[1024,2048]{1,0:T(8,128)(2,1)}, f32[8,2048]{1,0:T(8,128)S(1)}) custom-call(bf16[2048,768]{1,0:T(8,128)(2,1)S(1)} %bitcast.102, bf16[2048,768]{1,0:T(8,128)(2,1)} %all-gather.8.cloned.1.call-done.right.qkv_weight, bf16[2048,1024]{1,0:T(8,128)(2,1)} %copy-done.4, bf16[2048,1024]{1,0:T(8,128)(2,1)} %all-gather.4.cloned.1.call-done.weight, ...), custom_call_target="tpu_custom_call" | custom-call | flops 1000000000 | bytes 1000000 | tf_op jit(solution)/shard_map/share_far/pallas_call | solution.py:374
  458.8 20.9 %share_near.1 = (bf16[2,256,1024]{2,1,0:T(8,128)(2,1)S(1)}, bf16[2,256,1024]{2,1,0:T(8,128)(2,1)}, bf16[2,256,1024]{2,1,0:T(8,128)(2,1)S(1)}, bf16[2,256,1024]{2,1,0:T(8,128)(2,1)}, f32[8,2048]{1,0:T(8,128)S(1)}) custom-call(bf16[2048,768]{1,0:T(8,128)(2,1)} %bitcast.101, bf16[2048,768]{1,0:T(8,128)(2,1)} %all-gather.8.cloned.1.call-done.right.qkv_weight, ...), custom_call_target="tpu_custom_call" | custom-call | flops 1000000000 | bytes 1000000 | tf_op jit(solution)/shard_map/share_near/pallas_call | solution.py:374
  485.6 8.3 %columns.1 = f32[256,2048]{1,0:T(8,128)S(1)} custom-call(s32[8]{0:T(128)S(1)} %stack.68.places, bf16[256,2048]{1,0:T(8,128)(2,1)S(1)} %bitcast.117, bf16[8192,256]{1,0:T(8,128)(2,1)} %join.9.near, bf16[8192,256]{1,0:T(8,128)(2,1)} %collective-permute-done.32.far), custom_call_target="tpu_custom_call" | custom-call | flops 1000000000 | bytes 1000000 | tf_op jit(solution)/shard_map/columns/pallas_call | solution.py:478
  500.3 9.7 %spread.1 = (f32[512,6144]{1,0:T(8,128)}, f32[512,2048]{1,0:T(8,128)}) custom-call(s32[8]{0:T(128)S(1)} %stack.68.places, bf16[4,512,1024]{2,1,0:T(8,128)(2,1)S(1)} %bitcast.110, bf16[4,512,1024]{2,1,0:T(8,128)(2,1)} %bitcast.43.far), custom_call_target="tpu_custom_call" | custom-call | flops 1000000000 | bytes 1000000 | tf_op jit(solution)/shard_map/spread/pallas_call | solution.py:520
  510.8 6.4 %collective-permute-done.38.low = bf16[256,1024]{1,0:T(8,128)(2,1)} collective-permute-done((bf16[256,1024]{1,0:T(8,128)(2,1)}, bf16[256,1024]{1,0:T(8,128)(2,1)}, u32[]{:S(2)}, u32[]{:S(2)}) %collective-permute-start.38) | collective-permute-done | bytes 524320 | tf_op jit(solution)/shard_map/ppermute | solution.py:28
  526.4 26.3 %collective-permute-done.41 = bf16[256,1024]{1,0:T(8,128)(2,1)S(1)} collective-permute-done((bf16[256,1024]{1,0:T(8,128)(2,1)S(1)}, bf16[256,1024]{1,0:T(8,128)(2,1)S(1)}, u32[]{:S(2)}, u32[]{:S(2)}) %collective-permute-start.41) | collective-permute-done | bytes 524320 | tf_op jit(solution)/shard_map/ppermute | solution.py:28
  554.4 4.2 join.10.blocks
  567.6 8.3 %collective-permute-done.48 = f32[200,128]{1,0:T(8,128)S(1)} collective-permute-done((f32[200,128]{1,0:T(8,128)S(1)}, f32[200,128]{1,0:T(8,128)S(1)}, u32[]{:S(2)}, u32[]{:S(2)}) %collective-permute-start.48) | collective-permute-done | bytes 102432 | tf_op jit(solution)/shard_map/ppermute | solution.py:153
  583.0 4.2 place.4.rest_0_
  587.3 4.2 place.5.rest_0_
  591.5 4.2 place.6
  598.1 6.6 %place.7 = f32[512,8192]{1,0:T(8,128)} custom-call(s32[4]{0:T(128)S(1)} %pad_add_fusion.2.places, bf16[2048,1024]{1,0:T(8,128)(2,1)} %collective-permute-done.50.blocks, f32[512,8192]{1,0:T(8,128)} %place.4.rest_0_), custom_call_target="tpu_custom_call", output_to_operand_aliasing={{}: (2, {})} | custom-call | flops 1000000000 | bytes 1000000 | tf_op jit(solution)/shard_map/place/pallas_call | solution.py:543
  (389 shorter events, 164.6 us)
Async XLA Ops:
  7.2 76.0 %all-gather.6.cloned.1.call-start = ((), (), s32[]{:S(2)}) async-start(), calls=%async_computation.6 | async-start | bytes 1310720 | tf_op jit(solution)/shard_map/all_gather | solution.py:55
  9.5 26.3 %collective-permute-start = (bf16[256,2048]{1,0:T(8,128)(2,1)}, bf16[256,2048]{1,0:T(8,128)(2,1)S(1)}, u32[]{:S(2)}, u32[]{:S(2)}) collective-permute-start(bf16[256,2048]{1,0:T(8,128)(2,1)} %bitcast.103), channel_id=1, source_target_pairs={{0,2},{2,0},{4,6},{6,4},{1,3},{3,1},{5,7},{7,5},{8,10},{10,8},{12,... | collective-permute-start | bytes 3145736 | tf_op jit(solution)/shard_map/ppermute | solution.py:28
  12.4 24.8 %collective-permute-start.1 = (bf16[256,2048]{1,0:T(8,128)(2,1)}, bf16[256,2048]{1,0:T(8,128)(2,1)S(1)}, u32[]{:S(2)}, u32[]{:S(2)}) collective-permute-start(bf16[256,2048]{1,0:T(8,128)(2,1)} %bitcast.104), channel_id=1, source_target_pairs={{0,4},{2,6},{4,0},{6,2},{1,5},{3,7},{5,1},{7,3},{8,12},{10,14},{12... | collective-permute-start | bytes 3145736 | tf_op jit(solution)/shard_map/ppermute | solution.py:28
  14.0 104.8 %all-gather.8.cloned.1.call-start = ((), (), s32[]{:S(2)}) async-start(), calls=%async_computation.7 | async-start | bytes 3932160 | tf_op jit(solution)/shard_map/all_gather | solution.py:55
  55.1 150.6 %all-gather.4.cloned.1.call-start = ((), (), s32[]{:S(2)}) async-start(), calls=%async_computation.5 | async-start | bytes 5242880 | tf_op jit(solution)/shard_map/all_gather | solution.py:55
  58.0 25.6 %collective-permute-start.4 = (bf16[256,2048]{1,0:T(8,128)(2,1)S(1)}, bf16[256,2048]{1,0:T(8,128)(2,1)S(1)}, u32[]{:S(2)}, u32[]{:S(2)}) collective-permute-start(bf16[256,2048]{1,0:T(8,128)(2,1)S(1)} %bitcast.111), channel_id=1, source_target_pairs={{0,2},{2,0},{4,6},{6,4},{1,3},{3,1},{5,7},{7,5},{8,10},{10,8},{12,... | collective-permute-start | bytes 3145736 | tf_op jit(solution)/shard_map/ppermute | solution.py:28
  58.6 25.4 %collective-permute-start.5 = (bf16[256,2048]{1,0:T(8,128)(2,1)S(1)}, bf16[256,2048]{1,0:T(8,128)(2,1)}, u32[]{:S(2)}, u32[]{:S(2)}) collective-permute-start(bf16[256,2048]{1,0:T(8,128)(2,1)S(1)} %bitcast.112), channel_id=1, source_target_pairs={{0,4},{2,6},{4,0},{6,2},{1,5},{3,7},{5,1},{7,3},{8,12},{10,14},{12... | collective-permute-start | bytes 3145736 | tf_op jit(solution)/shard_map/ppermute | solution.py:28
  103.0 28.4 %collective-permute-start.9 = (bf16[1024,2048]{1,0:T(8,128)(2,1)}, bf16[1024,2048]{1,0:T(8,128)(2,1)}, u32[]{:S(2)}, u32[]{:S(2)}) collective-permute-start(bf16[1024,2048]{1,0:T(8,128)(2,1)} %join.7), channel_id=1, source_target_pairs={{0,1},{1,0},{2,3},{3,2},{4,5},{5,4},{6,7},{7,6},{8,9},{9,8},{10,11... | collective-permute-start | bytes 12582920 | tf_op jit(solution)/shard_map/ppermute | solution.py:32
  103.1 28.3 %all-to-all-start = ((bf16[8,256,256]{2,1,0:T(8,128)(2,1)}), bf16[8,256,256]{2,1,0:T(8,128)(2,1)S(1)}, u32[]{:S(2)}, u32[]{:S(2)}) async-start(bf16[8,256,256]{2,1,0:T(8,128)(2,1)} %bitcast.17), calls=%async_computation | async-start | bytes 2097152 | tf_op jit(solution)/shard_map/all_to_all | solution.py:785
  182.2 19.0 %all-to-all-start.1 = ((bf16[256,8,256]{2,0,1:T(8,128)(2,1)}), bf16[256,8,256]{2,0,1:T(8,128)(2,1)S(1)}, u32[]{:S(2)}, u32[]{:S(2)}) async-start(bf16[256,8,256]{2,0,1:T(8,128)(2,1)} %bitcast.97), calls=%async_computation.1 | async-start | bytes 2097152 | tf_op jit(solution)/shard_map/all_to_all | solution.py:815
  185.8 238.7 %reduce-scatter.3.cloned.1.call-start = ((), (), s32[]{:S(2)}) async-start(), calls=%async_computation.8 | async-start | bytes 5242880 | tf_op jit(solution)/shard_map/reduce_scatter | solution.py:59
  208.7 22.9 %collective-permute-start.10 = (bf16[512,1024]{1,0:T(8,128)(2,1)}, bf16[512,1024]{1,0:T(8,128)(2,1)}, u32[]{:S(2)}, u32[]{:S(2)}) collective-permute-start(bf16[512,1024]{1,0:T(8,128)(2,1)} %get-tuple-element.374), channel_id=1, source_target_pairs={{0,8},{8,16},{16,24},{1,9},{9,17},{17,25},{2,10},{10,18},{18,26},{... | collective-permute-start | bytes 3145736 | tf_op jit(solution)/shard_map/ppermute | solution.py:63
  211.0 25.7 %collective-permute-start.11 = (bf16[512,1024]{1,0:T(8,128)(2,1)}, bf16[512,1024]{1,0:T(8,128)(2,1)}, u32[]{:S(2)}, u32[]{:S(2)}) collective-permute-start(bf16[512,1024]{1,0:T(8,128)(2,1)} %get-tuple-element.373), channel_id=1, source_target_pairs={{24,16},{16,8},{8,0},{25,17},{17,9},{9,1},{26,18},{18,10},{10,2},{... | collective-permute-start | bytes 3145736 | tf_op jit(solution)/shard_map/ppermute | solution.py:67
  212.3 24.4 %collective-permute-start.12 = (bf16[2048,256]{1,0:T(8,128)(2,1)}, bf16[2048,256]{1,0:T(8,128)(2,1)S(1)}, u32[]{:S(2)}, u32[]{:S(2)}) collective-permute-start(bf16[2048,256]{1,0:T(8,128)(2,1)} %all-gather.6.cloned.1.call-done.own), channel_id=1, source_target_pairs={{0,2},{2,0},{4,6},{6,4},{1,3},{3,1},{5,7},{7,5},{8,10},{10,8},{12,... | collective-permute-start | bytes 3145736 | tf_op jit(solution)/shard_map/ppermute | solution.py:28
  212.9 25.3 %collective-permute-start.13 = (bf16[2048,256]{1,0:T(8,128)(2,1)}, bf16[2048,256]{1,0:T(8,128)(2,1)}, u32[]{:S(2)}, u32[]{:S(2)}) collective-permute-start(bf16[2048,256]{1,0:T(8,128)(2,1)} %all-gather.6.cloned.1.call-done.own), channel_id=1, source_target_pairs={{0,4},{2,6},{4,0},{6,2},{1,5},{3,7},{5,1},{7,3},{8,12},{10,14},{12... | collective-permute-start | bytes 3145736 | tf_op jit(solution)/shard_map/ppermute | solution.py:28
  243.6 25.8 %collective-permute-start.14 = (bf16[512,1024]{1,0:T(8,128)(2,1)}, bf16[512,1024]{1,0:T(8,128)(2,1)}, u32[]{:S(2)}, u32[]{:S(2)}) collective-permute-start(bf16[512,1024]{1,0:T(8,128)(2,1)} %get-tuple-element.372), channel_id=1, source_target_pairs={{0,8},{8,16},{16,24},{1,9},{9,17},{17,25},{2,10},{10,18},{18,26},{... | collective-permute-start | bytes 3145736 | tf_op jit(solution)/shard_map/ppermute | solution.py:63
  248.8 25.7 %collective-permute-start.15 = (bf16[512,1024]{1,0:T(8,128)(2,1)}, bf16[512,1024]{1,0:T(8,128)(2,1)}, u32[]{:S(2)}, u32[]{:S(2)}) collective-permute-start(bf16[512,1024]{1,0:T(8,128)(2,1)} %get-tuple-element.371), channel_id=1, source_target_pairs={{24,16},{16,8},{8,0},{25,17},{17,9},{9,1},{26,18},{18,10},{10,2},{... | collective-permute-start | bytes 3145736 | tf_op jit(solution)/shard_map/ppermute | solution.py:67
  250.9 17.7 %collective-permute-start.16 = (bf16[1024,256]{1,0:T(8,128)(2,1)}, bf16[1024,256]{1,0:T(8,128)(2,1)S(1)}, u32[]{:S(2)}, u32[]{:S(2)}) collective-permute-start(bf16[1024,256]{1,0:T(8,128)(2,1)} %slice.190), channel_id=1, source_target_pairs={{0,4},{2,6},{4,0},{6,2},{1,5},{3,7},{5,1},{7,3},{8,12},{10,14},{12... | collective-permute-start | bytes 1572872 | tf_op jit(solution)/shard_map/ppermute | solution.py:28
  253.7 15.0 %collective-permute-start.17 = (bf16[1024,256]{1,0:T(8,128)(2,1)}, bf16[1024,256]{1,0:T(8,128)(2,1)S(1)}, u32[]{:S(2)}, u32[]{:S(2)}) collective-permute-start(bf16[1024,256]{1,0:T(8,128)(2,1)} %slice.191), channel_id=1, source_target_pairs={{0,2},{2,0},{4,6},{6,4},{1,3},{3,1},{5,7},{7,5},{8,10},{10,8},{12,... | collective-permute-start | bytes 1572872 | tf_op jit(solution)/shard_map/ppermute | solution.py:28
  279.9 22.4 %collective-permute-start.18 = (bf16[512,1024]{1,0:T(8,128)(2,1)S(1)}, bf16[512,1024]{1,0:T(8,128)(2,1)S(1)}, u32[]{:S(2)}, u32[]{:S(2)}) collective-permute-start(bf16[512,1024]{1,0:T(8,128)(2,1)S(1)} %get-tuple-element.378), channel_id=1, source_target_pairs={{0,8},{8,16},{16,24},{1,9},{9,17},{17,25},{2,10},{10,18},{18,26},{... | collective-permute-start | bytes 3145736 | tf_op jit(solution)/shard_map/ppermute | solution.py:63
  281.4 24.6 %collective-permute-start.19 = (bf16[512,1024]{1,0:T(8,128)(2,1)S(1)}, bf16[512,1024]{1,0:T(8,128)(2,1)S(1)}, u32[]{:S(2)}, u32[]{:S(2)}) collective-permute-start(bf16[512,1024]{1,0:T(8,128)(2,1)S(1)} %get-tuple-element.377), channel_id=1, source_target_pairs={{24,16},{16,8},{8,0},{25,17},{17,9},{9,1},{26,18},{18,10},{10,2},{... | collective-permute-start | bytes 3145736 | tf_op jit(solution)/shard_map/ppermute | solution.py:67
  307.1 22.9 %collective-permute-start.20 = (bf16[512,1024]{1,0:T(8,128)(2,1)S(1)}, bf16[512,1024]{1,0:T(8,128)(2,1)S(1)}, u32[]{:S(2)}, u32[]{:S(2)}) collective-permute-start(bf16[512,1024]{1,0:T(8,128)(2,1)S(1)} %get-tuple-element.376), channel_id=1, source_target_pairs={{0,8},{8,16},{16,24},{1,9},{9,17},{17,25},{2,10},{10,18},{18,26},{... | collective-permute-start | bytes 3145736 | tf_op jit(solution)/shard_map/ppermute | solution.py:63
  309.9 24.2 %collective-permute-start.21 = (bf16[512,1024]{1,0:T(8,128)(2,1)S(1)}, bf16[512,1024]{1,0:T(8,128)(2,1)S(1)}, u32[]{:S(2)}, u32[]{:S(2)}) collective-permute-start(bf16[512,1024]{1,0:T(8,128)(2,1)S(1)} %get-tuple-element.375), channel_id=1, source_target_pairs={{24,16},{16,8},{8,0},{25,17},{17,9},{9,1},{26,18},{18,10},{10,2},{... | collective-permute-start | bytes 3145736 | tf_op jit(solution)/shard_map/ppermute | solution.py:67
  335.1 175.7 %reduce-scatter.5.cloned.1.call-start = ((), (), s32[]{:S(2)}) async-start(), calls=%async_computation.9 | async-start | bytes 5242880 | tf_op jit(solution)/shard_map/reduce_scatter | solution.py:59
  357.1 26.7 %collective-permute-start.24 = (bf16[1024,2048]{1,0:T(8,128)(2,1)S(1)}, bf16[1024,2048]{1,0:T(8,128)(2,1)}, u32[]{:S(2)}, u32[]{:S(2)}) collective-permute-start(bf16[1024,2048]{1,0:T(8,128)(2,1)S(1)} %far.1), channel_id=1, source_target_pairs={{0,1},{1,0},{2,3},{3,2},{4,5},{5,4},{6,7},{7,6},{8,9},{9,8},{10,11... | collective-permute-start | bytes 12582920 | tf_op jit(solution)/shard_map/ppermute | solution.py:32
  357.2 25.6 %collective-permute-start.22 = (bf16[512,1024]{1,0:T(8,128)(2,1)S(1)}, bf16[512,1024]{1,0:T(8,128)(2,1)S(1)}, u32[]{:S(2)}, u32[]{:S(2)}) collective-permute-start(bf16[512,1024]{1,0:T(8,128)(2,1)S(1)} %add_convert_fusion.own), channel_id=1, source_target_pairs={{0,2},{2,0},{4,6},{6,4},{1,3},{3,1},{5,7},{7,5},{8,10},{10,8},{12,... | collective-permute-start | bytes 3145736 | tf_op jit(solution)/shard_map/ppermute | solution.py:28
  358.6 25.2 %collective-permute-start.23 = (bf16[512,1024]{1,0:T(8,128)(2,1)S(1)}, bf16[512,1024]{1,0:T(8,128)(2,1)S(1)}, u32[]{:S(2)}, u32[]{:S(2)}) collective-permute-start(bf16[512,1024]{1,0:T(8,128)(2,1)S(1)} %add_convert_fusion.own), channel_id=1, source_target_pairs={{0,4},{2,6},{4,0},{6,2},{1,5},{3,7},{5,1},{7,3},{8,12},{10,14},{12... | collective-permute-start | bytes 3145736 | tf_op jit(solution)/shard_map/ppermute | solution.py:28
  383.9 13.5 %collective-permute-start.25 = (bf16[256,1024]{1,0:T(8,128)(2,1)S(1)}, bf16[256,1024]{1,0:T(8,128)(2,1)S(1)}, u32[]{:S(2)}, u32[]{:S(2)}) collective-permute-start(bf16[256,1024]{1,0:T(8,128)(2,1)S(1)} %slice.192), channel_id=1, source_target_pairs={{0,4},{2,6},{4,0},{6,2},{1,5},{3,7},{5,1},{7,3},{8,12},{10,14},{12... | collective-permute-start | bytes 1572872 | tf_op jit(solution)/shard_map/ppermute | solution.py:28
  397.7 26.7 %collective-permute-start.27 = (bf16[2,256,1024]{2,1,0:T(8,128)(2,1)}, bf16[2,256,1024]{2,1,0:T(8,128)(2,1)}, u32[]{:S(2)}, u32[]{:S(2)}) collective-permute-start(bf16[2,256,1024]{2,1,0:T(8,128)(2,1)} %get-tuple-element.269), channel_id=1, source_target_pairs={{0,2},{2,0},{4,6},{6,4},{1,3},{3,1},{5,7},{7,5},{8,10},{10,8},{12,... | collective-permute-start | bytes 3145736 | tf_op jit(solution)/shard_map/ppermute | solution.py:28
  398.7 25.7 %collective-permute-start.28 = (bf16[2,256,1024]{2,1,0:T(8,128)(2,1)}, bf16[2,256,1024]{2,1,0:T(8,128)(2,1)}, u32[]{:S(2)}, u32[]{:S(2)}) collective-permute-start(bf16[2,256,1024]{2,1,0:T(8,128)(2,1)} %get-tuple-element.270), channel_id=1, source_target_pairs={{0,4},{2,6},{4,0},{6,2},{1,5},{3,7},{5,1},{7,3},{8,12},{10,14},{12... | collective-permute-start | bytes 3145736 | tf_op jit(solution)/shard_map/ppermute | solution.py:28
  424.4 26.7 %collective-permute-start.31 = (bf16[2048,1024]{1,0:T(8,128)(2,1)}, bf16[2048,1024]{1,0:T(8,128)(2,1)}, u32[]{:S(2)}, u32[]{:S(2)}) collective-permute-start(bf16[2048,1024]{1,0:T(8,128)(2,1)} %join.8), channel_id=1, source_target_pairs={{0,1},{1,0},{2,3},{3,2},{4,5},{5,4},{6,7},{7,6},{8,9},{9,8},{10,11... | collective-permute-start | bytes 12582920 | tf_op jit(solution)/shard_map/ppermute | solution.py:32
  424.5 26.7 %collective-permute-start.32 = (bf16[8192,256]{1,0:T(8,128)(2,1)}, bf16[8192,256]{1,0:T(8,128)(2,1)}, u32[]{:S(2)}, u32[]{:S(2)}) collective-permute-start(bf16[8192,256]{1,0:T(8,128)(2,1)} %join.9.near), channel_id=1, source_target_pairs={{0,1},{1,0},{2,3},{3,2},{4,5},{5,4},{6,7},{7,6},{8,9},{9,8},{10,11... | collective-permute-start | bytes 12582920 | tf_op jit(solution)/shard_map/ppermute | solution.py:32
  428.8 22.3 %collective-permute-start.30 = (bf16[256,1024]{1,0:T(8,128)(2,1)S(1)}, bf16[256,1024]{1,0:T(8,128)(2,1)S(1)}, u32[]{:S(2)}, u32[]{:S(2)}) collective-permute-start(bf16[256,1024]{1,0:T(8,128)(2,1)S(1)} %fusion.29), channel_id=1, source_target_pairs={{0,2},{2,0},{4,6},{6,4},{1,3},{3,1},{5,7},{7,5},{8,10},{10,8},{12,... | collective-permute-start | bytes 1572872 | tf_op jit(solution)/shard_map/ppermute | solution.py:28
  431.2 20.0 %collective-permute-start.29 = (bf16[256,1024]{1,0:T(8,128)(2,1)S(1)}, bf16[256,1024]{1,0:T(8,128)(2,1)S(1)}, u32[]{:S(2)}, u32[]{:S(2)}) collective-permute-start(bf16[256,1024]{1,0:T(8,128)(2,1)S(1)} %fusion.28), channel_id=1, source_target_pairs={{0,4},{2,6},{4,0},{6,2},{1,5},{3,7},{5,1},{7,3},{8,12},{10,14},{12... | collective-permute-start | bytes 1572872 | tf_op jit(solution)/shard_map/ppermute | solution.py:28
  452.7 27.0 %collective-permute-start.33 = (bf16[512,1024]{1,0:T(8,128)(2,1)}, bf16[512,1024]{1,0:T(8,128)(2,1)S(1)}, u32[]{:S(2)}, u32[]{:S(2)}) collective-permute-start(bf16[512,1024]{1,0:T(8,128)(2,1)} %reduce-scatter.3.cloned.1.call-done.own), channel_id=1, source_target_pairs={{0,2},{2,0},{4,6},{6,4},{1,3},{3,1},{5,7},{7,5},{8,10},{10,8},{12,... | collective-permute-start | bytes 3145736 | tf_op jit(solution)/shard_map/ppermute | solution.py:28
  453.6 26.1 %collective-permute-start.34 = (bf16[512,1024]{1,0:T(8,128)(2,1)}, bf16[512,1024]{1,0:T(8,128)(2,1)S(1)}, u32[]{:S(2)}, u32[]{:S(2)}) collective-permute-start(bf16[512,1024]{1,0:T(8,128)(2,1)} %reduce-scatter.3.cloned.1.call-done.own), channel_id=1, source_target_pairs={{0,4},{2,6},{4,0},{6,2},{1,5},{3,7},{5,1},{7,3},{8,12},{10,14},{12... | collective-permute-start | bytes 3145736 | tf_op jit(solution)/shard_map/ppermute | solution.py:28
  479.8 37.4 %collective-permute-start.36 = (bf16[2,256,1024]{2,1,0:T(8,128)(2,1)}, bf16[2,256,1024]{2,1,0:T(8,128)(2,1)}, u32[]{:S(2)}, u32[]{:S(2)}) collective-permute-start(bf16[2,256,1024]{2,1,0:T(8,128)(2,1)} %get-tuple-element.300), channel_id=1, source_target_pairs={{0,2},{2,0},{4,6},{6,4},{1,3},{3,1},{5,7},{7,5},{8,10},{10,8},{12,... | collective-permute-start | bytes 3145736 | tf_op jit(solution)/shard_map/ppermute | solution.py:28
  480.8 36.4 %collective-permute-start.37 = (bf16[2,256,1024]{2,1,0:T(8,128)(2,1)}, bf16[2,256,1024]{2,1,0:T(8,128)(2,1)}, u32[]{:S(2)}, u32[]{:S(2)}) collective-permute-start(bf16[2,256,1024]{2,1,0:T(8,128)(2,1)} %get-tuple-element.301), channel_id=1, source_target_pairs={{0,4},{2,6},{4,0},{6,2},{1,5},{3,7},{5,1},{7,3},{8,12},{10,14},{12... | collective-permute-start | bytes 3145736 | tf_op jit(solution)/shard_map/ppermute | solution.py:28
  483.2 34.0 %collective-permute-start.38 = (bf16[256,1024]{1,0:T(8,128)(2,1)}, bf16[256,1024]{1,0:T(8,128)(2,1)}, u32[]{:S(2)}, u32[]{:S(2)}) collective-permute-start(bf16[256,1024]{1,0:T(8,128)(2,1)} %slice.202), channel_id=1, source_target_pairs={{0,4},{2,6},{4,0},{6,2},{1,5},{3,7},{5,1},{7,3},{8,12},{10,14},{12... | collective-permute-start | bytes 1572872 | tf_op jit(solution)/shard_map/ppermute | solution.py:28
  484.5 32.7 %collective-permute-start.39 = (bf16[256,1024]{1,0:T(8,128)(2,1)}, bf16[256,1024]{1,0:T(8,128)(2,1)}, u32[]{:S(2)}, u32[]{:S(2)}) collective-permute-start(bf16[256,1024]{1,0:T(8,128)(2,1)} %slice.203), channel_id=1, source_target_pairs={{0,2},{2,0},{4,6},{6,4},{1,3},{3,1},{5,7},{7,5},{8,10},{10,8},{12,... | collective-permute-start | bytes 1572872 | tf_op jit(solution)/shard_map/ppermute | solution.py:28
  517.2 36.4 %collective-permute-start.42 = (bf16[512,1024]{1,0:T(8,128)(2,1)}, bf16[512,1024]{1,0:T(8,128)(2,1)S(1)}, u32[]{:S(2)}, u32[]{:S(2)}) collective-permute-start(bf16[512,1024]{1,0:T(8,128)(2,1)} %reduce-scatter.5.cloned.1.call-done.own), channel_id=1, source_target_pairs={{0,2},{2,0},{4,6},{6,4},{1,3},{3,1},{5,7},{7,5},{8,10},{10,8},{12,... | collective-permute-start | bytes 3145736 | tf_op jit(solution)/shard_map/ppermute | solution.py:28
  518.4 36.0 %collective-permute-start.43 = (bf16[512,1024]{1,0:T(8,128)(2,1)}, bf16[512,1024]{1,0:T(8,128)(2,1)S(1)}, u32[]{:S(2)}, u32[]{:S(2)}) collective-permute-start(bf16[512,1024]{1,0:T(8,128)(2,1)} %reduce-scatter.5.cloned.1.call-done.own), channel_id=1, source_target_pairs={{0,4},{2,6},{4,0},{6,2},{1,5},{3,7},{5,1},{7,3},{8,12},{10,14},{12... | collective-permute-start | bytes 3145736 | tf_op jit(solution)/shard_map/ppermute | solution.py:28
  521.1 31.6 %collective-permute-start.41 = (bf16[256,1024]{1,0:T(8,128)(2,1)S(1)}, bf16[256,1024]{1,0:T(8,128)(2,1)S(1)}, u32[]{:S(2)}, u32[]{:S(2)}) collective-permute-start(bf16[256,1024]{1,0:T(8,128)(2,1)S(1)} %fusion.31), channel_id=1, source_target_pairs={{0,2},{2,0},{4,6},{6,4},{1,3},{3,1},{5,7},{7,5},{8,10},{10,8},{12,... | collective-permute-start | bytes 1572872 | tf_op jit(solution)/shard_map/ppermute | solution.py:28
  523.6 30.0 %collective-permute-start.40 = (bf16[256,1024]{1,0:T(8,128)(2,1)S(1)}, bf16[256,1024]{1,0:T(8,128)(2,1)S(1)}, u32[]{:S(2)}, u32[]{:S(2)}) collective-permute-start(bf16[256,1024]{1,0:T(8,128)(2,1)S(1)} %fusion.30), channel_id=1, source_target_pairs={{0,4},{2,6},{4,0},{6,2},{1,5},{3,7},{5,1},{7,3},{8,12},{10,14},{12... | collective-permute-start | bytes 1572872 | tf_op jit(solution)/shard_map/ppermute | solution.py:28
  558.6 17.4 %collective-permute-start.49 = (bf16[2048,1024]{1,0:T(8,128)(2,1)}, bf16[2048,1024]{1,0:T(8,128)(2,1)S(1)}, u32[]{:S(2)}, u32[]{:S(2)}) collective-permute-start(bf16[2048,1024]{1,0:T(8,128)(2,1)} %join.10.blocks), channel_id=1, source_target_pairs={{0,1},{1,0},{2,3},{3,2},{4,5},{5,4},{6,7},{7,6},{8,9},{9,8},{10,11... | collective-permute-start | bytes 12582920 | tf_op jit(solution)/shard_map/ppermute | solution.py:32
  559.7 16.3 %collective-permute-start.45 = (bf16[256,1024]{1,0:T(8,128)(2,1)S(1)}, bf16[256,1024]{1,0:T(8,128)(2,1)S(1)}, u32[]{:S(2)}, u32[]{:S(2)}) collective-permute-start(bf16[256,1024]{1,0:T(8,128)(2,1)S(1)} %slice.216), channel_id=1, source_target_pairs={{0,4},{2,6},{4,0},{6,2},{1,5},{3,7},{5,1},{7,3},{8,12},{10,14},{12... | collective-permute-start | bytes 1572872 | tf_op jit(solution)/shard_map/ppermute | solution.py:28
  561.4 14.6 %collective-permute-start.46 = (bf16[256,1024]{1,0:T(8,128)(2,1)S(1)}, bf16[256,1024]{1,0:T(8,128)(2,1)S(1)}, u32[]{:S(2)}, u32[]{:S(2)}) collective-permute-start(bf16[256,1024]{1,0:T(8,128)(2,1)S(1)} %slice.217), channel_id=1, source_target_pairs={{0,2},{2,0},{4,6},{6,4},{1,3},{3,1},{5,7},{7,5},{8,10},{10,8},{12,... | collective-permute-start | bytes 1572872 | tf_op jit(solution)/shard_map/ppermute | solution.py:28
  578.5 17.1 %collective-permute-start.50 = (bf16[2048,1024]{1,0:T(8,128)(2,1)}, bf16[2048,1024]{1,0:T(8,128)(2,1)}, u32[]{:S(2)}, u32[]{:S(2)}) collective-permute-start(bf16[2048,1024]{1,0:T(8,128)(2,1)} %join.11.blocks), channel_id=1, source_target_pairs={{0,1},{1,0},{2,3},{3,2},{4,5},{5,4},{6,7},{7,6},{8,9},{9,8},{10,11... | collective-permute-start | bytes 12582920 | tf_op jit(solution)/shard_map/ppermute | solution.py:32
  (98 other events, 847.4 us)
Sparse Core Ops, SparseCore 0:
  14.1 27.2 all-gather.5
  55.2 63.6 all-gather.7
  121.0 79.4 all-gather.3
  334.3 74.5 reduce-scatter.2
  425.2 74.9 reduce-scatter.4

commit v4 on v3

--- a/solution.py
+++ b/solution.py
@@ -917,11 +917,13 @@
     )
     share_done = collect_middle(share_parts, share_got)
     fc1_moved = gather_start(fc1_sum)
-    vector = sum_move(vector, moves[0])
-    share_done, fc1_moved, vector, fc2_moved = tie(share_done, fc1_moved, vector, fc2_moved)
+    vector = sum_move(sum_move(vector, moves[0]), moves[1])
+    fc2_near = join(*fc2_moved)
+    share_done, fc1_moved, vector, fc2_near = tie(share_done, fc1_moved, vector, fc2_near)
     fc1_moved = gather_middle(*fc1_moved)
-    fc2_near, fc2_far = gather_end(*fc2_moved)
-    vector = sum_move(sum_move(vector, moves[1]), moves[2])
+    fc2_far = other_core(fc2_near)
+    fc2_out = place_blocks(fc2_near, place_list[:head_count])
+    vector = sum_move(vector, moves[2])
 
     share = collect_end(*share_done)
     own_centred = own_float - jnp.mean(own_float, axis=-1, keepdims=True)
@@ -934,11 +936,10 @@
     )
     input_grad = (own_up.astype(F32) + share).astype(BF).reshape(block_in.shape)
 
-    fc1_moved, vector, fc2_near, fc2_far, input_grad = tie(
-        fc1_moved, vector, fc2_near, fc2_far, input_grad
+    fc1_moved, vector, fc2_out, fc2_far, input_grad = tie(
+        fc1_moved, vector, fc2_out, fc2_far, input_grad
     )
     fc1_near, fc1_far = gather_end(*fc1_moved)
-    fc2_out = place_blocks(fc2_near, place_list[:head_count])
     fc2_out = place_blocks(fc2_far, place_list[head_count:], fc2_out)
     fc1_out = place_blocks(fc1_near, place_list[:head_count])
     for move in moves[3:]:

time: 620 us -> 616 us (level)
  waiting for transfers between devices: 150 us -> 142 us
    ppermute x32, waiting for transfers between devices: 87 us -> 61.8 us  [across(): return lax.ppermute(values, 'head', [(i, i ^ offset) for i in range(count)])]
    ppermute x5, waiting for transfers between devices: 8.98 us -> 26.7 us  [sum_move(): return vector + lax.ppermute(vector, *move)]
    unnamed x176 -> x172, local copies, waits for them, and re-layouts: 36.7 us -> 36.5 us
  transfers between devices with their start and end apart: 60 -> 60, of which waited for: 27 -> 27; matrix products, arithmetic and copies ran while one was open for 11% -> 12% of each run, Pallas kernels for 37% -> 38%
where the time goes in v4:
time: 616 us; the launch traced here: 608 us
  Pallas kernels  239 us (39%)
  waiting for transfers between devices  142 us (23%)
  local copies, waits for them, and re-layouts  72.4 us (12%)
  starting transfers between devices  65.6 us (11%)
  other arithmetic  55.3 us (9%)
  blocking collectives  18.2 us (3%)
  between operations  15.3 us (2%)
    ppermute x32, waiting for transfers between devices, across(): return lax.ppermute(values, 'head', [(i, i ^ offset) for i in range(count)])  61.8 us
    pallas_call x5, Pallas kernels, product(): pl.pallas_call(kernel, grid=(rows // tile,), in_specs=[left_spec, whole(t...  51.5 us
    pallas_call x2, Pallas kernels, shares(): pl.pallas_call(functools.partial(share_kernel, near), grid=(steps,), in_s...  37.8 us
    unnamed x172, local copies, waits for them, and re-layouts  36.5 us
    ppermute x32, starting transfers between devices, across(): return lax.ppermute(values, 'head', [(i, i ^ offset) for i in range(count)])  34.4 us
    pallas_call x1, Pallas kernels, attention(): pl.pallas_call(attention_kernel, grid_spec=pltpu.PrefetchScalarGridSpec(n...  29.5 us
    ppermute x5, waiting for transfers between devices, sum_move(): return vector + lax.ppermute(vector, *move)  26.7 us
    ppermute x4, waiting for transfers between devices, hop_up(): return lax.ppermute(values, 'dp', [(0, 1), (1, 2), (2, 3)])  20.4 us
  transfers between devices with their start and end apart: 60, of which 27 were waited for; matrix products, arithmetic and copies ran while one was open for 12% of the time, Pallas kernels for 38%

profile of v4, /device:TPU:0, one launch (start us, length us, event | category | flops | bytes accessed | tf_op | source)
XLA Modules:
  0.0 608.2 jit_solution(14869463404486344819)
XLA Ops:
  14.1 4.0 fusion.41
  19.1 16.7 %collective-permute-done.one = bf16[256,2048]{1,0:T(8,128)(2,1)S(1)} collective-permute-done((bf16[256,2048]{1,0:T(8,128)(2,1)}, bf16[256,2048]{1,0:T(8,128)(2,1)S(1)}, u32[]{:S(2)}, u32[]{:S(2)}) %collective-permute-start) | collective-permute-done | bytes 1048608 | tf_op jit(solution)/shard_map/ppermute | solution.py:28
  39.6 10.4 %collective-permute-done.2.low = bf16[128,2048]{1,0:T(8,128)(2,1)S(1)} collective-permute-done((bf16[128,2048]{1,0:T(8,128)(2,1)S(1)}, bf16[128,2048]{1,0:T(8,128)(2,1)S(1)}, u32[]{:S(2)}, u32[]{:S(2)}) %collective-permute-start.2) | collective-permute-done | bytes 524320 | tf_op jit(solution)/shard_map/ppermute | solution.py:28
  62.4 3.7 fusion.32
  69.0 14.2 %norms.1 = (bf16[2048,2048]{1,0:T(8,128)(2,1)}, bf16[2048,2048]{1,0:T(8,128)(2,1)}, bf16[2048,2048]{1,0:T(8,128)(2,1)}) custom-call(bf16[1024,2048]{1,0:T(8,128)(2,1)S(1)} %copy-done.10, bf16[1024,2048]{1,0:T(8,128)(2,1)} %collective-permute-done.6.far, f32[1,2048]{1,0:T(1,128)S(1)} %bitcast.121, f32[1,2048]{1,0:T(1,128)S(1)} %bitcast.127, ...), custom_call_target="tpu_custom_call" | custom-call | flops 1000000000 | bytes 1000000 | tf_op jit(solution)/shard_map/norms/pallas_call | solution.py:420
  87.9 9.5 %collective-permute-done.7.low = bf16[128,2048]{1,0:T(8,128)(2,1)S(1)} collective-permute-done((bf16[128,2048]{1,0:T(8,128)(2,1)S(1)}, bf16[128,2048]{1,0:T(8,128)(2,1)S(1)}, u32[]{:S(2)}, u32[]{:S(2)}) %collective-permute-start.7) | collective-permute-done | bytes 524320 | tf_op jit(solution)/shard_map/ppermute | solution.py:28
  99.4 3.7 join.7
  103.1 3.8 all-to-all-start
  107.8 11.1 %all-gather.8.cloned.1.call-done.right.qkv_weight = bf16[2048,768]{1,0:T(8,128)(2,1)} async-done(((bf16[512,768]{1,0:T(8,128)(2,1)}), bf16[2048,768]{1,0:T(8,128)(2,1)}) %all-gather.8.cloned.1.call-update) | async-done | bytes 3145744 | tf_op jit(solution)/shard_map/all_gather | solution.py:55
  120.7 10.6 %product.5 = f32[2048,768]{1,0:T(8,128)} custom-call(bf16[2048,2048]{1,0:T(8,128)(2,1)} %get-tuple-element.199.left, bf16[2048,768]{1,0:T(8,128)(2,1)S(1)} %copy-done.5), custom_call_target="tpu_custom_call" | custom-call | flops 1000000000 | bytes 1000000 | tf_op jit(solution)/shard_map/product/pallas_call | solution.py:171
  136.5 3.3 copy-done.52
  139.9 5.8 product.6
  145.7 29.5 %attention.1 = (bf16[8,256,256]{2,1,0:T(8,128)(2,1)S(1)}, bf16[8,256,256]{2,1,0:T(8,128)(2,1)S(1)}, bf16[8,256,768]{2,1,0:T(8,128)(2,1)}) custom-call(s32[8]{0:T(128)S(1)} %get-tuple-element.393.order, s32[8]{0:T(128)S(1)} %get-tuple-element.392.first, f32[8,256,768]{2,1,0:T(8,128)} %bitcast.131, f32[1,768]{1,0:T(1,128)S(1)} %maximum_convert_fusion.bias, ...), custom_call_target="tpu_custom_call" | custom-call | flops 1000000000 | bytes 1000000 | tf_op jit(solution)/shard_map/attention/pallas_call | solution.py:660
  175.2 6.0 wide.1
  182.3 3.6 all-to-all-start.1
  187.2 10.3 %product.7 = bf16[2048,768]{1,0:T(8,128)(2,1)S(1)} custom-call(bf16[2048,2048]{1,0:T(8,128)(2,1)} %get-tuple-element.199.left, bf16[2048,768]{1,0:T(8,128)(2,1)} %bitcast.100), custom_call_target="tpu_custom_call" | custom-call | flops 1000000000 | bytes 1000000 | tf_op jit(solution)/shard_map/product/pallas_call | solution.py:171
  201.2 4.5 pad_maximum_fusion
  205.7 3.0 slice_select_fusion
  214.5 16.2 %hidden.1 = (bf16[2048,1024]{1,0:T(8,128)(2,1)S(1)}, bf16[2048,1024]{1,0:T(8,128)(2,1)}) custom-call(bf16[2048,2048]{1,0:T(8,128)(2,1)} %get-tuple-element.215.tokens.left, bf16[2048,1024]{1,0:T(8,128)(2,1)} %all-gather.4.cloned.1.call-done.weight, f32[1,1024]{1,0:T(1,128)S(1)} %bitcast.129), custom_call_target="tpu_custom_call" | custom-call | flops 1000000000 | bytes 1000000 | tf_op jit(solution)/shard_map/hidden/pallas_call | solution.py:213
  231.6 5.2 collective-permute-done.11
  238.2 5.4 fusion.24
  243.6 5.2 collective-permute-start.14
  254.3 12.3 %product.8 = bf16[2048,1024]{1,0:T(8,128)(2,1)S(1)} custom-call(bf16[2048,2048]{1,0:T(8,128)(2,1)} %copy-done.52, bf16[2048,1024]{1,0:T(8,128)(2,1)} %copy-done.3), custom_call_target="tpu_custom_call" | custom-call | flops 1000000000 | bytes 1000000 | tf_op jit(solution)/shard_map/product/pallas_call | solution.py:171
  269.4 5.1 collective-permute-done.15
  274.5 5.4 fusion.22
  283.0 18.2 %all_to_all.54 = bf16[8,256,256]{2,1,0:T(8,128)(2,1)S(1)} all-to-all(bf16[8,256,256]{2,1,0:T(8,128)(2,1)S(1)} %copy-done.42), channel_id=1, replica_groups=mesh['dp'=4,'head'=4,'blk'=2] {'head','blk'}, dimensions={0} | all-to-all | bytes 2097152 | tf_op jit(solution)/shard_map/all_to_all | solution.py:842
  302.3 3.7 collective-permute-done.19
  311.3 18.7 %collective-permute-done.20 = bf16[512,1024]{1,0:T(8,128)(2,1)S(1)} collective-permute-done((bf16[512,1024]{1,0:T(8,128)(2,1)S(1)}, bf16[512,1024]{1,0:T(8,128)(2,1)S(1)}, u32[]{:S(2)}, u32[]{:S(2)}) %collective-permute-start.20) | collective-permute-done | bytes 1048608 | tf_op jit(solution)/shard_map/ppermute | solution.py:63
  330.0 4.2 collective-permute-done.21
  335.1 3.7 add_convert_fusion.own
  349.9 7.3 %far.1 = bf16[1024,2048]{1,0:T(8,128)(2,1)S(1)} custom-call(bf16[2048,1024]{1,0:T(8,128)(2,1)} %copy-done.3, bf16[2048,1024]{1,0:T(8,128)(2,1)} %copy-done.53), custom_call_target="tpu_custom_call" | custom-call | flops 1000000000 | bytes 1000000 | tf_op jit(solution)/shard_map/far/pallas_call | solution.py:305
  359.2 13.2 %hidden_grad.1 = (bf16[2048,1024]{1,0:T(8,128)(2,1)S(1)}, f32[1,1024]{1,0:T(1,128)S(1)}) custom-call(bf16[2048,2048]{1,0:T(8,128)(2,1)} %copy-done.52, bf16[2048,1024]{1,0:T(8,128)(2,1)} %copy-done.53, bf16[2048,1024]{1,0:T(8,128)(2,1)} %get-tuple-element.252.slope), custom_call_target="tpu_custom_call" | custom-call | flops 1000000000 | bytes 1000000 | tf_op jit(solution)/shard_map/hidden_grad/pallas_call | solution.py:241
  374.4 8.4 %collective-permute-done.22.one = bf16[512,1024]{1,0:T(8,128)(2,1)S(1)} collective-permute-done((bf16[512,1024]{1,0:T(8,128)(2,1)S(1)}, bf16[512,1024]{1,0:T(8,128)(2,1)S(1)}, u32[]{:S(2)}, u32[]{:S(2)}) %collective-permute-start.22) | collective-permute-done | bytes 1048608 | tf_op jit(solution)/shard_map/ppermute | solution.py:28
  385.5 9.9 %near.1 = (bf16[2,256,1024]{2,1,0:T(8,128)(2,1)S(1)}, bf16[2,256,1024]{2,1,0:T(8,128)(2,1)}, bf16[2,256,1024]{2,1,0:T(8,128)(2,1)S(1)}, bf16[2,256,1024]{2,1,0:T(8,128)(2,1)}) custom-call(bf16[2048,1024]{1,0:T(8,128)(2,1)} %copy-done.3, bf16[2048,1024]{1,0:T(8,128)(2,1)} %copy-done.53, bf16[1024,2048]{1,0:T(8,128)(2,1)} %collective-permute-done.24.more), custom_call_target="tpu_custom_call" | custom-call | flops 1000000000 | bytes 1000000 | tf_op jit(solution)/shard_map/near/pallas_call | solution.py:328
  400.1 4.0 join.9.near
  404.2 12.5 %product.9 = bf16[2048,1024]{1,0:T(8,128)(2,1)S(1)} custom-call(bf16[2048,2048]{1,0:T(8,128)(2,1)} %get-tuple-element.215.tokens.left, bf16[2048,1024]{1,0:T(8,128)(2,1)} %copy-done.4), custom_call_target="tpu_custom_call" | custom-call | flops 1000000000 | bytes 1000000 | tf_op jit(solution)/shard_map/product/pallas_call | solution.py:171
  432.0 16.9 %share_far.1 = (bf16[1024,2048]{1,0:T(8,128)(2,1)}, f32[8,2048]{1,0:T(8,128)S(1)}) custom-call(bf16[2048,768]{1,0:T(8,128)(2,1)S(1)} %bitcast.102, bf16[2048,768]{1,0:T(8,128)(2,1)} %all-gather.8.cloned.1.call-done.right.qkv_weight, bf16[2048,1024]{1,0:T(8,128)(2,1)} %copy-done.4, bf16[2048,1024]{1,0:T(8,128)(2,1)} %all-gather.4.cloned.1.call-done.weight, ...), custom_call_target="tpu_custom_call" | custom-call | flops 1000000000 | bytes 1000000 | tf_op jit(solution)/shard_map/share_far/pallas_call | solution.py:374
  458.8 20.9 %share_near.1 = (bf16[2,256,1024]{2,1,0:T(8,128)(2,1)S(1)}, bf16[2,256,1024]{2,1,0:T(8,128)(2,1)}, bf16[2,256,1024]{2,1,0:T(8,128)(2,1)S(1)}, bf16[2,256,1024]{2,1,0:T(8,128)(2,1)}, f32[8,2048]{1,0:T(8,128)S(1)}) custom-call(bf16[2048,768]{1,0:T(8,128)(2,1)} %bitcast.101, bf16[2048,768]{1,0:T(8,128)(2,1)} %all-gather.8.cloned.1.call-done.right.qkv_weight, ...), custom_call_target="tpu_custom_call" | custom-call | flops 1000000000 | bytes 1000000 | tf_op jit(solution)/shard_map/share_near/pallas_call | solution.py:374
  487.6 8.4 %columns.1 = f32[256,2048]{1,0:T(8,128)S(1)} custom-call(s32[8]{0:T(128)S(1)} %stack.68.places, bf16[256,2048]{1,0:T(8,128)(2,1)S(1)} %bitcast.117, bf16[8192,256]{1,0:T(8,128)(2,1)} %join.9.near, bf16[8192,256]{1,0:T(8,128)(2,1)} %collective-permute-done.32.far), custom_call_target="tpu_custom_call" | custom-call | flops 1000000000 | bytes 1000000 | tf_op jit(solution)/shard_map/columns/pallas_call | solution.py:478
  498.8 9.7 %spread.1 = (f32[512,6144]{1,0:T(8,128)}, f32[512,2048]{1,0:T(8,128)}) custom-call(s32[8]{0:T(128)S(1)} %stack.68.places, bf16[4,512,1024]{2,1,0:T(8,128)(2,1)S(1)} %bitcast.110, bf16[4,512,1024]{2,1,0:T(8,128)(2,1)} %bitcast.43.far), custom_call_target="tpu_custom_call" | custom-call | flops 1000000000 | bytes 1000000 | tf_op jit(solution)/shard_map/spread/pallas_call | solution.py:520
  513.7 5.5 collective-permute-done.38.low
  529.5 4.2 join.10.blocks
  533.7 23.2 %collective-permute-done.45 = f32[200,128]{1,0:T(8,128)S(1)} collective-permute-done((f32[200,128]{1,0:T(8,128)S(1)}, f32[200,128]{1,0:T(8,128)S(1)}, u32[]{:S(2)}, u32[]{:S(2)}) %collective-permute-start.45) | collective-permute-done | bytes 102432 | tf_op jit(solution)/shard_map/ppermute | solution.py:153
  567.8 4.2 place.4.rest_0_
  579.5 3.5 collective-permute-done.51
  585.9 4.2 place.5.rest_0_
  590.0 4.2 place.6
  596.7 4.2 place.7
  (385 shorter events, 172.0 us)
Async XLA Ops:
  7.2 76.0 %all-gather.6.cloned.1.call-start = ((), (), s32[]{:S(2)}) async-start(), calls=%async_computation.6 | async-start | bytes 1310720 | tf_op jit(solution)/shard_map/all_gather | solution.py:55
  9.5 26.3 %collective-permute-start = (bf16[256,2048]{1,0:T(8,128)(2,1)}, bf16[256,2048]{1,0:T(8,128)(2,1)S(1)}, u32[]{:S(2)}, u32[]{:S(2)}) collective-permute-start(bf16[256,2048]{1,0:T(8,128)(2,1)} %bitcast.103), channel_id=1, source_target_pairs={{0,2},{2,0},{4,6},{6,4},{1,3},{3,1},{5,7},{7,5},{8,10},{10,8},{12,... | collective-permute-start | bytes 3145736 | tf_op jit(solution)/shard_map/ppermute | solution.py:28
  12.5 24.8 %collective-permute-start.1 = (bf16[256,2048]{1,0:T(8,128)(2,1)}, bf16[256,2048]{1,0:T(8,128)(2,1)S(1)}, u32[]{:S(2)}, u32[]{:S(2)}) collective-permute-start(bf16[256,2048]{1,0:T(8,128)(2,1)} %bitcast.104), channel_id=1, source_target_pairs={{0,4},{2,6},{4,0},{6,2},{1,5},{3,7},{5,1},{7,3},{8,12},{10,14},{12... | collective-permute-start | bytes 3145736 | tf_op jit(solution)/shard_map/ppermute | solution.py:28
  14.0 104.8 %all-gather.8.cloned.1.call-start = ((), (), s32[]{:S(2)}) async-start(), calls=%async_computation.7 | async-start | bytes 3932160 | tf_op jit(solution)/shard_map/all_gather | solution.py:55
  55.1 150.6 %all-gather.4.cloned.1.call-start = ((), (), s32[]{:S(2)}) async-start(), calls=%async_computation.5 | async-start | bytes 5242880 | tf_op jit(solution)/shard_map/all_gather | solution.py:55
  58.0 25.6 %collective-permute-start.4 = (bf16[256,2048]{1,0:T(8,128)(2,1)S(1)}, bf16[256,2048]{1,0:T(8,128)(2,1)S(1)}, u32[]{:S(2)}, u32[]{:S(2)}) collective-permute-start(bf16[256,2048]{1,0:T(8,128)(2,1)S(1)} %bitcast.111), channel_id=1, source_target_pairs={{0,2},{2,0},{4,6},{6,4},{1,3},{3,1},{5,7},{7,5},{8,10},{10,8},{12,... | collective-permute-start | bytes 3145736 | tf_op jit(solution)/shard_map/ppermute | solution.py:28
  58.6 25.4 %collective-permute-start.5 = (bf16[256,2048]{1,0:T(8,128)(2,1)S(1)}, bf16[256,2048]{1,0:T(8,128)(2,1)}, u32[]{:S(2)}, u32[]{:S(2)}) collective-permute-start(bf16[256,2048]{1,0:T(8,128)(2,1)S(1)} %bitcast.112), channel_id=1, source_target_pairs={{0,4},{2,6},{4,0},{6,2},{1,5},{3,7},{5,1},{7,3},{8,12},{10,14},{12... | collective-permute-start | bytes 3145736 | tf_op jit(solution)/shard_map/ppermute | solution.py:28
  103.1 28.4 %collective-permute-start.9 = (bf16[1024,2048]{1,0:T(8,128)(2,1)}, bf16[1024,2048]{1,0:T(8,128)(2,1)}, u32[]{:S(2)}, u32[]{:S(2)}) collective-permute-start(bf16[1024,2048]{1,0:T(8,128)(2,1)} %join.7), channel_id=1, source_target_pairs={{0,1},{1,0},{2,3},{3,2},{4,5},{5,4},{6,7},{7,6},{8,9},{9,8},{10,11... | collective-permute-start | bytes 12582920 | tf_op jit(solution)/shard_map/ppermute | solution.py:32
  103.1 28.3 %all-to-all-start = ((bf16[8,256,256]{2,1,0:T(8,128)(2,1)}), bf16[8,256,256]{2,1,0:T(8,128)(2,1)S(1)}, u32[]{:S(2)}, u32[]{:S(2)}) async-start(bf16[8,256,256]{2,1,0:T(8,128)(2,1)} %bitcast.17), calls=%async_computation | async-start | bytes 2097152 | tf_op jit(solution)/shard_map/all_to_all | solution.py:785
  182.3 19.0 %all-to-all-start.1 = ((bf16[256,8,256]{2,0,1:T(8,128)(2,1)}), bf16[256,8,256]{2,0,1:T(8,128)(2,1)S(1)}, u32[]{:S(2)}, u32[]{:S(2)}) async-start(bf16[256,8,256]{2,0,1:T(8,128)(2,1)} %bitcast.97), calls=%async_computation.1 | async-start | bytes 2097152 | tf_op jit(solution)/shard_map/all_to_all | solution.py:815
  185.8 238.7 %reduce-scatter.3.cloned.1.call-start = ((), (), s32[]{:S(2)}) async-start(), calls=%async_computation.8 | async-start | bytes 5242880 | tf_op jit(solution)/shard_map/reduce_scatter | solution.py:59
  208.7 22.9 %collective-permute-start.10 = (bf16[512,1024]{1,0:T(8,128)(2,1)}, bf16[512,1024]{1,0:T(8,128)(2,1)}, u32[]{:S(2)}, u32[]{:S(2)}) collective-permute-start(bf16[512,1024]{1,0:T(8,128)(2,1)} %get-tuple-element.366), channel_id=1, source_target_pairs={{0,8},{8,16},{16,24},{1,9},{9,17},{17,25},{2,10},{10,18},{18,26},{... | collective-permute-start | bytes 3145736 | tf_op jit(solution)/shard_map/ppermute | solution.py:63
  211.0 25.7 %collective-permute-start.11 = (bf16[512,1024]{1,0:T(8,128)(2,1)}, bf16[512,1024]{1,0:T(8,128)(2,1)}, u32[]{:S(2)}, u32[]{:S(2)}) collective-permute-start(bf16[512,1024]{1,0:T(8,128)(2,1)} %get-tuple-element.365), channel_id=1, source_target_pairs={{24,16},{16,8},{8,0},{25,17},{17,9},{9,1},{26,18},{18,10},{10,2},{... | collective-permute-start | bytes 3145736 | tf_op jit(solution)/shard_map/ppermute | solution.py:67
  212.3 24.4 %collective-permute-start.12 = (bf16[2048,256]{1,0:T(8,128)(2,1)}, bf16[2048,256]{1,0:T(8,128)(2,1)S(1)}, u32[]{:S(2)}, u32[]{:S(2)}) collective-permute-start(bf16[2048,256]{1,0:T(8,128)(2,1)} %all-gather.6.cloned.1.call-done.own), channel_id=1, source_target_pairs={{0,2},{2,0},{4,6},{6,4},{1,3},{3,1},{5,7},{7,5},{8,10},{10,8},{12,... | collective-permute-start | bytes 3145736 | tf_op jit(solution)/shard_map/ppermute | solution.py:28
  212.9 25.3 %collective-permute-start.13 = (bf16[2048,256]{1,0:T(8,128)(2,1)}, bf16[2048,256]{1,0:T(8,128)(2,1)}, u32[]{:S(2)}, u32[]{:S(2)}) collective-permute-start(bf16[2048,256]{1,0:T(8,128)(2,1)} %all-gather.6.cloned.1.call-done.own), channel_id=1, source_target_pairs={{0,4},{2,6},{4,0},{6,2},{1,5},{3,7},{5,1},{7,3},{8,12},{10,14},{12... | collective-permute-start | bytes 3145736 | tf_op jit(solution)/shard_map/ppermute | solution.py:28
  243.6 25.8 %collective-permute-start.14 = (bf16[512,1024]{1,0:T(8,128)(2,1)}, bf16[512,1024]{1,0:T(8,128)(2,1)}, u32[]{:S(2)}, u32[]{:S(2)}) collective-permute-start(bf16[512,1024]{1,0:T(8,128)(2,1)} %get-tuple-element.364), channel_id=1, source_target_pairs={{0,8},{8,16},{16,24},{1,9},{9,17},{17,25},{2,10},{10,18},{18,26},{... | collective-permute-start | bytes 3145736 | tf_op jit(solution)/shard_map/ppermute | solution.py:63
  248.8 25.7 %collective-permute-start.15 = (bf16[512,1024]{1,0:T(8,128)(2,1)}, bf16[512,1024]{1,0:T(8,128)(2,1)}, u32[]{:S(2)}, u32[]{:S(2)}) collective-permute-start(bf16[512,1024]{1,0:T(8,128)(2,1)} %get-tuple-element.363), channel_id=1, source_target_pairs={{24,16},{16,8},{8,0},{25,17},{17,9},{9,1},{26,18},{18,10},{10,2},{... | collective-permute-start | bytes 3145736 | tf_op jit(solution)/shard_map/ppermute | solution.py:67
  250.9 17.7 %collective-permute-start.16 = (bf16[1024,256]{1,0:T(8,128)(2,1)}, bf16[1024,256]{1,0:T(8,128)(2,1)S(1)}, u32[]{:S(2)}, u32[]{:S(2)}) collective-permute-start(bf16[1024,256]{1,0:T(8,128)(2,1)} %slice.190), channel_id=1, source_target_pairs={{0,4},{2,6},{4,0},{6,2},{1,5},{3,7},{5,1},{7,3},{8,12},{10,14},{12... | collective-permute-start | bytes 1572872 | tf_op jit(solution)/shard_map/ppermute | solution.py:28
  253.7 14.9 %collective-permute-start.17 = (bf16[1024,256]{1,0:T(8,128)(2,1)}, bf16[1024,256]{1,0:T(8,128)(2,1)S(1)}, u32[]{:S(2)}, u32[]{:S(2)}) collective-permute-start(bf16[1024,256]{1,0:T(8,128)(2,1)} %slice.191), channel_id=1, source_target_pairs={{0,2},{2,0},{4,6},{6,4},{1,3},{3,1},{5,7},{7,5},{8,10},{10,8},{12,... | collective-permute-start | bytes 1572872 | tf_op jit(solution)/shard_map/ppermute | solution.py:28
  279.9 22.4 %collective-permute-start.18 = (bf16[512,1024]{1,0:T(8,128)(2,1)S(1)}, bf16[512,1024]{1,0:T(8,128)(2,1)S(1)}, u32[]{:S(2)}, u32[]{:S(2)}) collective-permute-start(bf16[512,1024]{1,0:T(8,128)(2,1)S(1)} %get-tuple-element.370), channel_id=1, source_target_pairs={{0,8},{8,16},{16,24},{1,9},{9,17},{17,25},{2,10},{10,18},{18,26},{... | collective-permute-start | bytes 3145736 | tf_op jit(solution)/shard_map/ppermute | solution.py:63
  281.5 24.6 %collective-permute-start.19 = (bf16[512,1024]{1,0:T(8,128)(2,1)S(1)}, bf16[512,1024]{1,0:T(8,128)(2,1)S(1)}, u32[]{:S(2)}, u32[]{:S(2)}) collective-permute-start(bf16[512,1024]{1,0:T(8,128)(2,1)S(1)} %get-tuple-element.369), channel_id=1, source_target_pairs={{24,16},{16,8},{8,0},{25,17},{17,9},{9,1},{26,18},{18,10},{10,2},{... | collective-permute-start | bytes 3145736 | tf_op jit(solution)/shard_map/ppermute | solution.py:67
  307.1 22.9 %collective-permute-start.20 = (bf16[512,1024]{1,0:T(8,128)(2,1)S(1)}, bf16[512,1024]{1,0:T(8,128)(2,1)S(1)}, u32[]{:S(2)}, u32[]{:S(2)}) collective-permute-start(bf16[512,1024]{1,0:T(8,128)(2,1)S(1)} %get-tuple-element.368), channel_id=1, source_target_pairs={{0,8},{8,16},{16,24},{1,9},{9,17},{17,25},{2,10},{10,18},{18,26},{... | collective-permute-start | bytes 3145736 | tf_op jit(solution)/shard_map/ppermute | solution.py:63
  310.0 24.2 %collective-permute-start.21 = (bf16[512,1024]{1,0:T(8,128)(2,1)S(1)}, bf16[512,1024]{1,0:T(8,128)(2,1)S(1)}, u32[]{:S(2)}, u32[]{:S(2)}) collective-permute-start(bf16[512,1024]{1,0:T(8,128)(2,1)S(1)} %get-tuple-element.367), channel_id=1, source_target_pairs={{24,16},{16,8},{8,0},{25,17},{17,9},{9,1},{26,18},{18,10},{10,2},{... | collective-permute-start | bytes 3145736 | tf_op jit(solution)/shard_map/ppermute | solution.py:67
  335.1 178.6 %reduce-scatter.5.cloned.1.call-start = ((), (), s32[]{:S(2)}) async-start(), calls=%async_computation.9 | async-start | bytes 5242880 | tf_op jit(solution)/shard_map/reduce_scatter | solution.py:59
  357.1 26.7 %collective-permute-start.24 = (bf16[1024,2048]{1,0:T(8,128)(2,1)S(1)}, bf16[1024,2048]{1,0:T(8,128)(2,1)}, u32[]{:S(2)}, u32[]{:S(2)}) collective-permute-start(bf16[1024,2048]{1,0:T(8,128)(2,1)S(1)} %far.1), channel_id=1, source_target_pairs={{0,1},{1,0},{2,3},{3,2},{4,5},{5,4},{6,7},{7,6},{8,9},{9,8},{10,11... | collective-permute-start | bytes 12582920 | tf_op jit(solution)/shard_map/ppermute | solution.py:32
  357.2 25.6 %collective-permute-start.22 = (bf16[512,1024]{1,0:T(8,128)(2,1)S(1)}, bf16[512,1024]{1,0:T(8,128)(2,1)S(1)}, u32[]{:S(2)}, u32[]{:S(2)}) collective-permute-start(bf16[512,1024]{1,0:T(8,128)(2,1)S(1)} %add_convert_fusion.own), channel_id=1, source_target_pairs={{0,2},{2,0},{4,6},{6,4},{1,3},{3,1},{5,7},{7,5},{8,10},{10,8},{12,... | collective-permute-start | bytes 3145736 | tf_op jit(solution)/shard_map/ppermute | solution.py:28
  358.6 25.2 %collective-permute-start.23 = (bf16[512,1024]{1,0:T(8,128)(2,1)S(1)}, bf16[512,1024]{1,0:T(8,128)(2,1)S(1)}, u32[]{:S(2)}, u32[]{:S(2)}) collective-permute-start(bf16[512,1024]{1,0:T(8,128)(2,1)S(1)} %add_convert_fusion.own), channel_id=1, source_target_pairs={{0,4},{2,6},{4,0},{6,2},{1,5},{3,7},{5,1},{7,3},{8,12},{10,14},{12... | collective-permute-start | bytes 3145736 | tf_op jit(solution)/shard_map/ppermute | solution.py:28
  397.7 26.8 %collective-permute-start.27 = (bf16[2,256,1024]{2,1,0:T(8,128)(2,1)}, bf16[2,256,1024]{2,1,0:T(8,128)(2,1)}, u32[]{:S(2)}, u32[]{:S(2)}) collective-permute-start(bf16[2,256,1024]{2,1,0:T(8,128)(2,1)} %get-tuple-element.265), channel_id=1, source_target_pairs={{0,2},{2,0},{4,6},{6,4},{1,3},{3,1},{5,7},{7,5},{8,10},{10,8},{12,... | collective-permute-start | bytes 3145736 | tf_op jit(solution)/shard_map/ppermute | solution.py:28
  398.7 25.7 %collective-permute-start.28 = (bf16[2,256,1024]{2,1,0:T(8,128)(2,1)}, bf16[2,256,1024]{2,1,0:T(8,128)(2,1)}, u32[]{:S(2)}, u32[]{:S(2)}) collective-permute-start(bf16[2,256,1024]{2,1,0:T(8,128)(2,1)} %get-tuple-element.266), channel_id=1, source_target_pairs={{0,4},{2,6},{4,0},{6,2},{1,5},{3,7},{5,1},{7,3},{8,12},{10,14},{12... | collective-permute-start | bytes 3145736 | tf_op jit(solution)/shard_map/ppermute | solution.py:28
  424.5 26.8 %collective-permute-start.31 = (bf16[2048,1024]{1,0:T(8,128)(2,1)}, bf16[2048,1024]{1,0:T(8,128)(2,1)}, u32[]{:S(2)}, u32[]{:S(2)}) collective-permute-start(bf16[2048,1024]{1,0:T(8,128)(2,1)} %join.8), channel_id=1, source_target_pairs={{0,1},{1,0},{2,3},{3,2},{4,5},{5,4},{6,7},{7,6},{8,9},{9,8},{10,11... | collective-permute-start | bytes 12582920 | tf_op jit(solution)/shard_map/ppermute | solution.py:32
  424.6 26.7 %collective-permute-start.32 = (bf16[8192,256]{1,0:T(8,128)(2,1)}, bf16[8192,256]{1,0:T(8,128)(2,1)}, u32[]{:S(2)}, u32[]{:S(2)}) collective-permute-start(bf16[8192,256]{1,0:T(8,128)(2,1)} %join.9.near), channel_id=1, source_target_pairs={{0,1},{1,0},{2,3},{3,2},{4,5},{5,4},{6,7},{7,6},{8,9},{9,8},{10,11... | collective-permute-start | bytes 12582920 | tf_op jit(solution)/shard_map/ppermute | solution.py:32
  428.9 22.3 %collective-permute-start.30 = (bf16[256,1024]{1,0:T(8,128)(2,1)S(1)}, bf16[256,1024]{1,0:T(8,128)(2,1)S(1)}, u32[]{:S(2)}, u32[]{:S(2)}) collective-permute-start(bf16[256,1024]{1,0:T(8,128)(2,1)S(1)} %fusion.29), channel_id=1, source_target_pairs={{0,2},{2,0},{4,6},{6,4},{1,3},{3,1},{5,7},{7,5},{8,10},{10,8},{12,... | collective-permute-start | bytes 1572872 | tf_op jit(solution)/shard_map/ppermute | solution.py:28
  431.2 20.0 %collective-permute-start.29 = (bf16[256,1024]{1,0:T(8,128)(2,1)S(1)}, bf16[256,1024]{1,0:T(8,128)(2,1)S(1)}, u32[]{:S(2)}, u32[]{:S(2)}) collective-permute-start(bf16[256,1024]{1,0:T(8,128)(2,1)S(1)} %fusion.28), channel_id=1, source_target_pairs={{0,4},{2,6},{4,0},{6,2},{1,5},{3,7},{5,1},{7,3},{8,12},{10,14},{12... | collective-permute-start | bytes 1572872 | tf_op jit(solution)/shard_map/ppermute | solution.py:28
  452.7 29.0 %collective-permute-start.33 = (bf16[512,1024]{1,0:T(8,128)(2,1)}, bf16[512,1024]{1,0:T(8,128)(2,1)S(1)}, u32[]{:S(2)}, u32[]{:S(2)}) collective-permute-start(bf16[512,1024]{1,0:T(8,128)(2,1)} %reduce-scatter.3.cloned.1.call-done.own), channel_id=1, source_target_pairs={{0,2},{2,0},{4,6},{6,4},{1,3},{3,1},{5,7},{7,5},{8,10},{10,8},{12,... | collective-permute-start | bytes 3145736 | tf_op jit(solution)/shard_map/ppermute | solution.py:28
  453.7 28.1 %collective-permute-start.34 = (bf16[512,1024]{1,0:T(8,128)(2,1)}, bf16[512,1024]{1,0:T(8,128)(2,1)S(1)}, u32[]{:S(2)}, u32[]{:S(2)}) collective-permute-start(bf16[512,1024]{1,0:T(8,128)(2,1)} %reduce-scatter.3.cloned.1.call-done.own), channel_id=1, source_target_pairs={{0,4},{2,6},{4,0},{6,2},{1,5},{3,7},{5,1},{7,3},{8,12},{10,14},{12... | collective-permute-start | bytes 3145736 | tf_op jit(solution)/shard_map/ppermute | solution.py:28
  481.8 37.4 %collective-permute-start.36 = (bf16[2,256,1024]{2,1,0:T(8,128)(2,1)}, bf16[2,256,1024]{2,1,0:T(8,128)(2,1)}, u32[]{:S(2)}, u32[]{:S(2)}) collective-permute-start(bf16[2,256,1024]{2,1,0:T(8,128)(2,1)} %get-tuple-element.296), channel_id=1, source_target_pairs={{0,2},{2,0},{4,6},{6,4},{1,3},{3,1},{5,7},{7,5},{8,10},{10,8},{12,... | collective-permute-start | bytes 3145736 | tf_op jit(solution)/shard_map/ppermute | solution.py:28
  482.8 36.4 %collective-permute-start.37 = (bf16[2,256,1024]{2,1,0:T(8,128)(2,1)}, bf16[2,256,1024]{2,1,0:T(8,128)(2,1)}, u32[]{:S(2)}, u32[]{:S(2)}) collective-permute-start(bf16[2,256,1024]{2,1,0:T(8,128)(2,1)} %get-tuple-element.297), channel_id=1, source_target_pairs={{0,4},{2,6},{4,0},{6,2},{1,5},{3,7},{5,1},{7,3},{8,12},{10,14},{12... | collective-permute-start | bytes 3145736 | tf_op jit(solution)/shard_map/ppermute | solution.py:28
  485.2 34.0 %collective-permute-start.38 = (bf16[256,1024]{1,0:T(8,128)(2,1)}, bf16[256,1024]{1,0:T(8,128)(2,1)}, u32[]{:S(2)}, u32[]{:S(2)}) collective-permute-start(bf16[256,1024]{1,0:T(8,128)(2,1)} %slice.202), channel_id=1, source_target_pairs={{0,4},{2,6},{4,0},{6,2},{1,5},{3,7},{5,1},{7,3},{8,12},{10,14},{12... | collective-permute-start | bytes 1572872 | tf_op jit(solution)/shard_map/ppermute | solution.py:28
  486.5 32.7 %collective-permute-start.39 = (bf16[256,1024]{1,0:T(8,128)(2,1)}, bf16[256,1024]{1,0:T(8,128)(2,1)}, u32[]{:S(2)}, u32[]{:S(2)}) collective-permute-start(bf16[256,1024]{1,0:T(8,128)(2,1)} %slice.203), channel_id=1, source_target_pairs={{0,2},{2,0},{4,6},{6,4},{1,3},{3,1},{5,7},{7,5},{8,10},{10,8},{12,... | collective-permute-start | bytes 1572872 | tf_op jit(solution)/shard_map/ppermute | solution.py:28
  519.2 37.8 %collective-permute-start.42 = (bf16[512,1024]{1,0:T(8,128)(2,1)}, bf16[512,1024]{1,0:T(8,128)(2,1)S(1)}, u32[]{:S(2)}, u32[]{:S(2)}) collective-permute-start(bf16[512,1024]{1,0:T(8,128)(2,1)} %reduce-scatter.5.cloned.1.call-done.own), channel_id=1, source_target_pairs={{0,2},{2,0},{4,6},{6,4},{1,3},{3,1},{5,7},{7,5},{8,10},{10,8},{12,... | collective-permute-start | bytes 3145736 | tf_op jit(solution)/shard_map/ppermute | solution.py:28
  520.4 36.6 %collective-permute-start.43 = (bf16[512,1024]{1,0:T(8,128)(2,1)}, bf16[512,1024]{1,0:T(8,128)(2,1)S(1)}, u32[]{:S(2)}, u32[]{:S(2)}) collective-permute-start(bf16[512,1024]{1,0:T(8,128)(2,1)} %reduce-scatter.5.cloned.1.call-done.own), channel_id=1, source_target_pairs={{0,4},{2,6},{4,0},{6,2},{1,5},{3,7},{5,1},{7,3},{8,12},{10,14},{12... | collective-permute-start | bytes 3145736 | tf_op jit(solution)/shard_map/ppermute | solution.py:28
  523.1 33.8 %collective-permute-start.41 = (bf16[256,1024]{1,0:T(8,128)(2,1)S(1)}, bf16[256,1024]{1,0:T(8,128)(2,1)S(1)}, u32[]{:S(2)}, u32[]{:S(2)}) collective-permute-start(bf16[256,1024]{1,0:T(8,128)(2,1)S(1)} %fusion.31), channel_id=1, source_target_pairs={{0,2},{2,0},{4,6},{6,4},{1,3},{3,1},{5,7},{7,5},{8,10},{10,8},{12,... | collective-permute-start | bytes 1572872 | tf_op jit(solution)/shard_map/ppermute | solution.py:28
  525.6 31.4 %collective-permute-start.40 = (bf16[256,1024]{1,0:T(8,128)(2,1)S(1)}, bf16[256,1024]{1,0:T(8,128)(2,1)S(1)}, u32[]{:S(2)}, u32[]{:S(2)}) collective-permute-start(bf16[256,1024]{1,0:T(8,128)(2,1)S(1)} %fusion.30), channel_id=1, source_target_pairs={{0,4},{2,6},{4,0},{6,2},{1,5},{3,7},{5,1},{7,3},{8,12},{10,14},{12... | collective-permute-start | bytes 1572872 | tf_op jit(solution)/shard_map/ppermute | solution.py:28
  527.2 29.7 %collective-permute-start.45 = (f32[200,128]{1,0:T(8,128)S(1)}, f32[200,128]{1,0:T(8,128)S(1)}, u32[]{:S(2)}, u32[]{:S(2)}) collective-permute-start(f32[200,128]{1,0:T(8,128)S(1)} %add.294), channel_id=1, source_target_pairs={{0,2},{2,0},{4,6},{6,4},{1,3},{3,1},{5,7},{7,5},{8,10},{10,8},{12,... | collective-permute-start | bytes 307208 | tf_op jit(solution)/shard_map/ppermute | solution.py:153
  557.0 17.9 %collective-permute-start.49 = (bf16[2048,1024]{1,0:T(8,128)(2,1)}, bf16[2048,1024]{1,0:T(8,128)(2,1)S(1)}, u32[]{:S(2)}, u32[]{:S(2)}) collective-permute-start(bf16[2048,1024]{1,0:T(8,128)(2,1)} %join.10.blocks), channel_id=1, source_target_pairs={{0,1},{1,0},{2,3},{3,2},{4,5},{5,4},{6,7},{7,6},{8,9},{9,8},{10,11... | collective-permute-start | bytes 12582920 | tf_op jit(solution)/shard_map/ppermute | solution.py:32
  557.2 14.8 %collective-permute-start.48 = (f32[200,128]{1,0:T(8,128)S(1)}, f32[200,128]{1,0:T(8,128)S(1)}, u32[]{:S(2)}, u32[]{:S(2)}) collective-permute-start(f32[200,128]{1,0:T(8,128)S(1)} %add.295), channel_id=1, source_target_pairs={{0,4},{2,6},{4,0},{6,2},{1,5},{3,7},{5,1},{7,3},{8,12},{10,14},{12... | collective-permute-start | bytes 307208 | tf_op jit(solution)/shard_map/ppermute | solution.py:153
  559.6 14.2 %collective-permute-start.46 = (bf16[256,1024]{1,0:T(8,128)(2,1)}, bf16[256,1024]{1,0:T(8,128)(2,1)S(1)}, u32[]{:S(2)}, u32[]{:S(2)}) collective-permute-start(bf16[256,1024]{1,0:T(8,128)(2,1)} %slice.216), channel_id=1, source_target_pairs={{0,4},{2,6},{4,0},{6,2},{1,5},{3,7},{5,1},{7,3},{8,12},{10,14},{12... | collective-permute-start | bytes 1572872 | tf_op jit(solution)/shard_map/ppermute | solution.py:28
  577.3 16.9 %collective-permute-start.50 = (bf16[2048,1024]{1,0:T(8,128)(2,1)}, bf16[2048,1024]{1,0:T(8,128)(2,1)S(1)}, u32[]{:S(2)}, u32[]{:S(2)}) collective-permute-start(bf16[2048,1024]{1,0:T(8,128)(2,1)} %join.11.blocks), channel_id=1, source_target_pairs={{0,1},{1,0},{2,3},{3,2},{4,5},{5,4},{6,7},{7,6},{8,9},{9,8},{10,11... | collective-permute-start | bytes 12582920 | tf_op jit(solution)/shard_map/ppermute | solution.py:32
  (96 other events, 792.3 us)
Sparse Core Ops, SparseCore 0:
  14.1 27.2 all-gather.5
  55.2 63.6 all-gather.7
  121.0 79.4 all-gather.3
  334.3 74.5 reduce-scatter.2
  425.2 74.9 reduce-scatter.4
